TPU v7x, 128 devices: a whole 4x4x4 slice. The times are simulated.
128 devices in a mesh: gx: 8 (over y, core), gy: 16 (over x, z).
Axes of the slice: x: 4, y: 4, z: 4, core: 2. Of those that a mesh axis runs over, the one named last changes fastest.
Arguments:
- rhs: float32 [8, 2, 1024, 2048], P(None, None, 'gy', 'gx'), may hold values from -16.5 to 16.5
- metric: float32 [1024], replicated, may hold values from 0.5 to 2
- wavenumber: float32 [8], replicated, may hold values from 2e-05 to 0.002
Outputs:
- pressure: float32 [8, 2, 1024, 2048], P(None, None, 'gy', 'gx')
All inputs are finite; a program needn't handle non-finite values.
Results may differ from a plain program's by a relative error of at most 0.0009.
Values sent between devices are 32-bit elements; how exact they have to be, the bound alone decides.
No kernel may reach another device: no remote copies, remote signals or barrier semaphores. Data moves between devices by JAX's collectives and lax.ppermute only.
A program may use at most 64 MiB of HBM per device.

v0:
```python
import functools
import math

import jax
import jax.numpy as jnp
import numpy as np
from jax import lax
from jax.experimental import pallas as pl
from jax.experimental.pallas import tpu as pltpu
from jax.sharding import PartitionSpec as P


ASPECT = 0.02
STRIPS = 8
COLS = 256
ROWS = 64
BANDS = 16
NX = STRIPS * COLS
VMEM_LIMIT = 48 * 1024 * 1024
F32 = jnp.float32


def f32(values):
    return np.asarray(values, np.float32)


def sine_table():
    ramp = np.arange(COLS)
    table = np.sin(np.pi * (np.outer(ramp, ramp) % (2 * COLS)) / COLS) * math.sqrt(2.0 / COLS)
    table[0, :] = 0.0
    table[:, 0] = 0.0
    table[0, 0] = 1.0
    return f32(table)


def edge_table():
    ramp = np.arange(COLS)
    left = np.sin(np.pi * ramp / COLS) * math.sqrt(2.0 / COLS)
    right = left * np.where(ramp % 2 == 1, 1.0, -1.0)
    left[0] = right[0] = 0.0
    along = 4.0 * np.sin(np.pi * ramp / (2 * COLS)) ** 2
    rows = [ASPECT * left, ASPECT * right, ASPECT * along]
    return f32(np.stack([np.broadcast_to(r, (8, COLS)) for r in rows]))


def dft_table():
    ramp = np.arange(COLS)
    angle = 2.0 * np.pi * (np.outer(ramp, ramp) % COLS) / COLS
    return f32(np.concatenate([np.cos(angle), np.sin(angle)], 1))


def wave_table():
    kappa = np.arange(STRIPS)[:, None]
    j = np.arange(COLS)[None, :]
    angle = 2.0 * np.pi * j * kappa / NX
    along = ASPECT * (2.0 * np.sin(np.pi * (STRIPS * j + kappa) / NX)) ** 2
    return f32(np.stack([np.cos(angle), np.sin(angle), along]))


def octet_forward():
    ramp = np.arange(STRIPS)
    angle = 2.0 * np.pi * np.outer(ramp, ramp) / STRIPS
    c, s = np.cos(angle), np.sin(angle)
    return f32(np.block([[c, s], [-s, c]]))


def octet_inverse():
    ramp = np.arange(STRIPS)
    parts = []
    for offset in (0, 1):
        angle = 2.0 * np.pi * np.outer(ramp + offset, ramp) / STRIPS
        c, s = np.cos(angle), np.sin(angle)
        parts.append(np.block([[c, -s], [s, c]]))
    return f32(np.concatenate(parts, 0) / NX)


def dot(a, b):
    return jnp.dot(a, b, precision=lax.Precision.HIGHEST, preferred_element_type=F32)


def lane_ids():
    return lax.broadcasted_iota(jnp.int32, (8, 128), 1)


def wide(column):
    return jnp.broadcast_to(column, (8, 128))


def row_sum(values):
    return wide(jnp.sum(values[:, :128] + values[:, 128:], axis=1, keepdims=True))


def splat_inverse(metric_ref, index):
    return 1.0 / jnp.full((8, COLS), metric_ref[index], F32)


def local_kernel(rhs_ref, metric_ref, wave_ref, sine_ref, edge_ref, solved_ref, ratio_ref, send_ref, z_ref, f_lo, f_hi):
    first = lax.axis_index("gy") * ROWS
    sine = sine_ref[...]
    lanes = lane_ids()
    sub = lax.broadcasted_iota(jnp.int32, (8, COLS), 0)
    shift = edge_ref[2]
    for mode in range(8):
        shift = shift + jnp.where(sub == mode, wave_ref[mode], 0.0)
    height = jnp.ones((8, COLS), F32)
    slope = jnp.ones((8, COLS), F32)
    state = [jnp.zeros((8, COLS), F32)] * 2
    for mode in range(8):
        block = slice(mode * 2 * ROWS, (mode + 1) * 2 * ROWS)
        lines = dot(rhs_ref[block, :], sine)
        f_lo[block, :] = lines[:, :128]
        f_hi[block, :] = lines[:, 128:]
    for y in range(1, ROWS):
        inverse = splat_inverse(metric_ref, first + y)
        slope = slope + shift * inverse * height
        taller = height + slope
        ratio = height / taller
        height = taller
        ratio_ref[y] = ratio
        for c in range(2):
            rows = pl.ds(c * ROWS + y, 8, stride=2 * ROWS)
            line = jnp.concatenate([f_lo[rows, :], f_hi[rows, :]], 1)
            state[c] = (line * inverse + state[c]) * ratio
            z_ref[y, c] = state[c]
    left = edge_ref[0]
    right = edge_ref[1]
    columns = [[jnp.zeros((8, 128), F32)] * 2 for _ in range(2)]
    upper = [jnp.zeros((8, COLS), F32)] * 2
    for y in range(ROWS - 1, 0, -1):
        ratio = ratio_ref[y]
        inverse = splat_inverse(metric_ref, first + y)
        for c in range(2):
            upper[c] = z_ref[y, c] + ratio * upper[c]
            solved_ref[y, c] = upper[c]
            scaled = upper[c] * inverse
            a = scaled * left
            a = a[:, :128] + a[:, 128:] + jnp.where(
                lanes == 0, f_lo[pl.ds(c * ROWS + y, 8, stride=2 * ROWS), :] * inverse[:, :128], 0.0
            )
            b = scaled * right
            b = b[:, :128] + b[:, 128:]
            columns[0][c] = jnp.where(lanes == y, wide(jnp.sum(a, axis=1, keepdims=True)), columns[0][c])
            columns[1][c] = jnp.where(lanes == y + ROWS, wide(jnp.sum(b, axis=1, keepdims=True)), columns[1][c])
    edges = jnp.concatenate([solved_ref[y, c] for y in (1, ROWS - 1) for c in range(2)], 0)
    edges = dot(edges, sine)
    zero_lane = lax.broadcasted_iota(jnp.int32, (8, COLS), 1) == 0
    inverse = splat_inverse(metric_ref, first)
    for c in range(2):
        near = jnp.where(zero_lane, 0.0, edges[c * 8 : c * 8 + 8])
        row = [rhs_ref[(mode * 2 + c) * ROWS : (mode * 2 + c) * ROWS + 1, :] for mode in range(8)]
        near = near + jnp.concatenate(row, 0) * inverse
        far = jnp.where(zero_lane, 0.0, edges[16 + c * 8 : 24 + c * 8])
        for half in range(2):
            part = slice(half * 128, half * 128 + 128)
            send_ref[pl.ds(c * 2 + half, 8, stride=16), :] = near[:, part]
            send_ref[pl.ds(4 + c * 2 + half, 8, stride=16), :] = far[:, part]
        send_ref[pl.ds(8 + c, 8, stride=16), :] = jnp.where(lanes < ROWS, columns[0][c], columns[1][c])
        for pad in range(3):
            send_ref[pl.ds(10 + c * 3 + pad, 8, stride=16), :] = jnp.zeros((8, 128), F32)


def factor_kernel(metric_ref, inverse_ref, wave_ref, table_ref, alpha_ref, beta_ref, ratio_ref, pivot_ref, carry_ref):
    mine = lax.axis_index("gy")
    shift = table_ref[2] + wave_ref[lax.axis_index("gx")]

    def excess(row):
        double = 2.0 * metric_ref[row]
        return ((double + shift) - double) * inverse_ref[row]

    one = jnp.ones((8, COLS), F32)
    zero = jnp.zeros((8, COLS), F32)
    together = 4

    def bands(outer, carry):
        gamma_below, excess_below, flow = carry
        state = [(one, zero, zero, zero)] * together

        def rows(y, state):
            out = []
            for i in range(together):
                height, slope, rest, rise = state[i]
                t = excess((outer * together + i) * ROWS + y)
                slope = slope + t * height
                height = height + (slope + 1.0)
                rise = rise + t * (rest + 1.0)
                rest = rest + rise
                out.append((height, slope, rest, rise))
            return tuple(out)

        state = lax.fori_loop(1, ROWS, rows, tuple(state), unroll=7)
        for i in range(together):
            height, slope, rest, _ = state[i]
            band = outer * together + i
            gamma = 1.0 / height
            x = excess(band * ROWS) + rest * gamma + excess_below + flow
            pivot = 1.0 / (gamma + x)
            forward = gamma * pivot
            pivot_ref[band] = pivot
            carry_ref[band] = forward
            excess_below = slope * gamma
            flow = forward * x
            gamma_below = gamma
        return gamma_below, excess_below, flow

    lax.fori_loop(0, BANDS // together, bands, (one, zero, one))

    height, slope = one, one
    for y in range(1, ROWS):
        beta_ref[y] = height
        slope = slope + excess(mine * ROWS + y) * height
        taller = height + slope
        ratio_ref[y] = height / taller
        height = taller
    gamma = 1.0 / height
    height, slope = one, one
    for y in range(ROWS - 1, 0, -1):
        alpha_ref[y] = height * gamma
        beta_ref[y] = beta_ref[y] * gamma
        slope = slope + excess(mine * ROWS + y) * height
        height = height + slope


def spectrum_kernel(recv_ref, alpha_ref, beta_ref, dft_ref, table_ref, octet_ref, send_ref, column_ref):
    def take(i):
        return recv_ref[pl.ds(i, 8, stride=16), :]

    pieces = [[], []]
    for c in range(2):
        for i in range(2):
            pieces[c].append(take(c * 2 + i))
        for i in range(2):
            pieces[c].append(take(4 + c * 2 + i))
        column = take(8 + c)
        pieces[c].append(column + pltpu.roll(pltpu.roll(column, 1, 0), ROWS, 1))
    stacked = jnp.concatenate([jnp.concatenate(pieces[0], 1), jnp.concatenate(pieces[1], 1)], 0)
    mixed = dot(octet_ref[...], stacked)
    cos, sin = table_ref[0], table_ref[1]
    turned = [[], []]
    for line in range(2):
        re = mixed[:8, line * COLS : line * COLS + COLS]
        im = mixed[8:, line * COLS : line * COLS + COLS]
        turned[0].append(re * cos + im * sin)
        turned[1].append(im * cos - re * sin)
    both = dot(jnp.concatenate(turned[0] + turned[1], 0), dft_ref[...])
    columns = [mixed[c * 8 : c * 8 + 8, 2 * COLS :] for c in range(2)]
    near = [jnp.zeros((8, COLS), F32)] * 2
    far = [jnp.zeros((8, COLS), F32)] * 2
    for y in range(1, ROWS):
        alpha, beta = alpha_ref[y], beta_ref[y]
        for c in range(2):
            source = wide(columns[c][:, y : y + 1])
            source = jnp.concatenate([source, source], 1)
            near[c] = near[c] + alpha * source
            far[c] = far[c] + beta * source
    for line, extra in enumerate((near, far)):
        re_cos = both[line * 8 : line * 8 + 8, :COLS]
        re_sin = both[line * 8 : line * 8 + 8, COLS:]
        im_cos = both[16 + line * 8 : 24 + line * 8, :COLS]
        im_sin = both[16 + line * 8 : 24 + line * 8, COLS:]
        send_ref[line * 2] = re_cos + im_sin + extra[0]
        send_ref[line * 2 + 1] = im_cos - re_sin + extra[1]
    for c in range(2):
        column_ref[c] = columns[c]


def column_kernel(column_ref, ratio_ref, sum_ref, z_ref):
    lanes = lane_ids()
    columns = [column_ref[c] for c in range(2)]
    state = [jnp.zeros((8, COLS), F32)] * 2
    for y in range(1, ROWS):
        ratio = ratio_ref[y]
        for c in range(2):
            source = wide(columns[c][:, y : y + 1])
            state[c] = (jnp.concatenate([source, source], 1) + state[c]) * ratio
            z_ref[y, c] = state[c]
    upper = [jnp.zeros((8, COLS), F32)] * 2
    total = [jnp.zeros((8, 128), F32)] * 2
    for y in range(ROWS - 1, 0, -1):
        ratio = ratio_ref[y]
        for c in range(2):
            upper[c] = z_ref[y, c] + ratio * upper[c]
            total[c] = jnp.where(lanes == y, row_sum(upper[c]), total[c])
    for c in range(2):
        sum_ref[c] = total[c]


def separator_kernel(
    q0, q1, q2, q3, alpha_ref, beta_ref, pivot_ref, carry_ref, sum_ref, dft_ref, table_ref, octet_ref, send_ref, b_ref, v_ref
):
    mine = lax.axis_index("gy")
    px, pz = mine // 4, mine % 4
    for sx, q in enumerate((q0, q1, q2, q3)):
        for sz in range(4):
            b_ref[((px + 4 - sx) % 4) * 4 + (pz + 4 - sz) % 4] = q[sz]
    state = [jnp.zeros((8, COLS), F32)] * 2
    for band in range(BANDS):
        for c in range(2):
            value = b_ref[band, c]
            if band:
                value = value + b_ref[band - 1, 2 + c] + carry_ref[band - 1] * state[c]
            state[c] = value
            v_ref[band, c] = value * pivot_ref[band]
    value = [jnp.zeros((8, COLS), F32)] * 2
    for c in range(2):
        v_ref[BANDS, c] = value[c]
    for band in range(BANDS - 1, -1, -1):
        for c in range(2):
            value[c] = v_ref[band, c] + carry_ref[band] * value[c]
            v_ref[band, c] = value[c]
    near = [v_ref[mine, c] for c in range(2)]
    far = [v_ref[mine + 1, c] for c in range(2)]
    lanes = lane_ids()
    both = dot(jnp.concatenate([near[0], far[0], near[1], far[1]], 0), dft_ref[...])
    total = [sum_ref[c] for c in range(2)]
    for y in range(1, ROWS):
        alpha, beta = alpha_ref[y], beta_ref[y]
        for c in range(2):
            extra = row_sum(alpha * near[c] + beta * far[c])
            total[c] = total[c] + jnp.where(lanes == y, extra, 0.0)
    cos, sin = table_ref[0], table_ref[1]
    turned = [[], []]
    for line in range(2):
        re_cos = both[line * 8 : line * 8 + 8, :COLS]
        re_sin = both[line * 8 : line * 8 + 8, COLS:]
        im_cos = both[16 + line * 8 : 24 + line * 8, :COLS]
        im_sin = both[16 + line * 8 : 24 + line * 8, COLS:]
        re = re_cos - im_sin
        im = re_sin + im_cos
        turned[0].append(re * cos - im * sin)
        turned[1].append(re * sin + im * cos)
    stacked = [jnp.concatenate(turned[c] + [total[c]], 1) for c in range(2)]
    out = dot(octet_ref[...], jnp.concatenate(stacked, 0))
    for c in range(2):
        for i in range(4):
            row = (i // 2) * 4 + c * 2 + i % 2
            send_ref[pl.ds(row, 8, stride=16), :] = out[c * 8 : c * 8 + 8, i * 128 : i * 128 + 128]
        here = out[c * 8 : c * 8 + 8, 2 * COLS :]
        there = out[16 + c * 8 : 24 + c * 8, 2 * COLS :]
        send_ref[pl.ds(8 + c, 8, stride=16), :] = jnp.where(lanes < ROWS, here, pltpu.roll(there, ROWS, 1))
        for pad in range(3):
            send_ref[pl.ds(10 + c * 3 + pad, 8, stride=16), :] = jnp.zeros((8, 128), F32)


def finish_kernel(recv_ref, solved_ref, ratio_ref, metric_ref, sine_ref, edge_ref, out_ref, z_ref, u_lo, u_hi):
    first = lax.axis_index("gy") * ROWS

    def take(i):
        return recv_ref[pl.ds(i, 8, stride=16), :]

    sine = sine_ref[...]
    near = [jnp.concatenate([take(c * 2), take(c * 2 + 1)], 1) for c in range(2)]
    far = [jnp.concatenate([take(4 + c * 2), take(5 + c * 2)], 1) for c in range(2)]
    columns = [take(8 + c) for c in range(2)]
    edges = dot(jnp.concatenate(near + far, 0), sine)
    left, right = edge_ref[0], edge_ref[1]
    zero_lane = lax.broadcasted_iota(jnp.int32, (8, COLS), 1) == 0
    state = [edges[c * 8 : c * 8 + 8] for c in range(2)]
    for y in range(1, ROWS):
        ratio = ratio_ref[y]
        inverse = splat_inverse(metric_ref, first + y)
        a, b = left * inverse, right * inverse
        for c in range(2):
            here = wide(columns[c][:, y : y + 1])
            there = wide(columns[c][:, ROWS + y : ROWS + y + 1])
            here = jnp.concatenate([here, here], 1)
            there = jnp.concatenate([there, there], 1)
            state[c] = (state[c] + a * here + b * there) * ratio
            z_ref[y, c] = state[c]
    upper = [edges[16 + c * 8 : 24 + c * 8] for c in range(2)]
    for y in range(ROWS - 1, -1, -1):
        for c in range(2):
            if y:
                upper[c] = z_ref[y, c] + ratio_ref[y] * upper[c]
                here = wide(columns[c][:, y : y + 1])
                here = jnp.concatenate([here, here], 1)
                line = jnp.where(zero_lane, here, upper[c] + solved_ref[y, c])
            else:
                line = edges[c * 8 : c * 8 + 8]
            rows = pl.ds(c * ROWS + y, 8, stride=2 * ROWS)
            u_lo[rows, :] = line[:, :128]
            u_hi[rows, :] = line[:, 128:]
    for mode in range(8):
        block = slice(mode * 2 * ROWS, (mode + 1) * 2 * ROWS)
        out_ref[block, :] = dot(jnp.concatenate([u_lo[block, :], u_hi[block, :]], 1), sine)


def call(kernel, outs, scratch, *operands, scalars=()):
    vmem = pl.BlockSpec(memory_space=pltpu.VMEM)
    smem = pl.BlockSpec(memory_space=pltpu.SMEM)
    shapes = [jax.ShapeDtypeStruct(s, F32) for s in outs]
    return pl.pallas_call(
        kernel,
        out_shape=shapes,
        in_specs=[smem if i in scalars else vmem for i in range(len(operands))],
        out_specs=[vmem] * len(shapes),
        scratch_shapes=[pltpu.VMEM(s, F32) for s in scratch],
        compiler_params=pltpu.CompilerParams(vmem_limit_bytes=VMEM_LIMIT),
    )(*operands)


def gather_bands(piece):
    def along(values, near):
        return [values] + [
            lax.ppermute(values, "gy", [(a, near(a, s)) for a in range(BANDS)]) for s in range(1, 4)
        ]

    line = jnp.stack(along(piece, lambda a, s: a // 4 * 4 + (a + s) % 4))
    return along(line, lambda a, s: (a + 4 * s) % BANDS)


def per_device(rhs, metric, wavenumber):
    sine, edge = jnp.asarray(sine_table()), jnp.asarray(edge_table())
    dft, table = jnp.asarray(dft_table()), jnp.asarray(wave_table())
    full = (ROWS, 8, COLS)
    solved, local_ratio, send = call(
        local_kernel,
        [(ROWS, 2, 8, COLS), full, (128, 128)],
        [(ROWS, 2, 8, COLS), (1024, 128), (1024, 128)],
        rhs.reshape(1024, COLS), metric, wavenumber, sine, edge,
        scalars=(1, 2),
    )
    recv = lax.all_to_all(send.reshape(8, 16, 128), "gx", 0, 0, tiled=True)
    alpha, beta, ratio, pivot, carry = call(
        factor_kernel,
        [full, full, full, (BANDS, 8, COLS), (BANDS, 8, COLS)],
        [],
        metric, 1.0 / metric, wavenumber, table,
        scalars=(0, 1, 2),
    )
    piece, column = call(
        spectrum_kernel,
        [(4, 8, COLS), (2, 8, 128)],
        [],
        recv.reshape(128, 128), alpha, beta, dft, table, jnp.asarray(octet_forward()),
    )
    pieces = gather_bands(piece)
    (total,) = call(column_kernel, [(2, 8, 128)], [(ROWS, 2, 8, COLS)], column, ratio)
    (send,) = call(
        separator_kernel,
        [(128, 128)],
        [(BANDS, 4, 8, COLS), (BANDS + 1, 2, 8, COLS)],
        *pieces, alpha, beta, pivot, carry, total, dft, table, jnp.asarray(octet_inverse()),
    )
    recv = lax.all_to_all(send.reshape(8, 16, 128), "gx", 0, 0, tiled=True)
    (out,) = call(
        finish_kernel,
        [(1024, COLS)],
        [(ROWS, 2, 8, COLS), (1024, 128), (1024, 128)],
        recv.reshape(128, 128), solved, local_ratio, metric, sine, edge,
        scalars=(3,),
    )
    return out.reshape(8, 2, ROWS, COLS)


def solution(mesh):
    placed = (P(None, None, "gy", "gx"), P(), P())
    return jax.shard_map(
        per_device, mesh=mesh, in_specs=placed, out_specs=P(None, None, "gy", "gx"), check_vma=False
    )
```

profile of v0, /device:TPU:1, one launch (start us, length us, event | category | flops | bytes accessed | tf_op | source)
XLA Modules:
  0.0 55.3 jit_solution(14518255945125029512)
XLA Ops:
  0.0 0.0 copy-start.13
  0.0 0.7 %copy-done.13 = f32[8]{0:T(128)S(1)} copy-done((f32[8]{0:T(128)S(1)}, f32[8]{0:T(128)}, u32[]{:S(2)}) %copy-start.13) | copy-done | bytes 56
  0.7 0.0 copy-start.1
  0.7 0.9 %copy-done.1 = f32[256,256]{1,0:T(8,128)S(1)} copy-done((f32[256,256]{1,0:T(8,128)S(1)}, f32[256,256]{1,0:T(8,128)}, u32[]{:S(2)}) %copy-start.1) | copy-done | bytes 262168
  1.6 0.0 copy-start.3
  1.6 1.2 %copy-done.3 = f32[8,2,64,256]{3,2,1,0:T(8,128)S(1)} copy-done((f32[8,2,64,256]{3,2,1,0:T(8,128)S(1)}, f32[8,2,64,256]{3,2,1,0:T(8,128)}, u32[]{:S(2)}) %copy-start.3) | copy-done | bytes 1048600
  2.8 0.0 copy-start.7
  2.8 0.7 %copy-done.7 = f32[3,8,256]{2,1,0:T(8,128)S(1)} copy-done((f32[3,8,256]{2,1,0:T(8,128)S(1)}, f32[3,8,256]{2,1,0:T(8,128)}, u32[]{:S(2)}) %copy-start.7) | copy-done | bytes 24600
  3.6 0.0 copy-start.9
  3.6 0.7 %copy-done.9 = f32[1024]{0:T(1024)S(1)} copy-done((f32[1024]{0:T(1024)S(1)}, f32[1024]{0:T(1024)}, u32[]{:S(2)}) %copy-start.9) | copy-done | bytes 4120
  4.3 0.0 copy-start
  4.3 3.7 %shard_map.91 = (f32[64,2,8,256]{3,2,1,0:T(8,128)S(1)}, f32[64,8,256]{2,1,0:T(8,128)S(1)}, f32[128,128]{1,0:T(8,128)}) custom-call(f32[1024,256]{1,0:T(8,128)S(1)} %bitcast.10, f32[1024]{0:T(1024)S(1)} %copy-done.9, f32[8]{0:T(128)S(1)} %copy-done.13, f32[256,256]{1,0:T(8,128)S(1)} %copy-done.1, f32[3,8,256]{2,1,0:T(8,128)S(1)} %copy-done.7), custom_call_target="tpu_custom_call" | custom-call | tf_op jit(solution)/shard_map/pallas_call | solution.py:391
  7.9 0.0 copy-start.4
  7.9 0.8 %copy-done.4 = f32[64,8,256]{2,1,0:T(8,128)} copy-done((f32[64,8,256]{2,1,0:T(8,128)}, f32[64,8,256]{2,1,0:T(8,128)S(1)}, u32[]{:S(2)}) %copy-start.4) | copy-done | bytes 524312
  8.7 0.0 copy-start.10
  8.7 0.0 copy-start.6
  8.7 6.1 %all-to-all-start = ((f32[8,16,128]{2,1,0:T(8,128)}), f32[8,16,128]{2,1,0:T(8,128)S(1)}, u32[]{:S(2)}, u32[]{:S(2)}) async-start(f32[8,16,128]{2,1,0:T(8,128)} %bitcast.1), calls=%async_computation | async-start | bytes 131072 | tf_op jit(solution)/shard_map/all_to_all | solution.py:422
  14.8 0.0 copy-done.10
  14.8 0.0 copy-done.6
  14.8 0.0 copy-start.12
  14.8 4.8 %shard_map.92 = (f32[64,8,256]{2,1,0:T(8,128)S(1)}, f32[64,8,256]{2,1,0:T(8,128)S(1)}, f32[64,8,256]{2,1,0:T(8,128)S(1)}, f32[16,8,256]{2,1,0:T(8,128)S(1)}, f32[16,8,256]{2,1,0:T(8,128)S(1)}) custom-call(f32[1024]{0:T(1024)S(1)} %copy-done.10, f32[1024]{0:T(1024)S(1)} %broadcast_divide_fusion.inverse_ref, f32[8]{0:T(128)S(1)} %copy-done.13, ...), custom_call_target="tpu_custom_call" | custom-call | tf_op jit(solution)/shard_map/pallas_call | solution.py:391
  19.7 0.0 all-to-all-done
  19.7 0.0 copy-done
  19.7 0.0 copy-done.12
  19.7 0.6 %shard_map.93 = (f32[4,8,256]{2,1,0:T(8,128)S(1)}, f32[2,8,128]{2,1,0:T(8,128)S(1)}) custom-call(f32[128,128]{1,0:T(8,128)S(1)} %bitcast.11, f32[64,8,256]{2,1,0:T(8,128)S(1)} %get-tuple-element.16.alpha_ref, f32[64,8,256]{2,1,0:T(8,128)S(1)} %get-tuple-element.17.beta_ref, f32[256,512]{1,0:T(8,128)S(1)} %copy-done, f32[3,8,256]{2,1,0:T(8,128)S(1)} %copy-done.6, ...), custom_call_target="tpu_custom_call" | custom-call | tf_op jit(solution)/shard_map/pallas_call | solution.py:391
  20.3 3.8 %collective-permute-start.2 = (f32[4,8,256]{2,1,0:T(8,128)S(1)}, f32[4,8,256]{2,1,0:T(8,128)S(1)}, u32[]{:S(2)}, u32[]{:S(2)}) collective-permute-start(f32[4,8,256]{2,1,0:T(8,128)S(1)} %get-tuple-element.18), channel_id=1, source_target_pairs={{0,3},{1,0},{2,1},{3,2},{4,7},{5,4},{6,5},{7,6},{8,11},{9,8},{10,9... | collective-permute-start | bytes 98312 | tf_op jit(solution)/shard_map/ppermute | solution.py:404
  24.1 0.0 collective-permute-start.1
  24.1 0.7 %collective-permute-start = (f32[4,8,256]{2,1,0:T(8,128)S(1)}, f32[4,8,256]{2,1,0:T(8,128)S(1)}, u32[]{:S(2)}, u32[]{:S(2)}) collective-permute-start(f32[4,8,256]{2,1,0:T(8,128)S(1)} %get-tuple-element.18), channel_id=1, source_target_pairs={{0,1},{1,2},{2,3},{3,0},{4,5},{5,6},{6,7},{7,4},{8,9},{9,10},{10,1... | collective-permute-start | bytes 98312 | tf_op jit(solution)/shard_map/ppermute | solution.py:404
  24.8 0.3 collective-permute-done.2
  25.1 3.3 %collective-permute-done.1 = f32[4,8,256]{2,1,0:T(8,128)S(1)} collective-permute-done((f32[4,8,256]{2,1,0:T(8,128)S(1)}, f32[4,8,256]{2,1,0:T(8,128)S(1)}, u32[]{:S(2)}, u32[]{:S(2)}) %collective-permute-start.1) | collective-permute-done | bytes 32800 | tf_op jit(solution)/shard_map/ppermute | solution.py:404
  28.4 0.0 collective-permute-done
  28.5 2.5 %collective-permute-start.5 = (f32[4,4,8,256]{3,2,1,0:T(8,128)S(1)}, f32[4,4,8,256]{3,2,1,0:T(8,128)S(1)}, u32[]{:S(2)}, u32[]{:S(2)}) collective-permute-start(f32[4,4,8,256]{3,2,1,0:T(8,128)S(1)} %pad_maximum_fusion.q0), channel_id=1, source_target_pairs={{0,12},{1,13},{2,14},{3,15},{4,0},{5,1},{6,2},{7,3},{8,4},{9,5},{1... | collective-permute-start | bytes 393224 | tf_op jit(solution)/shard_map/ppermute | solution.py:404
  31.0 0.5 collective-permute-start.4
  31.5 0.6 %collective-permute-start.3 = (f32[4,4,8,256]{3,2,1,0:T(8,128)S(1)}, f32[4,4,8,256]{3,2,1,0:T(8,128)S(1)}, u32[]{:S(2)}, u32[]{:S(2)}) collective-permute-start(f32[4,4,8,256]{3,2,1,0:T(8,128)S(1)} %pad_maximum_fusion.q0), channel_id=1, source_target_pairs={{0,4},{1,5},{2,6},{3,7},{4,8},{5,9},{6,10},{7,11},{8,12},{9,13},{1... | collective-permute-start | bytes 393224 | tf_op jit(solution)/shard_map/ppermute | solution.py:404
  32.1 0.0 copy-start.11
  32.1 0.5 shard_map.94.sum_ref
  32.6 1.1 %collective-permute-done.5.q3 = f32[4,4,8,256]{3,2,1,0:T(8,128)S(1)} collective-permute-done((f32[4,4,8,256]{3,2,1,0:T(8,128)S(1)}, f32[4,4,8,256]{3,2,1,0:T(8,128)S(1)}, u32[]{:S(2)}, u32[]{:S(2)}) %collective-permute-start.5) | collective-permute-done | bytes 131104 | tf_op jit(solution)/shard_map/ppermute | solution.py:404
  33.8 2.7 %collective-permute-done.4.q2 = f32[4,4,8,256]{3,2,1,0:T(8,128)S(1)} collective-permute-done((f32[4,4,8,256]{3,2,1,0:T(8,128)S(1)}, f32[4,4,8,256]{3,2,1,0:T(8,128)S(1)}, u32[]{:S(2)}, u32[]{:S(2)}) %collective-permute-start.4) | collective-permute-done | bytes 131104 | tf_op jit(solution)/shard_map/ppermute | solution.py:404
  36.4 1.3 %collective-permute-done.3.q1 = f32[4,4,8,256]{3,2,1,0:T(8,128)S(1)} collective-permute-done((f32[4,4,8,256]{3,2,1,0:T(8,128)S(1)}, f32[4,4,8,256]{3,2,1,0:T(8,128)S(1)}, u32[]{:S(2)}, u32[]{:S(2)}) %collective-permute-start.3) | collective-permute-done | bytes 131104 | tf_op jit(solution)/shard_map/ppermute | solution.py:404
  37.7 0.0 copy-done.11
  37.7 0.0 copy-start.2
  37.7 0.0 copy-start.5
  37.7 0.8 %shard_map.95 = f32[128,128]{1,0:T(8,128)S(1)} custom-call(f32[4,4,8,256]{3,2,1,0:T(8,128)S(1)} %pad_maximum_fusion.q0, f32[4,4,8,256]{3,2,1,0:T(8,128)S(1)} %collective-permute-done.3.q1, f32[4,4,8,256]{3,2,1,0:T(8,128)S(1)} %collective-permute-done.4.q2, f32[4,4,8,256]{3,2,1,0:T(8,128)S(1)} %collective-permute-done.5.q3, ...), custom_call_target="tpu_custom_call" | custom-call | tf_op jit(solution)/shard_map/pallas_call | solution.py:391
  38.6 12.8 %all_to_all.10 = f32[8,16,128]{2,1,0:T(8,128)S(1)} all-to-all(f32[8,16,128]{2,1,0:T(8,128)S(1)} %bitcast.12), channel_id=1, replica_groups=mesh['gx'=8,'gy'=16] {'gx'}, dimensions={0} | all-to-all | bytes 131072 | tf_op jit(solution)/shard_map/all_to_all | solution.py:444
  51.3 0.0 copy-done.2
  51.3 0.0 copy-done.5
  51.3 0.0 copy-done.8
  51.3 3.9 %shard_map.96 = f32[1024,256]{1,0:T(8,128)} custom-call(f32[128,128]{1,0:T(8,128)S(1)} %bitcast.13, f32[64,2,8,256]{3,2,1,0:T(8,128)S(1)} %get-tuple-element.23.solved_ref, f32[64,8,256]{2,1,0:T(8,128)S(1)} %copy-done.5, f32[1024]{0:T(1024)S(1)} %copy-done.10, f32[256,256]{1,0:T(8,128)S(1)} %copy-done.2, f32[3,8,256]{2,1,0:T(8,128)S(1)} %copy-done.8), custom_call_target="tpu_custom_call" | custom-call | tf_op jit(solution)/shard_map/pallas_call | solution.py:391
  (3 shorter events, 0.0 us)
Async XLA Ops:
  0.0 0.7 %copy-start.13 = (f32[8]{0:T(128)S(1)}, f32[8]{0:T(128)}, u32[]{:S(2)}) copy-start(f32[8]{0:T(128)} %wave_ref.3) | copy-start | bytes 100
  0.7 0.9 %copy-start.1 = (f32[256,256]{1,0:T(8,128)S(1)}, f32[256,256]{1,0:T(8,128)}, u32[]{:S(2)}) copy-start(f32[256,256]{1,0:T(8,128)} %constant.14.clone.sine_ref) | copy-start | bytes 786436
  1.6 1.2 %copy-start.3 = (f32[8,2,64,256]{3,2,1,0:T(8,128)S(1)}, f32[8,2,64,256]{3,2,1,0:T(8,128)}, u32[]{:S(2)}) copy-start(f32[8,2,64,256]{3,2,1,0:T(8,128)} %param.9) | copy-start | bytes 3145732
  2.8 0.7 %copy-start.7 = (f32[3,8,256]{2,1,0:T(8,128)S(1)}, f32[3,8,256]{2,1,0:T(8,128)}, u32[]{:S(2)}) copy-start(f32[3,8,256]{2,1,0:T(8,128)} %constant.15.clone.edge_ref) | copy-start | bytes 73732
  3.6 0.7 %copy-start.9 = (f32[1024]{0:T(1024)S(1)}, f32[1024]{0:T(1024)}, u32[]{:S(2)}) copy-start(f32[1024]{0:T(1024)} %metric_ref.5) | copy-start | bytes 12292
  4.3 15.4 %copy-start = (f32[256,512]{1,0:T(8,128)S(1)}, f32[256,512]{1,0:T(8,128)}, u32[]{:S(2)}) copy-start(f32[256,512]{1,0:T(8,128)} %constant.16.clone.dft_ref) | copy-start | bytes 1572868
  7.9 0.8 %copy-start.4 = (f32[64,8,256]{2,1,0:T(8,128)}, f32[64,8,256]{2,1,0:T(8,128)S(1)}, u32[]{:S(2)}) copy-start(f32[64,8,256]{2,1,0:T(8,128)S(1)} %get-tuple-element.24.ratio_ref) | copy-start | bytes 1572868
  8.7 6.1 %copy-start.10 = (f32[1024]{0:T(1024)S(1)}, f32[1024]{0:T(1024)}, u32[]{:S(2)}) copy-start(f32[1024]{0:T(1024)} %metric_ref.5) | copy-start | bytes 12292
  8.7 6.1 %copy-start.6 = (f32[3,8,256]{2,1,0:T(8,128)S(1)}, f32[3,8,256]{2,1,0:T(8,128)}, u32[]{:S(2)}) copy-start(f32[3,8,256]{2,1,0:T(8,128)} %constant.17.clone.table_ref) | copy-start | bytes 73732
  8.7 11.0 %all-to-all-start = ((f32[8,16,128]{2,1,0:T(8,128)}), f32[8,16,128]{2,1,0:T(8,128)S(1)}, u32[]{:S(2)}, u32[]{:S(2)}) async-start(f32[8,16,128]{2,1,0:T(8,128)} %bitcast.1), calls=%async_computation | async-start | bytes 131072 | tf_op jit(solution)/shard_map/all_to_all | solution.py:422
  14.8 4.8 %copy-start.12 = (f32[16,16]{1,0:T(8,128)S(1)}, f32[16,16]{1,0:T(8,128)}, u32[]{:S(2)}) copy-start(f32[16,16]{1,0:T(8,128)} %constant.18.clone.octet_ref) | copy-start | bytes 3076
  20.3 4.8 %collective-permute-start.2 = (f32[4,8,256]{2,1,0:T(8,128)S(1)}, f32[4,8,256]{2,1,0:T(8,128)S(1)}, u32[]{:S(2)}, u32[]{:S(2)}) collective-permute-start(f32[4,8,256]{2,1,0:T(8,128)S(1)} %get-tuple-element.18), channel_id=1, source_target_pairs={{0,3},{1,0},{2,1},{3,2},{4,7},{5,4},{6,5},{7,6},{8,11},{9,8},{10,9... | collective-permute-start | bytes 98312 | tf_op jit(solution)/shard_map/ppermute | solution.py:404
  24.1 4.3 %collective-permute-start.1 = (f32[4,8,256]{2,1,0:T(8,128)S(1)}, f32[4,8,256]{2,1,0:T(8,128)S(1)}, u32[]{:S(2)}, u32[]{:S(2)}) collective-permute-start(f32[4,8,256]{2,1,0:T(8,128)S(1)} %get-tuple-element.18), channel_id=1, source_target_pairs={{0,2},{1,3},{2,0},{3,1},{4,6},{5,7},{6,4},{7,5},{8,10},{9,11},{10,... | collective-permute-start | bytes 98312 | tf_op jit(solution)/shard_map/ppermute | solution.py:404
  24.1 4.3 %collective-permute-start = (f32[4,8,256]{2,1,0:T(8,128)S(1)}, f32[4,8,256]{2,1,0:T(8,128)S(1)}, u32[]{:S(2)}, u32[]{:S(2)}) collective-permute-start(f32[4,8,256]{2,1,0:T(8,128)S(1)} %get-tuple-element.18), channel_id=1, source_target_pairs={{0,1},{1,2},{2,3},{3,0},{4,5},{5,6},{6,7},{7,4},{8,9},{9,10},{10,1... | collective-permute-start | bytes 98312 | tf_op jit(solution)/shard_map/ppermute | solution.py:404
  28.5 5.3 %collective-permute-start.5 = (f32[4,4,8,256]{3,2,1,0:T(8,128)S(1)}, f32[4,4,8,256]{3,2,1,0:T(8,128)S(1)}, u32[]{:S(2)}, u32[]{:S(2)}) collective-permute-start(f32[4,4,8,256]{3,2,1,0:T(8,128)S(1)} %pad_maximum_fusion.q0), channel_id=1, source_target_pairs={{0,12},{1,13},{2,14},{3,15},{4,0},{5,1},{6,2},{7,3},{8,4},{9,5},{1... | collective-permute-start | bytes 393224 | tf_op jit(solution)/shard_map/ppermute | solution.py:404
  31.0 5.4 %collective-permute-start.4 = (f32[4,4,8,256]{3,2,1,0:T(8,128)S(1)}, f32[4,4,8,256]{3,2,1,0:T(8,128)S(1)}, u32[]{:S(2)}, u32[]{:S(2)}) collective-permute-start(f32[4,4,8,256]{3,2,1,0:T(8,128)S(1)} %pad_maximum_fusion.q0), channel_id=1, source_target_pairs={{0,8},{1,9},{2,10},{3,11},{4,12},{5,13},{6,14},{7,15},{8,0},{9,1},... | collective-permute-start | bytes 393224 | tf_op jit(solution)/shard_map/ppermute | solution.py:404
  31.5 6.2 %collective-permute-start.3 = (f32[4,4,8,256]{3,2,1,0:T(8,128)S(1)}, f32[4,4,8,256]{3,2,1,0:T(8,128)S(1)}, u32[]{:S(2)}, u32[]{:S(2)}) collective-permute-start(f32[4,4,8,256]{3,2,1,0:T(8,128)S(1)} %pad_maximum_fusion.q0), channel_id=1, source_target_pairs={{0,4},{1,5},{2,6},{3,7},{4,8},{5,9},{6,10},{7,11},{8,12},{9,13},{1... | collective-permute-start | bytes 393224 | tf_op jit(solution)/shard_map/ppermute | solution.py:404
  32.1 5.6 %copy-start.11 = (f32[32,16]{1,0:T(8,128)S(1)}, f32[32,16]{1,0:T(8,128)}, u32[]{:S(2)}) copy-start(f32[32,16]{1,0:T(8,128)} %constant.19.clone.octet_ref) | copy-start | bytes 6148
  37.7 13.6 %copy-start.2 = (f32[256,256]{1,0:T(8,128)S(1)}, f32[256,256]{1,0:T(8,128)}, u32[]{:S(2)}) copy-start(f32[256,256]{1,0:T(8,128)} %constant.14.clone.sine_ref) | copy-start | bytes 786436
  37.7 13.6 %copy-start.5 = (f32[64,8,256]{2,1,0:T(8,128)S(1)}, f32[64,8,256]{2,1,0:T(8,128)}, u32[]{:S(2)}) copy-start(f32[64,8,256]{2,1,0:T(8,128)} %copy-done.4) | copy-start | bytes 1572868
  38.6 12.8 %copy-start.8 = (f32[3,8,256]{2,1,0:T(8,128)S(1)}, f32[3,8,256]{2,1,0:T(8,128)}, u32[]{:S(2)}) copy-start(f32[3,8,256]{2,1,0:T(8,128)} %constant.15.clone.edge_ref) | copy-start | bytes 73732
where the time goes:
time: 55.7 us; the launch traced here: 55.3 us
  Pallas kernels  14.3 us (26%)
  starting transfers between devices  14.3 us (26%)
  blocking collectives  12.8 us (23%)
  waiting for transfers between devices  8.74 us (16%)
  local copies, waits for them, and re-layouts  5.08 us (9%)
    pallas_call x6, Pallas kernels, call(): pl.pallas_call(kernel, out_shape=shapes, in_specs=[smem if i in scalars e...  14.3 us
    all_to_all x1, blocking collectives, per_device(): recv = lax.all_to_all(send.reshape(8, 16, 128), 'gx', 0, 0, tiled=True)  12.8 us
    ppermute x6, waiting for transfers between devices, along(): lax.ppermute(values, 'gy', [(a, near(a, s)) for a in range(BANDS)])  8.73 us
    ppermute x6, starting transfers between devices, along(): lax.ppermute(values, 'gy', [(a, near(a, s)) for a in range(BANDS)])  8.2 us
    all_to_all x1, starting transfers between devices, per_device(): recv = lax.all_to_all(send.reshape(8, 16, 128), 'gx', 0, 0, tiled=True)  6.1 us
    unnamed x28, local copies, waits for them, and re-layouts  5.08 us
  transfers between devices with their start and end apart: 7, of which 5 were waited for; matrix products, arithmetic and copies ran while one was open for 0% of the time, Pallas kernels for 10%

commit v1 on v0

--- a/solution.py
+++ b/solution.py
@@ -16,7 +16,7 @@
 ROWS = 64
 BANDS = 16
 NX = STRIPS * COLS
-VMEM_LIMIT = 48 * 1024 * 1024
+VMEM_LIMIT = 16 * 1024 * 1024
 F32 = jnp.float32
 
 
@@ -94,22 +94,44 @@
     return 1.0 / jnp.full((8, COLS), metric_ref[index], F32)
 
 
-def local_kernel(rhs_ref, metric_ref, wave_ref, sine_ref, edge_ref, solved_ref, ratio_ref, send_ref, z_ref, f_lo, f_hi):
-    first = lax.axis_index("gy") * ROWS
-    sine = sine_ref[...]
-    lanes = lane_ids()
+def local_shift(wave_ref, edge_ref):
     sub = lax.broadcasted_iota(jnp.int32, (8, COLS), 0)
     shift = edge_ref[2]
     for mode in range(8):
         shift = shift + jnp.where(sub == mode, wave_ref[mode], 0.0)
+    return shift
+
+
+def local_kernel(
+    rhs_hbm, metric_hbm, wave_hbm, sine_hbm, edge_hbm, solved_hbm, send_ref,
+    ratio_ref, z_ref, f_lo, f_hi, rhs_ref, sine_ref, edge_ref, metric_ref, wave_ref, rhs_sem, sems, out_sem,
+):
+    first = lax.axis_index("gy") * ROWS
+    small = [
+        pltpu.make_async_copy(a, b, sems.at[i])
+        for i, (a, b) in enumerate(
+            ((sine_hbm, sine_ref), (metric_hbm, metric_ref), (wave_hbm, wave_ref), (edge_hbm, edge_ref))
+        )
+    ]
+    blocks = [pl.ds(mode * 2 * ROWS, 2 * ROWS) for mode in range(8)]
+    large = [pltpu.make_async_copy(rhs_hbm.at[b], rhs_ref.at[b], rhs_sem.at[i]) for i, b in enumerate(blocks)]
+    small[0].start()
+    for copy in large[:2] + small[1:] + large[2:]:
+        copy.start()
+    small[0].wait()
+    sine = sine_ref[...]
+    for mode in range(8):
+        large[mode].wait()
+        lines = dot(rhs_ref[blocks[mode], :], sine)
+        f_lo[blocks[mode], :] = lines[:, :128]
+        f_hi[blocks[mode], :] = lines[:, 128:]
+    for copy in small[1:]:
+        copy.wait()
+    lanes = lane_ids()
+    shift = local_shift(wave_ref, edge_ref)
     height = jnp.ones((8, COLS), F32)
     slope = jnp.ones((8, COLS), F32)
     state = [jnp.zeros((8, COLS), F32)] * 2
-    for mode in range(8):
-        block = slice(mode * 2 * ROWS, (mode + 1) * 2 * ROWS)
-        lines = dot(rhs_ref[block, :], sine)
-        f_lo[block, :] = lines[:, :128]
-        f_hi[block, :] = lines[:, 128:]
     for y in range(1, ROWS):
         inverse = splat_inverse(metric_ref, first + y)
         slope = slope + shift * inverse * height
@@ -126,12 +148,13 @@
     right = edge_ref[1]
     columns = [[jnp.zeros((8, 128), F32)] * 2 for _ in range(2)]
     upper = [jnp.zeros((8, COLS), F32)] * 2
+    done = []
     for y in range(ROWS - 1, 0, -1):
         ratio = ratio_ref[y]
         inverse = splat_inverse(metric_ref, first + y)
         for c in range(2):
             upper[c] = z_ref[y, c] + ratio * upper[c]
-            solved_ref[y, c] = upper[c]
+            z_ref[y, c] = upper[c]
             scaled = upper[c] * inverse
             a = scaled * left
             a = a[:, :128] + a[:, 128:] + jnp.where(
@@ -141,7 +164,13 @@
             b = b[:, :128] + b[:, 128:]
             columns[0][c] = jnp.where(lanes == y, wide(jnp.sum(a, axis=1, keepdims=True)), columns[0][c])
             columns[1][c] = jnp.where(lanes == y + ROWS, wide(jnp.sum(b, axis=1, keepdims=True)), columns[1][c])
-    edges = jnp.concatenate([solved_ref[y, c] for y in (1, ROWS - 1) for c in range(2)], 0)
+        if y % 16 == 0:
+            done.append(pltpu.make_async_copy(z_ref.at[pl.ds(y, 16)], solved_hbm.at[pl.ds(y, 16)], out_sem.at[y // 16]))
+            done[-1].start()
+    z_ref[0] = jnp.zeros((2, 8, COLS), F32)
+    done.append(pltpu.make_async_copy(z_ref.at[pl.ds(0, 16)], solved_hbm.at[pl.ds(0, 16)], out_sem.at[0]))
+    done[-1].start()
+    edges = jnp.concatenate([z_ref[y, c] for y in (1, ROWS - 1) for c in range(2)], 0)
     edges = dot(edges, sine)
     zero_lane = lax.broadcasted_iota(jnp.int32, (8, COLS), 1) == 0
     inverse = splat_inverse(metric_ref, first)
@@ -157,9 +186,20 @@
         send_ref[pl.ds(8 + c, 8, stride=16), :] = jnp.where(lanes < ROWS, columns[0][c], columns[1][c])
         for pad in range(3):
             send_ref[pl.ds(10 + c * 3 + pad, 8, stride=16), :] = jnp.zeros((8, 128), F32)
-
-
-def factor_kernel(metric_ref, inverse_ref, wave_ref, table_ref, alpha_ref, beta_ref, ratio_ref, pivot_ref, carry_ref):
+    for copy in done:
+        copy.wait()
+
+
+def factors(ref):
+    sizes = (ROWS, ROWS, ROWS, BANDS, BANDS, 3)
+    starts = np.cumsum((0,) + sizes)
+    return [ref.at[pl.ds(int(a), n)] for a, n in zip(starts, sizes)]
+
+
+def factor_kernel(
+    metric_ref, inverse_ref, wave_ref, table_ref, factor_ref, gamma_ref, base_ref, x_ref
+):
+    alpha_ref, beta_ref, ratio_ref, up_ref, down_ref, final_ref = factors(factor_ref)
     mine = lax.axis_index("gy")
     shift = table_ref[2] + wave_ref[lax.axis_index("gx")]
 
@@ -172,7 +212,7 @@
     together = 4
 
     def bands(outer, carry):
-        gamma_below, excess_below, flow = carry
+        excess_below, flow = carry
         state = [(one, zero, zero, zero)] * together
 
         def rows(y, state):
@@ -192,17 +232,36 @@
             height, slope, rest, _ = state[i]
             band = outer * together + i
             gamma = 1.0 / height
-            x = excess(band * ROWS) + rest * gamma + excess_below + flow
-            pivot = 1.0 / (gamma + x)
-            forward = gamma * pivot
-            pivot_ref[band] = pivot
-            carry_ref[band] = forward
+            base = excess(band * ROWS) + rest * gamma + excess_below
+            x = base + flow
+            up = gamma / (gamma + x)
+            gamma_ref[band] = gamma
+            base_ref[band] = base
+            x_ref[band] = x
+            up_ref[band] = up
             excess_below = slope * gamma
-            flow = forward * x
-            gamma_below = gamma
-        return gamma_below, excess_below, flow
-
-    lax.fori_loop(0, BANDS // together, bands, (one, zero, one))
+            flow = up * x
+        return excess_below, flow
+
+    lax.fori_loop(0, BANDS // together, bands, (zero, one))
+
+    above, down, inverse = one, zero, zero
+    for band in range(BANDS - 1, -1, -1):
+        gamma = gamma_ref[band]
+        down_ref[band] = down
+
+        @pl.when(band == mine)
+        def _(above=above, down=down, inverse=inverse, gamma=gamma):
+            final_ref[0] = down
+            final_ref[1] = inverse
+            final_ref[2] = 1.0 / (x_ref[mine] + gamma * above)
+
+        if band:
+            x = base_ref[band] + gamma * above
+            below = gamma_ref[band - 1]
+            inverse = 1.0 / (below + x)
+            down = below * inverse
+            above = x * inverse
 
     height, slope = one, one
     for y in range(1, ROWS):
@@ -220,7 +279,12 @@
         height = height + slope
 
 
-def spectrum_kernel(recv_ref, alpha_ref, beta_ref, dft_ref, table_ref, octet_ref, send_ref, column_ref):
+def spectrum_kernel(
+    recv_ref, factor_ref, dft_ref, table_ref, octet_ref, send_hbm, own_ref, column_ref, send_ref, sem
+):
+    alpha_ref, beta_ref, _, up_ref, down_ref, _ = factors(factor_ref)
+    mine = lax.axis_index("gy")
+
     def take(i):
         return recv_ref[pl.ds(i, 8, stride=16), :]
 
@@ -252,18 +316,56 @@
             source = jnp.concatenate([source, source], 1)
             near[c] = near[c] + alpha * source
             far[c] = far[c] + beta * source
+    sides = []
     for line, extra in enumerate((near, far)):
         re_cos = both[line * 8 : line * 8 + 8, :COLS]
         re_sin = both[line * 8 : line * 8 + 8, COLS:]
         im_cos = both[16 + line * 8 : 24 + line * 8, :COLS]
         im_sin = both[16 + line * 8 : 24 + line * 8, COLS:]
-        send_ref[line * 2] = re_cos + im_sin + extra[0]
-        send_ref[line * 2 + 1] = im_cos - re_sin + extra[1]
+        sides.append((re_cos + im_sin + extra[0], im_cos - re_sin + extra[1]))
     for c in range(2):
+        own_ref[c], own_ref[2 + c] = sides[0][c], sides[1][c]
         column_ref[c] = columns[c]
-
-
-def column_kernel(column_ref, ratio_ref, sum_ref, z_ref):
+        send_ref[mine, c] = jnp.zeros((8, COLS), F32)
+
+    def copy(band):
+        return pltpu.make_async_copy(send_ref.at[band], send_hbm.at[band], sem.at[band])
+
+    copy(mine).start()
+    up, down = up_ref[mine], down_ref[mine]
+
+    def above(band, carry):
+        factor = up_ref[band]
+        for c in range(2):
+            send_ref[band, c] = carry[c]
+        copy(band).start()
+        return tuple(value * factor for value in carry)
+
+    def below(step, carry):
+        band = mine - 1 - step
+        factor = down_ref[band]
+        for c in range(2):
+            send_ref[band, c] = carry[c]
+        copy(band).start()
+        return tuple(value * factor for value in carry)
+
+    lax.fori_loop(mine + 1, BANDS, above, tuple(sides[1][c] + up * sides[0][c] for c in range(2)))
+    lax.fori_loop(0, mine, below, tuple(sides[0][c] + down * sides[1][c] for c in range(2)))
+    for band in range(BANDS):
+        copy(band).wait()
+
+
+def column_kernel(column_ref, factor_ref, metric_ref, wave_ref, edge_ref, sum_ref, local_ref, z_ref):
+    ratio_ref = factors(factor_ref)[2]
+    first = lax.axis_index("gy") * ROWS
+    shift = local_shift(wave_ref, edge_ref)
+    height = jnp.ones((8, COLS), F32)
+    slope = jnp.ones((8, COLS), F32)
+    for y in range(1, ROWS):
+        slope = slope + shift * splat_inverse(metric_ref, first + y) * height
+        taller = height + slope
+        local_ref[y] = height / taller
+        height = taller
     lanes = lane_ids()
     columns = [column_ref[c] for c in range(2)]
     state = [jnp.zeros((8, COLS), F32)] * 2
@@ -285,30 +387,20 @@
 
 
 def separator_kernel(
-    q0, q1, q2, q3, alpha_ref, beta_ref, pivot_ref, carry_ref, sum_ref, dft_ref, table_ref, octet_ref, send_ref, b_ref, v_ref
+    recv_ref, own_ref, factor_ref, sum_ref, dft_ref, table_ref, octet_ref, send_ref
 ):
+    alpha_ref, beta_ref, _, _, _, final_ref = factors(factor_ref)
     mine = lax.axis_index("gy")
-    px, pz = mine // 4, mine % 4
-    for sx, q in enumerate((q0, q1, q2, q3)):
-        for sz in range(4):
-            b_ref[((px + 4 - sx) % 4) * 4 + (pz + 4 - sz) % 4] = q[sz]
-    state = [jnp.zeros((8, COLS), F32)] * 2
+    from_below = [own_ref[c] for c in range(2)]
+    from_above = [own_ref[2 + c] for c in range(2)]
     for band in range(BANDS):
         for c in range(2):
-            value = b_ref[band, c]
-            if band:
-                value = value + b_ref[band - 1, 2 + c] + carry_ref[band - 1] * state[c]
-            state[c] = value
-            v_ref[band, c] = value * pivot_ref[band]
-    value = [jnp.zeros((8, COLS), F32)] * 2
-    for c in range(2):
-        v_ref[BANDS, c] = value[c]
-    for band in range(BANDS - 1, -1, -1):
-        for c in range(2):
-            value[c] = v_ref[band, c] + carry_ref[band] * value[c]
-            v_ref[band, c] = value[c]
-    near = [v_ref[mine, c] for c in range(2)]
-    far = [v_ref[mine + 1, c] for c in range(2)]
+            value = recv_ref[band, c]
+            from_below[c] = from_below[c] + jnp.where(band < mine, value, 0.0)
+            from_above[c] = from_above[c] + jnp.where(band > mine, value, 0.0)
+    down, inverse, pivot = final_ref[0], final_ref[1], final_ref[2]
+    near = [(from_below[c] + down * from_above[c]) * pivot for c in range(2)]
+    far = [from_above[c] * inverse + down * near[c] for c in range(2)]
     lanes = lane_ids()
     both = dot(jnp.concatenate([near[0], far[0], near[1], far[1]], 0), dft_ref[...])
     total = [sum_ref[c] for c in range(2)]
@@ -384,70 +476,74 @@
         out_ref[block, :] = dot(jnp.concatenate([u_lo[block, :], u_hi[block, :]], 1), sine)
 
 
-def call(kernel, outs, scratch, *operands, scalars=()):
-    vmem = pl.BlockSpec(memory_space=pltpu.VMEM)
+def call(kernel, outs, scratch, *operands, scalars=(), far=(), manual=(), space=pltpu.VMEM):
     smem = pl.BlockSpec(memory_space=pltpu.SMEM)
-    shapes = [jax.ShapeDtypeStruct(s, F32) for s in outs]
+    specs = [smem if i in scalars else pl.BlockSpec(memory_space=space) for i in range(len(operands))]
+    if space == pltpu.HBM:
+        operands = [pltpu.with_memory_space_constraint(a, space) for a in operands]
     return pl.pallas_call(
         kernel,
-        out_shape=shapes,
-        in_specs=[smem if i in scalars else vmem for i in range(len(operands))],
-        out_specs=[vmem] * len(shapes),
-        scratch_shapes=[pltpu.VMEM(s, F32) for s in scratch],
+        out_shape=[(pltpu.HBM if i in far else pltpu.VMEM)(s, F32) for i, s in enumerate(outs)],
+        in_specs=specs,
+        out_specs=[pl.BlockSpec(memory_space=pltpu.HBM if i in manual else pltpu.VMEM) for i in range(len(outs))],
+        scratch_shapes=[pltpu.VMEM(s, F32) if isinstance(s, tuple) else s for s in scratch],
         compiler_params=pltpu.CompilerParams(vmem_limit_bytes=VMEM_LIMIT),
     )(*operands)
-
-
-def gather_bands(piece):
-    def along(values, near):
-        return [values] + [
-            lax.ppermute(values, "gy", [(a, near(a, s)) for a in range(BANDS)]) for s in range(1, 4)
-        ]
-
-    line = jnp.stack(along(piece, lambda a, s: a // 4 * 4 + (a + s) % 4))
-    return along(line, lambda a, s: (a + 4 * s) % BANDS)
 
 
 def per_device(rhs, metric, wavenumber):
     sine, edge = jnp.asarray(sine_table()), jnp.asarray(edge_table())
     dft, table = jnp.asarray(dft_table()), jnp.asarray(wave_table())
-    full = (ROWS, 8, COLS)
-    solved, local_ratio, send = call(
+    full, lines, half = (ROWS, 8, COLS), (ROWS, 2, 8, COLS), (1024, 128)
+    solved, send = call(
         local_kernel,
-        [(ROWS, 2, 8, COLS), full, (128, 128)],
-        [(ROWS, 2, 8, COLS), (1024, 128), (1024, 128)],
+        [lines, (128, 128)],
+        [
+            full, lines, half, half, (1024, COLS), (COLS, COLS), (3, 8, COLS),
+            pltpu.SMEM((1024,), F32), pltpu.SMEM((8,), F32),
+            pltpu.SemaphoreType.DMA((8,)), pltpu.SemaphoreType.DMA((4,)), pltpu.SemaphoreType.DMA((4,)),
+        ],
         rhs.reshape(1024, COLS), metric, wavenumber, sine, edge,
-        scalars=(1, 2),
+        space=pltpu.HBM, far=(0, 1), manual=(0,),
     )
     recv = lax.all_to_all(send.reshape(8, 16, 128), "gx", 0, 0, tiled=True)
-    alpha, beta, ratio, pivot, carry = call(
+    bands = (BANDS, 8, COLS)
+    (factor,) = call(
         factor_kernel,
-        [full, full, full, (BANDS, 8, COLS), (BANDS, 8, COLS)],
-        [],
+        [(3 * ROWS + 2 * BANDS + 3, 8, COLS)],
+        [bands, bands, bands],
         metric, 1.0 / metric, wavenumber, table,
         scalars=(0, 1, 2),
     )
-    piece, column = call(
+    send, own, column = call(
         spectrum_kernel,
-        [(4, 8, COLS), (2, 8, 128)],
-        [],
-        recv.reshape(128, 128), alpha, beta, dft, table, jnp.asarray(octet_forward()),
-    )
-    pieces = gather_bands(piece)
-    (total,) = call(column_kernel, [(2, 8, 128)], [(ROWS, 2, 8, COLS)], column, ratio)
+        [(BANDS, 2, 8, COLS), (4, 8, COLS), (2, 8, 128)],
+        [(BANDS, 2, 8, COLS), pltpu.SemaphoreType.DMA((BANDS,))],
+        recv.reshape(128, 128), factor, dft, table, jnp.asarray(octet_forward()),
+        far=(0,), manual=(0,),
+    )
+    recv = lax.all_to_all(send, "gy", 0, 0, tiled=True)
+    total, local_ratio = call(
+        column_kernel,
+        [(2, 8, 128), full],
+        [lines],
+        column, factor, metric, wavenumber, edge,
+        scalars=(2, 3),
+    )
     (send,) = call(
         separator_kernel,
         [(128, 128)],
-        [(BANDS, 4, 8, COLS), (BANDS + 1, 2, 8, COLS)],
-        *pieces, alpha, beta, pivot, carry, total, dft, table, jnp.asarray(octet_inverse()),
+        [],
+        recv, own, factor, total, dft, table, jnp.asarray(octet_inverse()),
+        far=(0,),
     )
     recv = lax.all_to_all(send.reshape(8, 16, 128), "gx", 0, 0, tiled=True)
     (out,) = call(
         finish_kernel,
         [(1024, COLS)],
-        [(ROWS, 2, 8, COLS), (1024, 128), (1024, 128)],
+        [lines, half, half],
         recv.reshape(128, 128), solved, local_ratio, metric, sine, edge,
-        scalars=(3,),
+        scalars=(3,), far=(0,),
     )
     return out.reshape(8, 2, ROWS, COLS)
 

time: 55.7 us -> 54.2 us (0.973)
  Pallas kernels: 14.3 us -> 19.5 us
  local copies, waits for them, and re-layouts: 5.08 us -> 2.13 us
  waiting for transfers between devices: 8.74 us -> 6.66 us
  blocking collectives: 12.8 us -> 10.9 us
  starting transfers between devices: 14.3 us -> 13.6 us
  other arithmetic: 0.01 us -> 0.69 us
    ppermute x6 -> x0, waiting for transfers between devices: 8.73 us -> none  [along(): lax.ppermute(values, 'gy', [(a, near(a, s)) for a in range(BANDS)])]
    ppermute x6 -> x0, starting transfers between devices: 8.2 us -> none  [along(): lax.ppermute(values, 'gy', [(a, near(a, s)) for a in range(BANDS)])]
    all_to_all x0 -> x1, starting transfers between devices: none -> 7.65 us  [per_device(): recv = lax.all_to_all(send, 'gy', 0, 0, tiled=True)]
    all_to_all x0 -> x1, waiting for transfers between devices: none -> 6.66 us  [per_device(): recv = lax.all_to_all(send, 'gy', 0, 0, tiled=True)]
    pallas_call x6, Pallas kernels: 14.3 us -> 19.5 us  [call(): pl.pallas_call(kernel, out_shape=[(pltpu.HBM if i in far else pltpu.VMEM)...]
    unnamed x28 -> x24, local copies, waits for them, and re-layouts: 5.08 us -> 2.13 us
    all_to_all x1, blocking collectives: 12.8 us -> 10.9 us  [per_device(): recv = lax.all_to_all(send.reshape(8, 16, 128), 'gx', 0, 0, tiled=True)]
    div x1, other arithmetic: 0.01 us -> 0.69 us  [per_device(): 1.0 / metric]
  transfers between devices with their start and end apart: 7 -> 2, of which waited for: 5 -> 1; matrix products, arithmetic and copies ran while one was open for 0% -> 1% of each run, Pallas kernels for 10% -> 11%
where the time goes in v1:
time: 54.2 us; the launch traced here: 53.7 us
  Pallas kernels  19.5 us (36%)
  starting transfers between devices  13.6 us (25%)
  blocking collectives  10.9 us (20%)
  waiting for transfers between devices  6.66 us (12%)
  local copies, waits for them, and re-layouts  2.13 us (4%)
  other arithmetic  0.69 us (1%)
    pallas_call x6, Pallas kernels, call(): pl.pallas_call(kernel, out_shape=[(pltpu.HBM if i in far else pltpu.VMEM)...  19.5 us
    all_to_all x1, blocking collectives, per_device(): recv = lax.all_to_all(send.reshape(8, 16, 128), 'gx', 0, 0, tiled=True)  10.9 us
    all_to_all x1, starting transfers between devices, per_device(): recv = lax.all_to_all(send, 'gy', 0, 0, tiled=True)  7.65 us
    all_to_all x1, waiting for transfers between devices, per_device(): recv = lax.all_to_all(send, 'gy', 0, 0, tiled=True)  6.66 us
    all_to_all x1, starting transfers between devices, per_device(): recv = lax.all_to_all(send.reshape(8, 16, 128), 'gx', 0, 0, tiled=True)  5.98 us
    unnamed x24, local copies, waits for them, and re-layouts  2.13 us
  transfers between devices with their start and end apart: 2, of which 1 were waited for; matrix products, arithmetic and copies ran while one was open for 1% of the time, Pallas kernels for 11%

profile of v1, /device:TPU:1, one launch (start us, length us, event | category | flops | bytes accessed | tf_op | source)
XLA Modules:
  0.0 53.7 jit_solution(13032102763250059257)
XLA Ops:
  0.0 0.0 copy-start.4
  0.0 0.0 copy-start
  0.0 0.0 copy-start.9
  0.0 6.5 %shard_map.91 = (f32[64,2,8,256]{3,2,1,0:T(8,128)}, f32[128,128]{1,0:T(8,128)}) custom-call(f32[1024,256]{1,0:T(8,128)} %bitcast.8, f32[1024]{0:T(1024)} %metric_ref.5, f32[8]{0:T(128)} %wave_ref.3, f32[256,256]{1,0:T(8,128)} %constant.14.clone.sine_hbm.sine_ref, f32[3,8,256]{2,1,0:T(8,128)} %constant.15.clone.edge_hbm.edge_ref), custom_call_target="tpu_custom_call" | custom-call | tf_op jit(solution)/shard_map/pallas_call | solution.py:484
  6.6 6.0 %all-to-all-start = ((f32[8,16,128]{2,1,0:T(8,128)}), f32[8,16,128]{2,1,0:T(8,128)S(1)}, u32[]{:S(2)}, u32[]{:S(2)}) async-start(f32[8,16,128]{2,1,0:T(8,128)} %bitcast.10), calls=%async_computation | async-start | bytes 131072 | tf_op jit(solution)/shard_map/all_to_all | solution.py:509
  12.5 0.7 %broadcast_divide_fusion.inverse_ref = f32[1024]{0:T(1024)S(1)} fusion(f32[1024]{0:T(1024)} %metric_ref.5), kind=kLoop, calls=%fused_computation | loop fusion | flops 1024 | bytes 8192 | tf_op jit(solution)/shard_map/div | solution.py:515
  13.2 0.0 copy-start.3
  13.2 0.7 %copy-done.3 = f32[3,8,256]{2,1,0:T(8,128)S(1)} copy-done((f32[3,8,256]{2,1,0:T(8,128)S(1)}, f32[3,8,256]{2,1,0:T(8,128)}, u32[]{:S(2)}) %copy-start.3) | copy-done | bytes 24600
  14.0 0.0 copy-start.6
  14.0 0.7 %copy-done.6 = f32[1024]{0:T(1024)S(1)} copy-done((f32[1024]{0:T(1024)S(1)}, f32[1024]{0:T(1024)}, u32[]{:S(2)}) %copy-start.6) | copy-done | bytes 4120
  14.7 0.0 copy-start.10
  14.7 0.7 %copy-done.10 = f32[8]{0:T(128)S(1)} copy-done((f32[8]{0:T(128)S(1)}, f32[8]{0:T(128)}, u32[]{:S(2)}) %copy-start.10) | copy-done | bytes 56
  15.3 5.0 %shard_map.92.factor_ref = f32[227,8,256]{2,1,0:T(8,128)S(1)} custom-call(f32[1024]{0:T(1024)S(1)} %copy-done.6, f32[1024]{0:T(1024)S(1)} %broadcast_divide_fusion.inverse_ref, f32[8]{0:T(128)S(1)} %copy-done.10, f32[3,8,256]{2,1,0:T(8,128)S(1)} %copy-done.3), custom_call_target="tpu_custom_call" | custom-call | tf_op jit(solution)/shard_map/pallas_call | solution.py:484
  20.3 0.0 copy-start.5
  20.3 0.0 copy-start.7
  20.4 0.0 copy-start.11
  20.4 0.0 all-to-all-done
  20.4 0.0 copy-done.4
  20.4 0.0 copy-done
  20.4 0.0 copy-done.9
  20.4 0.0 copy-start.8
  20.4 1.5 %shard_map.93 = (f32[16,2,8,256]{3,2,1,0:T(8,128)}, f32[4,8,256]{2,1,0:T(8,128)S(1)}, f32[2,8,128]{2,1,0:T(8,128)S(1)}) custom-call(f32[128,128]{1,0:T(8,128)S(1)} %bitcast.6, f32[227,8,256]{2,1,0:T(8,128)S(1)} %shard_map.92.factor_ref, f32[256,512]{1,0:T(8,128)S(1)} %copy-done, f32[3,8,256]{2,1,0:T(8,128)S(1)} %copy-done.4, f32[16,16]{1,0:T(8,128)S(1)} %copy-done.9), custom_call_target="tpu_custom_call" | custom-call | tf_op jit(solution)/shard_map/pallas_call | solution.py:484
  21.9 7.7 %all-to-all-start.1 = ((f32[16,2,8,256]{3,2,1,0:T(8,128)}), f32[16,2,8,256]{3,2,1,0:T(8,128)S(1)}, u32[]{:S(2)}, u32[]{:S(2)}) async-start(f32[16,2,8,256]{3,2,1,0:T(8,128)} %get-tuple-element.13), calls=%async_computation.1 | async-start | bytes 524288 | tf_op jit(solution)/shard_map/all_to_all | solution.py:525
  29.5 0.0 copy-done.5
  29.6 0.0 copy-done.7
  29.6 0.0 copy-done.11
  29.6 1.1 %shard_map.94 = (f32[2,8,128]{2,1,0:T(8,128)S(1)}, f32[64,8,256]{2,1,0:T(8,128)S(1)}) custom-call(f32[2,8,128]{2,1,0:T(8,128)S(1)} %get-tuple-element.15.column_ref, f32[227,8,256]{2,1,0:T(8,128)S(1)} %shard_map.92.factor_ref, f32[1024]{0:T(1024)S(1)} %copy-done.7, f32[8]{0:T(128)S(1)} %copy-done.11, f32[3,8,256]{2,1,0:T(8,128)S(1)} %copy-done.5), custom_call_target="tpu_custom_call" | custom-call | tf_op jit(solution)/shard_map/pallas_call | solution.py:484
  30.7 0.0 copy-start.1
  30.7 6.7 %all-to-all-done.1.recv_ref = f32[16,2,8,256]{3,2,1,0:T(8,128)S(1)} async-done(((f32[16,2,8,256]{3,2,1,0:T(8,128)}), f32[16,2,8,256]{3,2,1,0:T(8,128)S(1)}, u32[]{:S(2)}, u32[]{:S(2)}) %all-to-all-start.1) | async-done | bytes 262176 | tf_op jit(solution)/shard_map/all_to_all | solution.py:525
  37.4 0.0 copy-start.2
  37.4 0.0 copy-done.8
  37.4 1.5 %shard_map.95 = f32[128,128]{1,0:T(8,128)} custom-call(f32[16,2,8,256]{3,2,1,0:T(8,128)S(1)} %all-to-all-done.1.recv_ref, f32[4,8,256]{2,1,0:T(8,128)S(1)} %get-tuple-element.14.own_ref, f32[227,8,256]{2,1,0:T(8,128)S(1)} %shard_map.92.factor_ref, f32[2,8,128]{2,1,0:T(8,128)S(1)} %get-tuple-element.16.sum_ref, f32[256,512]{1,0:T(8,128)S(1)} %copy-done, ...), custom_call_target="tpu_custom_call" | custom-call | tf_op jit(solution)/shard_map/pallas_call | solution.py:484
  38.9 10.9 %all_to_all.15 = f32[8,16,128]{2,1,0:T(8,128)S(1)} all-to-all(f32[8,16,128]{2,1,0:T(8,128)} %bitcast.9), channel_id=1, replica_groups=mesh['gx'=8,'gy'=16] {'gx'}, dimensions={0} | all-to-all | bytes 131072 | tf_op jit(solution)/shard_map/all_to_all | solution.py:540
  49.8 0.0 copy-done.1
  49.8 0.0 copy-done.2
  49.8 3.9 %shard_map.96 = f32[1024,256]{1,0:T(8,128)} custom-call(f32[128,128]{1,0:T(8,128)S(1)} %bitcast.7, f32[64,2,8,256]{3,2,1,0:T(8,128)S(1)} %copy-done.2, f32[64,8,256]{2,1,0:T(8,128)S(1)} %get-tuple-element.18.ratio_ref, f32[1024]{0:T(1024)S(1)} %copy-done.7, f32[256,256]{1,0:T(8,128)S(1)} %copy-done.1, f32[3,8,256]{2,1,0:T(8,128)S(1)} %copy-done.5), custom_call_target="tpu_custom_call" | custom-call | tf_op jit(solution)/shard_map/pallas_call | solution.py:484
Async XLA Ops:
  0.0 20.4 %copy-start.4 = (f32[3,8,256]{2,1,0:T(8,128)S(1)}, f32[3,8,256]{2,1,0:T(8,128)}, u32[]{:S(2)}) copy-start(f32[3,8,256]{2,1,0:T(8,128)} %constant.17.clone.table_ref) | copy-start | bytes 73732
  0.0 20.4 %copy-start = (f32[256,512]{1,0:T(8,128)S(1)}, f32[256,512]{1,0:T(8,128)}, u32[]{:S(2)}) copy-start(f32[256,512]{1,0:T(8,128)} %constant.16.clone.dft_ref) | copy-start | bytes 1572868
  0.0 20.4 %copy-start.9 = (f32[16,16]{1,0:T(8,128)S(1)}, f32[16,16]{1,0:T(8,128)}, u32[]{:S(2)}) copy-start(f32[16,16]{1,0:T(8,128)} %constant.18.clone.octet_ref) | copy-start | bytes 3076
  6.6 13.8 %all-to-all-start = ((f32[8,16,128]{2,1,0:T(8,128)}), f32[8,16,128]{2,1,0:T(8,128)S(1)}, u32[]{:S(2)}, u32[]{:S(2)}) async-start(f32[8,16,128]{2,1,0:T(8,128)} %bitcast.10), calls=%async_computation | async-start | bytes 131072 | tf_op jit(solution)/shard_map/all_to_all | solution.py:509
  13.2 0.7 %copy-start.3 = (f32[3,8,256]{2,1,0:T(8,128)S(1)}, f32[3,8,256]{2,1,0:T(8,128)}, u32[]{:S(2)}) copy-start(f32[3,8,256]{2,1,0:T(8,128)} %constant.17.clone.table_ref) | copy-start | bytes 73732
  14.0 0.7 %copy-start.6 = (f32[1024]{0:T(1024)S(1)}, f32[1024]{0:T(1024)}, u32[]{:S(2)}) copy-start(f32[1024]{0:T(1024)} %metric_ref.5) | copy-start | bytes 12292
  14.7 0.7 %copy-start.10 = (f32[8]{0:T(128)S(1)}, f32[8]{0:T(128)}, u32[]{:S(2)}) copy-start(f32[8]{0:T(128)} %wave_ref.3) | copy-start | bytes 100
  20.3 9.2 %copy-start.5 = (f32[3,8,256]{2,1,0:T(8,128)S(1)}, f32[3,8,256]{2,1,0:T(8,128)}, u32[]{:S(2)}) copy-start(f32[3,8,256]{2,1,0:T(8,128)} %constant.15.clone.edge_hbm.edge_ref) | copy-start | bytes 73732
  20.3 9.2 %copy-start.7 = (f32[1024]{0:T(1024)S(1)}, f32[1024]{0:T(1024)}, u32[]{:S(2)}) copy-start(f32[1024]{0:T(1024)} %metric_ref.5) | copy-start | bytes 12292
  20.4 9.2 %copy-start.11 = (f32[8]{0:T(128)S(1)}, f32[8]{0:T(128)}, u32[]{:S(2)}) copy-start(f32[8]{0:T(128)} %wave_ref.3) | copy-start | bytes 100
  20.4 17.0 %copy-start.8 = (f32[32,16]{1,0:T(8,128)S(1)}, f32[32,16]{1,0:T(8,128)}, u32[]{:S(2)}) copy-start(f32[32,16]{1,0:T(8,128)} %constant.19.clone.octet_ref) | copy-start | bytes 6148
  21.9 15.5 %all-to-all-start.1 = ((f32[16,2,8,256]{3,2,1,0:T(8,128)}), f32[16,2,8,256]{3,2,1,0:T(8,128)S(1)}, u32[]{:S(2)}, u32[]{:S(2)}) async-start(f32[16,2,8,256]{3,2,1,0:T(8,128)} %get-tuple-element.13), calls=%async_computation.1 | async-start | bytes 524288 | tf_op jit(solution)/shard_map/all_to_all | solution.py:525
  30.7 19.1 %copy-start.1 = (f32[256,256]{1,0:T(8,128)S(1)}, f32[256,256]{1,0:T(8,128)}, u32[]{:S(2)}) copy-start(f32[256,256]{1,0:T(8,128)} %constant.14.clone.sine_hbm.sine_ref) | copy-start | bytes 786436
  37.4 12.4 %copy-start.2 = (f32[64,2,8,256]{3,2,1,0:T(8,128)S(1)}, f32[64,2,8,256]{3,2,1,0:T(8,128)}, u32[]{:S(2)}) copy-start(f32[64,2,8,256]{3,2,1,0:T(8,128)} %get-tuple-element.17.solved_ref) | copy-start | bytes 3145732

commit v2 on v1

--- a/solution.py
+++ b/solution.py
@@ -40,7 +40,9 @@
     left[0] = right[0] = 0.0
     along = 4.0 * np.sin(np.pi * ramp / (2 * COLS)) ** 2
     rows = [ASPECT * left, ASPECT * right, ASPECT * along]
-    return f32(np.stack([np.broadcast_to(r, (8, COLS)) for r in rows]))
+    kappa = np.arange(STRIPS)[:, None]
+    whole = ASPECT * (2.0 * np.sin(np.pi * (STRIPS * ramp[None, :] + kappa) / NX)) ** 2
+    return f32(np.stack([np.broadcast_to(r, (8, COLS)) for r in rows] + [whole]))
 
 
 def dft_table():
@@ -53,8 +55,7 @@
     kappa = np.arange(STRIPS)[:, None]
     j = np.arange(COLS)[None, :]
     angle = 2.0 * np.pi * j * kappa / NX
-    along = ASPECT * (2.0 * np.sin(np.pi * (STRIPS * j + kappa) / NX)) ** 2
-    return f32(np.stack([np.cos(angle), np.sin(angle), along]))
+    return f32(np.stack([np.cos(angle), np.sin(angle)]))
 
 
 def octet_forward():
@@ -90,8 +91,12 @@
     return wide(jnp.sum(values[:, :128] + values[:, 128:], axis=1, keepdims=True))
 
 
-def splat_inverse(metric_ref, index):
-    return 1.0 / jnp.full((8, COLS), metric_ref[index], F32)
+def entry(ref, row):
+    return ref[row // 128, row % 128]
+
+
+def splat_inverse(metric_ref, row):
+    return 1.0 / jnp.full((8, COLS), entry(metric_ref, row), F32)
 
 
 def local_shift(wave_ref, edge_ref):
@@ -103,47 +108,62 @@
 
 
 def local_kernel(
-    rhs_hbm, metric_hbm, wave_hbm, sine_hbm, edge_hbm, solved_hbm, send_ref,
-    ratio_ref, z_ref, f_lo, f_hi, rhs_ref, sine_ref, edge_ref, metric_ref, wave_ref, rhs_sem, sems, out_sem,
+    rhs_hbm, metric_hbm, wave_hbm, sine_hbm, edge_hbm, solved_hbm, send_ref, metrics_ref, shift_ref,
+    ratio_ref, z_ref, r_lo, r_hi, sine_ref, edge_ref, metric_vec, metric_ref, wave_ref, rhs_sem, sems, out_sem,
 ):
     first = lax.axis_index("gy") * ROWS
-    small = [
-        pltpu.make_async_copy(a, b, sems.at[i])
-        for i, (a, b) in enumerate(
-            ((sine_hbm, sine_ref), (metric_hbm, metric_ref), (wave_hbm, wave_ref), (edge_hbm, edge_ref))
+    pairs = (
+        (metric_hbm, metric_ref), (wave_hbm, wave_ref), (edge_hbm, edge_ref), (metric_hbm, metric_vec), (sine_hbm, sine_ref)
+    )
+    small = [pltpu.make_async_copy(a, b, sems.at[i]) for i, (a, b) in enumerate(pairs)]
+    half = ROWS // 2
+    large = [
+        pltpu.make_async_copy(
+            rhs_hbm.at[:, pl.ds(part * half, half), pl.ds(side * 128, 128)],
+            ref.at[:, pl.ds(part * half, half), :],
+            rhs_sem.at[part * 2 + side],
         )
+        for part in range(2)
+        for side, ref in enumerate((r_lo, r_hi))
     ]
-    blocks = [pl.ds(mode * 2 * ROWS, 2 * ROWS) for mode in range(8)]
-    large = [pltpu.make_async_copy(rhs_hbm.at[b], rhs_ref.at[b], rhs_sem.at[i]) for i, b in enumerate(blocks)]
-    small[0].start()
-    for copy in large[:2] + small[1:] + large[2:]:
+    for copy in small + large:
         copy.start()
-    small[0].wait()
-    sine = sine_ref[...]
-    for mode in range(8):
-        large[mode].wait()
-        lines = dot(rhs_ref[blocks[mode], :], sine)
-        f_lo[blocks[mode], :] = lines[:, :128]
-        f_hi[blocks[mode], :] = lines[:, 128:]
-    for copy in small[1:]:
+    for copy in small[:4]:
         copy.wait()
+    metrics_ref[:8, :] = metric_vec[...]
+    metrics_ref[8:, :] = 1.0 / metric_vec[...]
+    shift_ref[...] = edge_ref[3] + wave_ref[lax.axis_index("gx")]
     lanes = lane_ids()
     shift = local_shift(wave_ref, edge_ref)
     height = jnp.ones((8, COLS), F32)
     slope = jnp.ones((8, COLS), F32)
+    for y in range(1, ROWS):
+        slope = slope + shift * splat_inverse(metric_ref, first + y) * height
+        taller = height + slope
+        ratio_ref[y] = height / taller
+        height = taller
+    small[4].wait()
+    sine = sine_ref[...]
+    flat = [ref.reshape(16 * ROWS, 128) for ref in (r_lo, r_hi)]
+
+    def line(y, c):
+        rows = pl.ds(c * ROWS + y, 8, stride=2 * ROWS)
+        return jnp.concatenate([ref[rows, :] for ref in flat], 1)
+
     state = [jnp.zeros((8, COLS), F32)] * 2
-    for y in range(1, ROWS):
-        inverse = splat_inverse(metric_ref, first + y)
-        slope = slope + shift * inverse * height
-        taller = height + slope
-        ratio = height / taller
-        height = taller
-        ratio_ref[y] = ratio
-        for c in range(2):
-            rows = pl.ds(c * ROWS + y, 8, stride=2 * ROWS)
-            line = jnp.concatenate([f_lo[rows, :], f_hi[rows, :]], 1)
-            state[c] = (line * inverse + state[c]) * ratio
-            z_ref[y, c] = state[c]
+    group = 8
+    for base in range(0, ROWS, group):
+        if base % half == 0:
+            for copy in large[base // half * 2 : base // half * 2 + 2]:
+                copy.wait()
+        lines = dot(jnp.concatenate([line(y, c) for y in range(base, base + group) for c in range(2)], 0), sine)
+        for y in range(max(base, 1), base + group):
+            ratio = ratio_ref[y]
+            inverse = splat_inverse(metric_ref, first + y)
+            for c in range(2):
+                at = ((y - base) * 2 + c) * 8
+                state[c] = (lines[at : at + 8] * inverse + state[c]) * ratio
+                z_ref[y, c] = state[c]
     left = edge_ref[0]
     right = edge_ref[1]
     columns = [[jnp.zeros((8, 128), F32)] * 2 for _ in range(2)]
@@ -155,13 +175,11 @@
         for c in range(2):
             upper[c] = z_ref[y, c] + ratio * upper[c]
             z_ref[y, c] = upper[c]
-            scaled = upper[c] * inverse
-            a = scaled * left
-            a = a[:, :128] + a[:, 128:] + jnp.where(
-                lanes == 0, f_lo[pl.ds(c * ROWS + y, 8, stride=2 * ROWS), :] * inverse[:, :128], 0.0
-            )
-            b = scaled * right
-            b = b[:, :128] + b[:, 128:]
+            a = upper[c] * left
+            source = flat[0][pl.ds(c * ROWS + y, 8, stride=2 * ROWS), :]
+            a = (a[:, :128] + a[:, 128:] + jnp.where(lanes == 0, source, 0.0)) * inverse[:, :128]
+            b = upper[c] * right
+            b = (b[:, :128] + b[:, 128:]) * inverse[:, :128]
             columns[0][c] = jnp.where(lanes == y, wide(jnp.sum(a, axis=1, keepdims=True)), columns[0][c])
             columns[1][c] = jnp.where(lanes == y + ROWS, wide(jnp.sum(b, axis=1, keepdims=True)), columns[1][c])
         if y % 16 == 0:
@@ -175,14 +193,12 @@
     zero_lane = lax.broadcasted_iota(jnp.int32, (8, COLS), 1) == 0
     inverse = splat_inverse(metric_ref, first)
     for c in range(2):
-        near = jnp.where(zero_lane, 0.0, edges[c * 8 : c * 8 + 8])
-        row = [rhs_ref[(mode * 2 + c) * ROWS : (mode * 2 + c) * ROWS + 1, :] for mode in range(8)]
-        near = near + jnp.concatenate(row, 0) * inverse
+        near = jnp.where(zero_lane, 0.0, edges[c * 8 : c * 8 + 8]) + line(0, c) * inverse
         far = jnp.where(zero_lane, 0.0, edges[16 + c * 8 : 24 + c * 8])
-        for half in range(2):
-            part = slice(half * 128, half * 128 + 128)
-            send_ref[pl.ds(c * 2 + half, 8, stride=16), :] = near[:, part]
-            send_ref[pl.ds(4 + c * 2 + half, 8, stride=16), :] = far[:, part]
+        for i in range(2):
+            part = slice(i * 128, i * 128 + 128)
+            send_ref[pl.ds(c * 2 + i, 8, stride=16), :] = near[:, part]
+            send_ref[pl.ds(4 + c * 2 + i, 8, stride=16), :] = far[:, part]
         send_ref[pl.ds(8 + c, 8, stride=16), :] = jnp.where(lanes < ROWS, columns[0][c], columns[1][c])
         for pad in range(3):
             send_ref[pl.ds(10 + c * 3 + pad, 8, stride=16), :] = jnp.zeros((8, 128), F32)
@@ -197,15 +213,15 @@
 
 
 def factor_kernel(
-    metric_ref, inverse_ref, wave_ref, table_ref, factor_ref, gamma_ref, base_ref, x_ref
+    metrics_ref, shift_ref, factor_ref, gamma_ref, base_ref, x_ref
 ):
     alpha_ref, beta_ref, ratio_ref, up_ref, down_ref, final_ref = factors(factor_ref)
     mine = lax.axis_index("gy")
-    shift = table_ref[2] + wave_ref[lax.axis_index("gx")]
+    shift = shift_ref[...]
 
     def excess(row):
-        double = 2.0 * metric_ref[row]
-        return ((double + shift) - double) * inverse_ref[row]
+        double = 2.0 * entry(metrics_ref, row)
+        return ((double + shift) - double) * entry(metrics_ref, 1024 + row)
 
     one = jnp.ones((8, COLS), F32)
     zero = jnp.zeros((8, COLS), F32)
@@ -213,7 +229,7 @@
 
     def bands(outer, carry):
         excess_below, flow = carry
-        state = [(one, zero, zero, zero)] * together
+        state = [(one, one, zero, zero)] * together
 
         def rows(y, state):
             out = []
@@ -221,13 +237,13 @@
                 height, slope, rest, rise = state[i]
                 t = excess((outer * together + i) * ROWS + y)
                 slope = slope + t * height
-                height = height + (slope + 1.0)
+                height = height + slope
                 rise = rise + t * (rest + 1.0)
                 rest = rest + rise
                 out.append((height, slope, rest, rise))
             return tuple(out)
 
-        state = lax.fori_loop(1, ROWS, rows, tuple(state), unroll=7)
+        state = lax.fori_loop(1, ROWS, rows, tuple(state), unroll=21)
         for i in range(together):
             height, slope, rest, _ = state[i]
             band = outer * together + i
@@ -239,7 +255,7 @@
             base_ref[band] = base
             x_ref[band] = x
             up_ref[band] = up
-            excess_below = slope * gamma
+            excess_below = (slope - 1.0) * gamma
             flow = up * x
         return excess_below, flow
 
@@ -280,7 +296,7 @@
 
 
 def spectrum_kernel(
-    recv_ref, factor_ref, dft_ref, table_ref, octet_ref, send_hbm, own_ref, column_ref, send_ref, sem
+    recv_ref, factor_ref, dft_ref, table_ref, octet_ref, send_ref, own_ref, column_ref
 ):
     alpha_ref, beta_ref, _, up_ref, down_ref, _ = factors(factor_ref)
     mine = lax.axis_index("gy")
@@ -327,18 +343,12 @@
         own_ref[c], own_ref[2 + c] = sides[0][c], sides[1][c]
         column_ref[c] = columns[c]
         send_ref[mine, c] = jnp.zeros((8, COLS), F32)
-
-    def copy(band):
-        return pltpu.make_async_copy(send_ref.at[band], send_hbm.at[band], sem.at[band])
-
-    copy(mine).start()
     up, down = up_ref[mine], down_ref[mine]
 
     def above(band, carry):
         factor = up_ref[band]
         for c in range(2):
             send_ref[band, c] = carry[c]
-        copy(band).start()
         return tuple(value * factor for value in carry)
 
     def below(step, carry):
@@ -346,13 +356,10 @@
         factor = down_ref[band]
         for c in range(2):
             send_ref[band, c] = carry[c]
-        copy(band).start()
         return tuple(value * factor for value in carry)
 
     lax.fori_loop(mine + 1, BANDS, above, tuple(sides[1][c] + up * sides[0][c] for c in range(2)))
     lax.fori_loop(0, mine, below, tuple(sides[0][c] + down * sides[1][c] for c in range(2)))
-    for band in range(BANDS):
-        copy(band).wait()
 
 
 def column_kernel(column_ref, factor_ref, metric_ref, wave_ref, edge_ref, sum_ref, local_ref, z_ref):
@@ -433,7 +440,7 @@
             send_ref[pl.ds(10 + c * 3 + pad, 8, stride=16), :] = jnp.zeros((8, 128), F32)
 
 
-def finish_kernel(recv_ref, solved_ref, ratio_ref, metric_ref, sine_ref, edge_ref, out_ref, z_ref, u_lo, u_hi):
+def finish_kernel(recv_ref, solved_ref, ratio_ref, metric_ref, sine_ref, edge_ref, out_hbm, z_ref, o_lo, o_hi, sems):
     first = lax.axis_index("gy") * ROWS
 
     def take(i):
@@ -456,24 +463,40 @@
             there = wide(columns[c][:, ROWS + y : ROWS + y + 1])
             here = jnp.concatenate([here, here], 1)
             there = jnp.concatenate([there, there], 1)
-            state[c] = (state[c] + a * here + b * there) * ratio
+            state[c] = (state[c] + (a * here + b * there)) * ratio
             z_ref[y, c] = state[c]
     upper = [edges[16 + c * 8 : 24 + c * 8] for c in range(2)]
-    for y in range(ROWS - 1, -1, -1):
-        for c in range(2):
-            if y:
-                upper[c] = z_ref[y, c] + ratio_ref[y] * upper[c]
-                here = wide(columns[c][:, y : y + 1])
-                here = jnp.concatenate([here, here], 1)
-                line = jnp.where(zero_lane, here, upper[c] + solved_ref[y, c])
-            else:
-                line = edges[c * 8 : c * 8 + 8]
-            rows = pl.ds(c * ROWS + y, 8, stride=2 * ROWS)
-            u_lo[rows, :] = line[:, :128]
-            u_hi[rows, :] = line[:, 128:]
-    for mode in range(8):
-        block = slice(mode * 2 * ROWS, (mode + 1) * 2 * ROWS)
-        out_ref[block, :] = dot(jnp.concatenate([u_lo[block, :], u_hi[block, :]], 1), sine)
+    flat = [ref.reshape(16 * ROWS, 128) for ref in (o_lo, o_hi)]
+    group, half = 8, ROWS // 2
+    copies = []
+    for base in range(ROWS - group, -1, -group):
+        lines = []
+        for y in range(base + group - 1, base - 1, -1):
+            for c in range(2):
+                if y:
+                    upper[c] = z_ref[y, c] + ratio_ref[y] * upper[c]
+                    here = wide(columns[c][:, y : y + 1])
+                    here = jnp.concatenate([here, here], 1)
+                    lines.append(jnp.where(zero_lane, here, upper[c] + solved_ref[y, c]))
+                else:
+                    lines.append(edges[c * 8 : c * 8 + 8])
+        product = dot(jnp.concatenate(lines, 0), sine)
+        for i in range(2 * group):
+            rows = pl.ds(i % 2 * ROWS + base + group - 1 - i // 2, 8, stride=2 * ROWS)
+            flat[0][rows, :] = product[i * 8 : i * 8 + 8, :128]
+            flat[1][rows, :] = product[i * 8 : i * 8 + 8, 128:]
+        if base % half == 0:
+            for side, ref in enumerate((o_lo, o_hi)):
+                copies.append(
+                    pltpu.make_async_copy(
+                        ref.at[:, pl.ds(base, half), :],
+                        out_hbm.at[:, pl.ds(base, half), pl.ds(side * 128, 128)],
+                        sems.at[len(copies)],
+                    )
+                )
+                copies[-1].start()
+    for copy in copies:
+        copy.wait()
 
 
 def call(kernel, outs, scratch, *operands, scalars=(), far=(), manual=(), space=pltpu.VMEM):
@@ -494,33 +517,33 @@
 def per_device(rhs, metric, wavenumber):
     sine, edge = jnp.asarray(sine_table()), jnp.asarray(edge_table())
     dft, table = jnp.asarray(dft_table()), jnp.asarray(wave_table())
-    full, lines, half = (ROWS, 8, COLS), (ROWS, 2, 8, COLS), (1024, 128)
-    solved, send = call(
+    metric = metric.reshape(8, 128)
+    full, lines, side, bands = (ROWS, 8, COLS), (ROWS, 2, 8, COLS), (16, ROWS, 128), (BANDS, 8, COLS)
+    solved, send, metrics, shift = call(
         local_kernel,
-        [lines, (128, 128)],
+        [lines, (128, 128), (16, 128), (8, COLS)],
         [
-            full, lines, half, half, (1024, COLS), (COLS, COLS), (3, 8, COLS),
-            pltpu.SMEM((1024,), F32), pltpu.SMEM((8,), F32),
-            pltpu.SemaphoreType.DMA((8,)), pltpu.SemaphoreType.DMA((4,)), pltpu.SemaphoreType.DMA((4,)),
+            full, lines, side, side, (COLS, COLS), (4, 8, COLS), (8, 128),
+            pltpu.SMEM((8, 128), F32), pltpu.SMEM((8,), F32),
+            pltpu.SemaphoreType.DMA((4,)), pltpu.SemaphoreType.DMA((5,)), pltpu.SemaphoreType.DMA((4,)),
         ],
-        rhs.reshape(1024, COLS), metric, wavenumber, sine, edge,
+        rhs.reshape(16, ROWS, COLS), metric, wavenumber, sine, edge,
         space=pltpu.HBM, far=(0, 1), manual=(0,),
     )
     recv = lax.all_to_all(send.reshape(8, 16, 128), "gx", 0, 0, tiled=True)
-    bands = (BANDS, 8, COLS)
     (factor,) = call(
         factor_kernel,
         [(3 * ROWS + 2 * BANDS + 3, 8, COLS)],
         [bands, bands, bands],
-        metric, 1.0 / metric, wavenumber, table,
-        scalars=(0, 1, 2),
+        metrics, shift,
+        scalars=(0,),
     )
     send, own, column = call(
         spectrum_kernel,
         [(BANDS, 2, 8, COLS), (4, 8, COLS), (2, 8, 128)],
-        [(BANDS, 2, 8, COLS), pltpu.SemaphoreType.DMA((BANDS,))],
+        [],
         recv.reshape(128, 128), factor, dft, table, jnp.asarray(octet_forward()),
-        far=(0,), manual=(0,),
+        far=(0,),
     )
     recv = lax.all_to_all(send, "gy", 0, 0, tiled=True)
     total, local_ratio = call(
@@ -535,15 +558,14 @@
         [(128, 128)],
         [],
         recv, own, factor, total, dft, table, jnp.asarray(octet_inverse()),
-        far=(0,),
     )
     recv = lax.all_to_all(send.reshape(8, 16, 128), "gx", 0, 0, tiled=True)
     (out,) = call(
         finish_kernel,
-        [(1024, COLS)],
-        [lines, half, half],
+        [(16, ROWS, COLS)],
+        [lines, side, side, pltpu.SemaphoreType.DMA((4,))],
         recv.reshape(128, 128), solved, local_ratio, metric, sine, edge,
-        scalars=(3,), far=(0,),
+        scalars=(3,), far=(0,), manual=(0,),
     )
     return out.reshape(8, 2, ROWS, COLS)
 

time: 54.2 us -> 60.9 us (1.12)
  Pallas kernels: 19.5 us -> 29.5 us
  local copies, waits for them, and re-layouts: 2.13 us -> 0.05 us
  other arithmetic: 0.69 us -> 0 us
    pallas_call x6, Pallas kernels: 19.5 us -> 29.5 us  [call(): pl.pallas_call(kernel, out_shape=[(pltpu.HBM if i in far else pltpu.VMEM)...]
    unnamed x24 -> x18, local copies, waits for them, and re-layouts: 2.13 us -> 0.05 us
    div x1 -> x0, other arithmetic: 0.69 us -> none  [per_device(): 1.0 / metric]
  transfers between devices with their start and end apart: 2 -> 2, of which waited for: 1 -> 1; matrix products, arithmetic and copies ran while one was open for 1% -> 0% of each run, Pallas kernels for 11% -> 31%
where the time goes in v2:
time: 60.9 us; the launch traced here: 60.6 us
  Pallas kernels  29.5 us (48%)
  starting transfers between devices  13.6 us (22%)
  blocking collectives  10.8 us (18%)
  waiting for transfers between devices  6.5 us (11%)
    pallas_call x6, Pallas kernels, call(): pl.pallas_call(kernel, out_shape=[(pltpu.HBM if i in far else pltpu.VMEM)...  29.5 us
    all_to_all x1, blocking collectives, per_device(): recv = lax.all_to_all(send.reshape(8, 16, 128), 'gx', 0, 0, tiled=True)  10.8 us
    all_to_all x1, starting transfers between devices, per_device(): recv = lax.all_to_all(send, 'gy', 0, 0, tiled=True)  7.6 us
    all_to_all x1, waiting for transfers between devices, per_device(): recv = lax.all_to_all(send, 'gy', 0, 0, tiled=True)  6.5 us
    all_to_all x1, starting transfers between devices, per_device(): recv = lax.all_to_all(send.reshape(8, 16, 128), 'gx', 0, 0, tiled=True)  5.98 us
  transfers between devices with their start and end apart: 2, of which 1 were waited for; matrix products, arithmetic and copies ran while one was open for 0% of the time, Pallas kernels for 31%

profile of v2, /device:TPU:1, one launch (start us, length us, event | category | flops | bytes accessed | tf_op | source)
XLA Modules:
  0.0 60.6 jit_solution(16528655852423106436)
XLA Ops:
  0.0 0.0 copy-start.4
  0.0 0.0 copy-start
  0.0 0.0 copy-start.7
  0.0 4.8 %shard_map.91 = (f32[64,2,8,256]{3,2,1,0:T(8,128)}, f32[128,128]{1,0:T(8,128)}, f32[16,128]{1,0:T(8,128)S(1)}, f32[8,256]{1,0:T(8,128)S(1)}) custom-call(f32[16,64,256]{2,1,0:T(8,128)} %bitcast.13, f32[8,128]{1,0:T(8,128)} %bitcast.10, f32[8]{0:T(128)} %wave_ref.1, f32[256,256]{1,0:T(8,128)} %constant.12.clone.sine_hbm.sine_ref, ...), custom_call_target="tpu_custom_call" | custom-call | tf_op jit(solution)/shard_map/pallas_call | solution.py:507
  4.9 6.0 %all-to-all-start = ((f32[8,16,128]{2,1,0:T(8,128)}), f32[8,16,128]{2,1,0:T(8,128)S(1)}, u32[]{:S(2)}, u32[]{:S(2)}) async-start(f32[8,16,128]{2,1,0:T(8,128)} %bitcast.14), calls=%async_computation | async-start | bytes 131072 | tf_op jit(solution)/shard_map/all_to_all | solution.py:533
  10.8 17.4 %shard_map.92.factor_ref = f32[227,8,256]{2,1,0:T(8,128)S(1)} custom-call(f32[16,128]{1,0:T(8,128)S(1)} %get-tuple-element.15.metrics_ref, f32[8,256]{1,0:T(8,128)S(1)} %get-tuple-element.16.shift_ref), custom_call_target="tpu_custom_call" | custom-call | tf_op jit(solution)/shard_map/pallas_call | solution.py:507
  28.2 0.0 copy-start.3
  28.3 0.0 copy-start.5
  28.3 0.0 copy-start.8
  28.3 0.0 all-to-all-done
  28.3 0.0 copy-done.4
  28.3 0.0 copy-done
  28.3 0.0 copy-done.7
  28.3 0.0 copy-start.6
  28.3 1.4 %shard_map.93 = (f32[16,2,8,256]{3,2,1,0:T(8,128)}, f32[4,8,256]{2,1,0:T(8,128)S(1)}, f32[2,8,128]{2,1,0:T(8,128)S(1)}) custom-call(f32[128,128]{1,0:T(8,128)S(1)} %bitcast.7, f32[227,8,256]{2,1,0:T(8,128)S(1)} %shard_map.92.factor_ref, f32[256,512]{1,0:T(8,128)S(1)} %copy-done, f32[2,8,256]{2,1,0:T(8,128)S(1)} %copy-done.4, f32[16,16]{1,0:T(8,128)S(1)} %copy-done.7), custom_call_target="tpu_custom_call" | custom-call | tf_op jit(solution)/shard_map/pallas_call | solution.py:507
  29.7 7.6 %all-to-all-start.1 = ((f32[16,2,8,256]{3,2,1,0:T(8,128)}), f32[16,2,8,256]{3,2,1,0:T(8,128)S(1)}, u32[]{:S(2)}, u32[]{:S(2)}) async-start(f32[16,2,8,256]{3,2,1,0:T(8,128)} %get-tuple-element.17), calls=%async_computation.1 | async-start | bytes 524288 | tf_op jit(solution)/shard_map/all_to_all | solution.py:548
  37.3 0.0 copy-done.3
  37.3 0.0 copy-done.5
  37.4 0.0 copy-done.8
  37.4 1.3 %shard_map.94 = (f32[2,8,128]{2,1,0:T(8,128)S(1)}, f32[64,8,256]{2,1,0:T(8,128)S(1)}) custom-call(f32[2,8,128]{2,1,0:T(8,128)S(1)} %get-tuple-element.19.column_ref, f32[227,8,256]{2,1,0:T(8,128)S(1)} %shard_map.92.factor_ref, f32[8,128]{1,0:T(8,128)S(1)} %bitcast.11, f32[8]{0:T(128)S(1)} %copy-done.8, f32[4,8,256]{2,1,0:T(8,128)S(1)} %copy-done.3), custom_call_target="tpu_custom_call" | custom-call | tf_op jit(solution)/shard_map/pallas_call | solution.py:507
  38.6 0.0 copy-start.1
  38.7 6.5 %all-to-all-done.1.recv_ref = f32[16,2,8,256]{3,2,1,0:T(8,128)S(1)} async-done(((f32[16,2,8,256]{3,2,1,0:T(8,128)}), f32[16,2,8,256]{3,2,1,0:T(8,128)S(1)}, u32[]{:S(2)}, u32[]{:S(2)}) %all-to-all-start.1) | async-done | bytes 262176 | tf_op jit(solution)/shard_map/all_to_all | solution.py:548
  45.2 0.0 copy-start.2
  45.2 0.0 copy-done.6
  45.2 0.8 %shard_map.95 = f32[128,128]{1,0:T(8,128)S(1)} custom-call(f32[16,2,8,256]{3,2,1,0:T(8,128)S(1)} %all-to-all-done.1.recv_ref, f32[4,8,256]{2,1,0:T(8,128)S(1)} %get-tuple-element.18.own_ref, f32[227,8,256]{2,1,0:T(8,128)S(1)} %shard_map.92.factor_ref, f32[2,8,128]{2,1,0:T(8,128)S(1)} %get-tuple-element.20.sum_ref, f32[256,512]{1,0:T(8,128)S(1)} %copy-done, ...), custom_call_target="tpu_custom_call" | custom-call | tf_op jit(solution)/shard_map/pallas_call | solution.py:507
  46.0 10.8 %all_to_all.15 = f32[8,16,128]{2,1,0:T(8,128)S(1)} all-to-all(f32[8,16,128]{2,1,0:T(8,128)S(1)} %bitcast.8), channel_id=1, replica_groups=mesh['gx'=8,'gy'=16] {'gx'}, dimensions={0} | all-to-all | bytes 131072 | tf_op jit(solution)/shard_map/all_to_all | solution.py:562
  56.7 0.0 copy-done.1
  56.7 0.0 copy-done.2
  56.7 3.8 %shard_map.96 = f32[16,64,256]{2,1,0:T(8,128)} custom-call(f32[128,128]{1,0:T(8,128)S(1)} %bitcast.9, f32[64,2,8,256]{3,2,1,0:T(8,128)S(1)} %copy-done.2, f32[64,8,256]{2,1,0:T(8,128)S(1)} %get-tuple-element.22.ratio_ref, f32[8,128]{1,0:T(8,128)S(1)} %bitcast.12, f32[256,256]{1,0:T(8,128)S(1)} %copy-done.1, f32[4,8,256]{2,1,0:T(8,128)S(1)} %copy-done.3), custom_call_target="tpu_custom_call" | custom-call | tf_op jit(solution)/shard_map/pallas_call | solution.py:507
Async XLA Ops:
  0.0 28.3 %copy-start.4 = (f32[2,8,256]{2,1,0:T(8,128)S(1)}, f32[2,8,256]{2,1,0:T(8,128)}, u32[]{:S(2)}) copy-start(f32[2,8,256]{2,1,0:T(8,128)} %constant.15.clone.table_ref) | copy-start | bytes 49156
  0.0 28.3 %copy-start = (f32[256,512]{1,0:T(8,128)S(1)}, f32[256,512]{1,0:T(8,128)}, u32[]{:S(2)}) copy-start(f32[256,512]{1,0:T(8,128)} %constant.14.clone.dft_ref) | copy-start | bytes 1572868
  0.0 28.3 %copy-start.7 = (f32[16,16]{1,0:T(8,128)S(1)}, f32[16,16]{1,0:T(8,128)}, u32[]{:S(2)}) copy-start(f32[16,16]{1,0:T(8,128)} %constant.16.clone.octet_ref) | copy-start | bytes 3076
  4.9 23.4 %all-to-all-start = ((f32[8,16,128]{2,1,0:T(8,128)}), f32[8,16,128]{2,1,0:T(8,128)S(1)}, u32[]{:S(2)}, u32[]{:S(2)}) async-start(f32[8,16,128]{2,1,0:T(8,128)} %bitcast.14), calls=%async_computation | async-start | bytes 131072 | tf_op jit(solution)/shard_map/all_to_all | solution.py:533
  28.2 9.1 %copy-start.3 = (f32[4,8,256]{2,1,0:T(8,128)S(1)}, f32[4,8,256]{2,1,0:T(8,128)}, u32[]{:S(2)}) copy-start(f32[4,8,256]{2,1,0:T(8,128)} %constant.13.clone.edge_hbm.edge_ref) | copy-start | bytes 98308
  28.3 9.1 %copy-start.5 = (f32[1024]{0:T(1024)S(1)}, f32[1024]{0:T(1024)}, u32[]{:S(2)}) copy-start(f32[1024]{0:T(1024)} %param.10) | copy-start | bytes 12292
  28.3 9.1 %copy-start.8 = (f32[8]{0:T(128)S(1)}, f32[8]{0:T(128)}, u32[]{:S(2)}) copy-start(f32[8]{0:T(128)} %wave_ref.1) | copy-start | bytes 100
  28.3 16.8 %copy-start.6 = (f32[32,16]{1,0:T(8,128)S(1)}, f32[32,16]{1,0:T(8,128)}, u32[]{:S(2)}) copy-start(f32[32,16]{1,0:T(8,128)} %constant.17.clone.octet_ref) | copy-start | bytes 6148
  29.7 15.4 %all-to-all-start.1 = ((f32[16,2,8,256]{3,2,1,0:T(8,128)}), f32[16,2,8,256]{3,2,1,0:T(8,128)S(1)}, u32[]{:S(2)}, u32[]{:S(2)}) async-start(f32[16,2,8,256]{3,2,1,0:T(8,128)} %get-tuple-element.17), calls=%async_computation.1 | async-start | bytes 524288 | tf_op jit(solution)/shard_map/all_to_all | solution.py:548
  38.6 18.1 %copy-start.1 = (f32[256,256]{1,0:T(8,128)S(1)}, f32[256,256]{1,0:T(8,128)}, u32[]{:S(2)}) copy-start(f32[256,256]{1,0:T(8,128)} %constant.12.clone.sine_hbm.sine_ref) | copy-start | bytes 786436
  45.2 11.6 %copy-start.2 = (f32[64,2,8,256]{3,2,1,0:T(8,128)S(1)}, f32[64,2,8,256]{3,2,1,0:T(8,128)}, u32[]{:S(2)}) copy-start(f32[64,2,8,256]{3,2,1,0:T(8,128)} %get-tuple-element.21.solved_ref) | copy-start | bytes 3145732

commit v3 on v2

--- a/solution.py
+++ b/solution.py
@@ -15,6 +15,7 @@
 COLS = 256
 ROWS = 64
 BANDS = 16
+PITCH = ROWS + 8
 NX = STRIPS * COLS
 VMEM_LIMIT = 16 * 1024 * 1024
 F32 = jnp.float32
@@ -36,13 +37,13 @@
 def edge_table():
     ramp = np.arange(COLS)
     left = np.sin(np.pi * ramp / COLS) * math.sqrt(2.0 / COLS)
-    right = left * np.where(ramp % 2 == 1, 1.0, -1.0)
-    left[0] = right[0] = 0.0
+    left[0] = 0.0
     along = 4.0 * np.sin(np.pi * ramp / (2 * COLS)) ** 2
-    rows = [ASPECT * left, ASPECT * right, ASPECT * along]
+    flip = np.where(ramp % 2 == 1, 1.0, -1.0)
+    rows = [ASPECT * left, ASPECT * left * flip, ASPECT * along]
     kappa = np.arange(STRIPS)[:, None]
     whole = ASPECT * (2.0 * np.sin(np.pi * (STRIPS * ramp[None, :] + kappa) / NX)) ** 2
-    return f32(np.stack([np.broadcast_to(r, (8, COLS)) for r in rows] + [whole]))
+    return f32(np.stack([np.broadcast_to(r, (8, COLS)) for r in rows] + [whole, np.broadcast_to(flip, (8, COLS))]))
 
 
 def dft_table():
@@ -91,12 +92,8 @@
     return wide(jnp.sum(values[:, :128] + values[:, 128:], axis=1, keepdims=True))
 
 
-def entry(ref, row):
-    return ref[row // 128, row % 128]
-
-
 def splat_inverse(metric_ref, row):
-    return 1.0 / jnp.full((8, COLS), entry(metric_ref, row), F32)
+    return 1.0 / jnp.full((8, COLS), metric_ref[row], F32)
 
 
 def local_shift(wave_ref, edge_ref):
@@ -108,12 +105,12 @@
 
 
 def local_kernel(
-    rhs_hbm, metric_hbm, wave_hbm, sine_hbm, edge_hbm, solved_hbm, send_ref, metrics_ref, shift_ref,
+    rhs_hbm, metric_hbm, tiled_hbm, wave_hbm, sine_hbm, edge_hbm, solved_hbm, send_ref, metrics_ref, shift_ref,
     ratio_ref, z_ref, r_lo, r_hi, sine_ref, edge_ref, metric_vec, metric_ref, wave_ref, rhs_sem, sems, out_sem,
 ):
     first = lax.axis_index("gy") * ROWS
     pairs = (
-        (metric_hbm, metric_ref), (wave_hbm, wave_ref), (edge_hbm, edge_ref), (metric_hbm, metric_vec), (sine_hbm, sine_ref)
+        (metric_hbm, metric_ref), (wave_hbm, wave_ref), (edge_hbm, edge_ref), (tiled_hbm, metric_vec), (sine_hbm, sine_ref)
     )
     small = [pltpu.make_async_copy(a, b, sems.at[i]) for i, (a, b) in enumerate(pairs)]
     half = ROWS // 2
@@ -144,10 +141,10 @@
         height = taller
     small[4].wait()
     sine = sine_ref[...]
-    flat = [ref.reshape(16 * ROWS, 128) for ref in (r_lo, r_hi)]
+    flat = [ref.reshape(16 * PITCH, 128) for ref in (r_lo, r_hi)]
 
     def line(y, c):
-        rows = pl.ds(c * ROWS + y, 8, stride=2 * ROWS)
+        rows = pl.ds(c * PITCH + y, 8, stride=2 * PITCH)
         return jnp.concatenate([ref[rows, :] for ref in flat], 1)
 
     state = [jnp.zeros((8, COLS), F32)] * 2
@@ -176,7 +173,7 @@
             upper[c] = z_ref[y, c] + ratio * upper[c]
             z_ref[y, c] = upper[c]
             a = upper[c] * left
-            source = flat[0][pl.ds(c * ROWS + y, 8, stride=2 * ROWS), :]
+            source = flat[0][pl.ds(c * PITCH + y, 8, stride=2 * PITCH), :]
             a = (a[:, :128] + a[:, 128:] + jnp.where(lanes == 0, source, 0.0)) * inverse[:, :128]
             b = upper[c] * right
             b = (b[:, :128] + b[:, 128:]) * inverse[:, :128]
@@ -220,8 +217,8 @@
     shift = shift_ref[...]
 
     def excess(row):
-        double = 2.0 * entry(metrics_ref, row)
-        return ((double + shift) - double) * entry(metrics_ref, 1024 + row)
+        double = 2.0 * metrics_ref[row]
+        return ((double + shift) - double) * metrics_ref[1024 + row]
 
     one = jnp.ones((8, COLS), F32)
     zero = jnp.zeros((8, COLS), F32)
@@ -362,14 +359,16 @@
     lax.fori_loop(0, mine, below, tuple(sides[0][c] + down * sides[1][c] for c in range(2)))
 
 
-def column_kernel(column_ref, factor_ref, metric_ref, wave_ref, edge_ref, sum_ref, local_ref, z_ref):
+def column_kernel(column_ref, factor_ref, metric_ref, wave_ref, edge_ref, sum_ref, local_ref, coupling_ref, z_ref):
     ratio_ref = factors(factor_ref)[2]
     first = lax.axis_index("gy") * ROWS
     shift = local_shift(wave_ref, edge_ref)
     height = jnp.ones((8, COLS), F32)
     slope = jnp.ones((8, COLS), F32)
     for y in range(1, ROWS):
-        slope = slope + shift * splat_inverse(metric_ref, first + y) * height
+        inverse = splat_inverse(metric_ref, first + y)
+        coupling_ref[y] = edge_ref[0] * inverse
+        slope = slope + shift * inverse * height
         taller = height + slope
         local_ref[y] = height / taller
         height = taller
@@ -440,9 +439,7 @@
             send_ref[pl.ds(10 + c * 3 + pad, 8, stride=16), :] = jnp.zeros((8, 128), F32)
 
 
-def finish_kernel(recv_ref, solved_ref, ratio_ref, metric_ref, sine_ref, edge_ref, out_hbm, z_ref, o_lo, o_hi, sems):
-    first = lax.axis_index("gy") * ROWS
-
+def finish_kernel(recv_ref, solved_ref, ratio_ref, coupling_ref, sine_ref, edge_ref, out_hbm, z_ref, o_lo, o_hi, sems):
     def take(i):
         return recv_ref[pl.ds(i, 8, stride=16), :]
 
@@ -451,22 +448,21 @@
     far = [jnp.concatenate([take(4 + c * 2), take(5 + c * 2)], 1) for c in range(2)]
     columns = [take(8 + c) for c in range(2)]
     edges = dot(jnp.concatenate(near + far, 0), sine)
-    left, right = edge_ref[0], edge_ref[1]
+    flip = edge_ref[4]
     zero_lane = lax.broadcasted_iota(jnp.int32, (8, COLS), 1) == 0
     state = [edges[c * 8 : c * 8 + 8] for c in range(2)]
     for y in range(1, ROWS):
         ratio = ratio_ref[y]
-        inverse = splat_inverse(metric_ref, first + y)
-        a, b = left * inverse, right * inverse
+        coupling = coupling_ref[y]
         for c in range(2):
             here = wide(columns[c][:, y : y + 1])
             there = wide(columns[c][:, ROWS + y : ROWS + y + 1])
             here = jnp.concatenate([here, here], 1)
             there = jnp.concatenate([there, there], 1)
-            state[c] = (state[c] + (a * here + b * there)) * ratio
+            state[c] = (state[c] + coupling * (here + flip * there)) * ratio
             z_ref[y, c] = state[c]
     upper = [edges[16 + c * 8 : 24 + c * 8] for c in range(2)]
-    flat = [ref.reshape(16 * ROWS, 128) for ref in (o_lo, o_hi)]
+    flat = [ref.reshape(16 * PITCH, 128) for ref in (o_lo, o_hi)]
     group, half = 8, ROWS // 2
     copies = []
     for base in range(ROWS - group, -1, -group):
@@ -482,7 +478,7 @@
                     lines.append(edges[c * 8 : c * 8 + 8])
         product = dot(jnp.concatenate(lines, 0), sine)
         for i in range(2 * group):
-            rows = pl.ds(i % 2 * ROWS + base + group - 1 - i // 2, 8, stride=2 * ROWS)
+            rows = pl.ds(i % 2 * PITCH + base + group - 1 - i // 2, 8, stride=2 * PITCH)
             flat[0][rows, :] = product[i * 8 : i * 8 + 8, :128]
             flat[1][rows, :] = product[i * 8 : i * 8 + 8, 128:]
         if base % half == 0:
@@ -517,17 +513,16 @@
 def per_device(rhs, metric, wavenumber):
     sine, edge = jnp.asarray(sine_table()), jnp.asarray(edge_table())
     dft, table = jnp.asarray(dft_table()), jnp.asarray(wave_table())
-    metric = metric.reshape(8, 128)
-    full, lines, side, bands = (ROWS, 8, COLS), (ROWS, 2, 8, COLS), (16, ROWS, 128), (BANDS, 8, COLS)
+    full, lines, side, bands = (ROWS, 8, COLS), (ROWS, 2, 8, COLS), (16, PITCH, 128), (BANDS, 8, COLS)
     solved, send, metrics, shift = call(
         local_kernel,
         [lines, (128, 128), (16, 128), (8, COLS)],
         [
-            full, lines, side, side, (COLS, COLS), (4, 8, COLS), (8, 128),
-            pltpu.SMEM((8, 128), F32), pltpu.SMEM((8,), F32),
+            full, lines, side, side, (COLS, COLS), (5, 8, COLS), (8, 128),
+            pltpu.SMEM((1024,), F32), pltpu.SMEM((8,), F32),
             pltpu.SemaphoreType.DMA((4,)), pltpu.SemaphoreType.DMA((5,)), pltpu.SemaphoreType.DMA((4,)),
         ],
-        rhs.reshape(16, ROWS, COLS), metric, wavenumber, sine, edge,
+        rhs.reshape(16, ROWS, COLS), metric, metric.reshape(8, 128), wavenumber, sine, edge,
         space=pltpu.HBM, far=(0, 1), manual=(0,),
     )
     recv = lax.all_to_all(send.reshape(8, 16, 128), "gx", 0, 0, tiled=True)
@@ -535,7 +530,7 @@
         factor_kernel,
         [(3 * ROWS + 2 * BANDS + 3, 8, COLS)],
         [bands, bands, bands],
-        metrics, shift,
+        metrics.reshape(2048), shift,
         scalars=(0,),
     )
     send, own, column = call(
@@ -546,9 +541,9 @@
         far=(0,),
     )
     recv = lax.all_to_all(send, "gy", 0, 0, tiled=True)
-    total, local_ratio = call(
+    total, local_ratio, coupling = call(
         column_kernel,
-        [(2, 8, 128), full],
+        [(2, 8, 128), full, full],
         [lines],
         column, factor, metric, wavenumber, edge,
         scalars=(2, 3),
@@ -564,8 +559,8 @@
         finish_kernel,
         [(16, ROWS, COLS)],
         [lines, side, side, pltpu.SemaphoreType.DMA((4,))],
-        recv.reshape(128, 128), solved, local_ratio, metric, sine, edge,
-        scalars=(3,), far=(0,), manual=(0,),
+        recv.reshape(128, 128), solved, local_ratio, coupling, sine, edge,
+        far=(0,), manual=(0,),
     )
     return out.reshape(8, 2, ROWS, COLS)
 

time: 60.9 us -> 47.5 us (0.78)
  Pallas kernels: 29.5 us -> 15.8 us
  local copies, waits for them, and re-layouts: 0.05 us -> 1.64 us
  waiting for transfers between devices: 6.5 us -> 5.03 us
    pallas_call x6, Pallas kernels: 29.5 us -> 15.8 us  [call(): pl.pallas_call(kernel, out_shape=[(pltpu.HBM if i in far else pltpu.VMEM)...]
    all_to_all x1, waiting for transfers between devices: 6.5 us -> 4.66 us  [per_device(): recv = lax.all_to_all(send, 'gy', 0, 0, tiled=True)]
    unnamed x18 -> x26, local copies, waits for them, and re-layouts: 0.05 us -> 1.64 us
  transfers between devices with their start and end apart: 2 -> 2, of which waited for: 1 -> 2; matrix products, arithmetic and copies ran while one was open for 0% -> 0% of each run, Pallas kernels for 31% -> 12%
where the time goes in v3:
time: 47.5 us; the launch traced here: 47.1 us
  Pallas kernels  15.8 us (33%)
  starting transfers between devices  13.6 us (29%)
  blocking collectives  10.9 us (23%)
  waiting for transfers between devices  5.03 us (11%)
  local copies, waits for them, and re-layouts  1.64 us (3%)
    pallas_call x6, Pallas kernels, call(): pl.pallas_call(kernel, out_shape=[(pltpu.HBM if i in far else pltpu.VMEM)...  15.8 us
    all_to_all x1, blocking collectives, per_device(): recv = lax.all_to_all(send.reshape(8, 16, 128), 'gx', 0, 0, tiled=True)  10.9 us
    all_to_all x1, starting transfers between devices, per_device(): recv = lax.all_to_all(send, 'gy', 0, 0, tiled=True)  7.65 us
    all_to_all x1, starting transfers between devices, per_device(): recv = lax.all_to_all(send.reshape(8, 16, 128), 'gx', 0, 0, tiled=True)  5.98 us
    all_to_all x1, waiting for transfers between devices, per_device(): recv = lax.all_to_all(send, 'gy', 0, 0, tiled=True)  4.66 us
    unnamed x26, local copies, waits for them, and re-layouts  1.64 us
  transfers between devices with their start and end apart: 2, of which 2 were waited for; matrix products, arithmetic and copies ran while one was open for 0% of the time, Pallas kernels for 12%

profile of v3, /device:TPU:1, one launch (start us, length us, event | category | flops | bytes accessed | tf_op | source)
XLA Modules:
  0.0 47.1 jit_solution(9429515368194761366)
XLA Ops:
  0.0 0.0 copy-start.8
  0.0 0.0 copy-start
  0.0 0.0 copy-start.11
  0.0 4.3 %shard_map.91 = (f32[64,2,8,256]{3,2,1,0:T(8,128)}, f32[128,128]{1,0:T(8,128)}, f32[16,128]{1,0:T(8,128)S(1)}, f32[8,256]{1,0:T(8,128)S(1)}) custom-call(f32[16,64,256]{2,1,0:T(8,128)} %bitcast.13, f32[1024]{0:T(1024)} %metric_ref.1, f32[8,128]{1,0:T(8,128)} %bitcast.11, f32[8]{0:T(128)} %wave_ref.1, f32[256,256]{1,0:T(8,128)} %constant.12.clone.sine_hbm.sine_ref, ...), custom_call_target="tpu_custom_call" | custom-call | tf_op jit(solution)/shard_map/pallas_call | solution.py:503
  4.4 6.0 %all-to-all-start = ((f32[8,16,128]{2,1,0:T(8,128)}), f32[8,16,128]{2,1,0:T(8,128)S(1)}, u32[]{:S(2)}, u32[]{:S(2)}) async-start(f32[8,16,128]{2,1,0:T(8,128)} %bitcast.14), calls=%async_computation | async-start | bytes 131072 | tf_op jit(solution)/shard_map/all_to_all | solution.py:528
  10.3 4.5 %shard_map.92.factor_ref = f32[227,8,256]{2,1,0:T(8,128)S(1)} custom-call(f32[2048]{0:T(1024)S(1)} %bitcast.12, f32[8,256]{1,0:T(8,128)S(1)} %get-tuple-element.17.shift_ref), custom_call_target="tpu_custom_call" | custom-call | tf_op jit(solution)/shard_map/pallas_call | solution.py:503
  14.8 0.0 copy-start.7
  14.8 0.0 copy-start.9
  14.8 0.0 copy-start.12
  14.8 0.4 all-to-all-done
  15.2 0.0 copy-done.8
  15.2 0.0 copy-done
  15.2 0.0 copy-done.11
  15.2 0.0 copy-start.10
  15.2 1.4 %shard_map.93 = (f32[16,2,8,256]{3,2,1,0:T(8,128)}, f32[4,8,256]{2,1,0:T(8,128)S(1)}, f32[2,8,128]{2,1,0:T(8,128)S(1)}) custom-call(f32[128,128]{1,0:T(8,128)S(1)} %bitcast.8, f32[227,8,256]{2,1,0:T(8,128)S(1)} %shard_map.92.factor_ref, f32[256,512]{1,0:T(8,128)S(1)} %copy-done, f32[2,8,256]{2,1,0:T(8,128)S(1)} %copy-done.8, f32[16,16]{1,0:T(8,128)S(1)} %copy-done.11), custom_call_target="tpu_custom_call" | custom-call | tf_op jit(solution)/shard_map/pallas_call | solution.py:503
  16.6 7.6 %all-to-all-start.1 = ((f32[16,2,8,256]{3,2,1,0:T(8,128)}), f32[16,2,8,256]{3,2,1,0:T(8,128)}, u32[]{:S(2)}, u32[]{:S(2)}) async-start(f32[16,2,8,256]{3,2,1,0:T(8,128)} %get-tuple-element.18), calls=%async_computation.1 | async-start | bytes 524288 | tf_op jit(solution)/shard_map/all_to_all | solution.py:543
  24.3 0.0 copy-done.7
  24.3 0.0 copy-done.9
  24.3 0.0 copy-done.12
  24.3 1.1 %shard_map.94 = (f32[2,8,128]{2,1,0:T(8,128)S(1)}, f32[64,8,256]{2,1,0:T(8,128)S(1)}, f32[64,8,256]{2,1,0:T(8,128)S(1)}) custom-call(f32[2,8,128]{2,1,0:T(8,128)S(1)} %get-tuple-element.20.column_ref, f32[227,8,256]{2,1,0:T(8,128)S(1)} %shard_map.92.factor_ref, f32[1024]{0:T(1024)S(1)} %copy-done.9, f32[8]{0:T(128)S(1)} %copy-done.12, f32[5,8,256]{2,1,0:T(8,128)S(1)} %copy-done.7), custom_call_target="tpu_custom_call" | custom-call | tf_op jit(solution)/shard_map/pallas_call | solution.py:503
  25.4 0.0 copy-start.3
  25.4 0.8 %copy-done.3 = f32[64,8,256]{2,1,0:T(8,128)} copy-done((f32[64,8,256]{2,1,0:T(8,128)}, f32[64,8,256]{2,1,0:T(8,128)S(1)}, u32[]{:S(2)}) %copy-start.3) | copy-done | bytes 524312
  26.2 0.0 copy-start.5
  26.2 0.8 %copy-done.5 = f32[64,8,256]{2,1,0:T(8,128)} copy-done((f32[64,8,256]{2,1,0:T(8,128)}, f32[64,8,256]{2,1,0:T(8,128)S(1)}, u32[]{:S(2)}) %copy-start.5) | copy-done | bytes 524312
  27.0 0.0 copy-start.1
  27.0 4.7 %all-to-all-done.1.recv_ref = f32[16,2,8,256]{3,2,1,0:T(8,128)} async-done(((f32[16,2,8,256]{3,2,1,0:T(8,128)}), f32[16,2,8,256]{3,2,1,0:T(8,128)}, u32[]{:S(2)}, u32[]{:S(2)}) %all-to-all-start.1) | async-done | bytes 262176 | tf_op jit(solution)/shard_map/all_to_all | solution.py:543
  31.7 0.0 copy-start.2
  31.7 0.0 copy-start.4
  31.7 0.0 copy-start.6
  31.7 0.0 copy-done.10
  31.7 1.8 %shard_map.95 = f32[128,128]{1,0:T(8,128)S(1)} custom-call(f32[16,2,8,256]{3,2,1,0:T(8,128)} %all-to-all-done.1.recv_ref, f32[4,8,256]{2,1,0:T(8,128)S(1)} %get-tuple-element.19.own_ref, f32[227,8,256]{2,1,0:T(8,128)S(1)} %shard_map.92.factor_ref, f32[2,8,128]{2,1,0:T(8,128)S(1)} %get-tuple-element.21.sum_ref, f32[256,512]{1,0:T(8,128)S(1)} %copy-done, ...), custom_call_target="tpu_custom_call" | custom-call | tf_op jit(solution)/shard_map/pallas_call | solution.py:503
  33.5 10.9 %all_to_all.15 = f32[8,16,128]{2,1,0:T(8,128)S(1)} all-to-all(f32[8,16,128]{2,1,0:T(8,128)S(1)} %bitcast.10), channel_id=1, replica_groups=mesh['gx'=8,'gy'=16] {'gx'}, dimensions={0} | all-to-all | bytes 131072 | tf_op jit(solution)/shard_map/all_to_all | solution.py:557
  44.4 0.0 copy-done.1
  44.4 0.0 copy-done.2
  44.4 0.0 copy-done.4
  44.4 0.0 copy-done.6
  44.4 2.7 %shard_map.96 = f32[16,64,256]{2,1,0:T(8,128)} custom-call(f32[128,128]{1,0:T(8,128)S(1)} %bitcast.9, f32[64,2,8,256]{3,2,1,0:T(8,128)S(1)} %copy-done.1, f32[64,8,256]{2,1,0:T(8,128)S(1)} %copy-done.4, f32[64,8,256]{2,1,0:T(8,128)S(1)} %copy-done.6, f32[256,256]{1,0:T(8,128)S(1)} %copy-done.2, f32[5,8,256]{2,1,0:T(8,128)S(1)} %copy-done.7), custom_call_target="tpu_custom_call" | custom-call | tf_op jit(solution)/shard_map/pallas_call | solution.py:503
Async XLA Ops:
  0.0 15.2 %copy-start.8 = (f32[2,8,256]{2,1,0:T(8,128)S(1)}, f32[2,8,256]{2,1,0:T(8,128)}, u32[]{:S(2)}) copy-start(f32[2,8,256]{2,1,0:T(8,128)} %constant.15.clone.table_ref) | copy-start | bytes 49156
  0.0 15.2 %copy-start = (f32[256,512]{1,0:T(8,128)S(1)}, f32[256,512]{1,0:T(8,128)}, u32[]{:S(2)}) copy-start(f32[256,512]{1,0:T(8,128)} %constant.14.clone.dft_ref) | copy-start | bytes 1572868
  0.0 15.2 %copy-start.11 = (f32[16,16]{1,0:T(8,128)S(1)}, f32[16,16]{1,0:T(8,128)}, u32[]{:S(2)}) copy-start(f32[16,16]{1,0:T(8,128)} %constant.16.clone.octet_ref) | copy-start | bytes 3076
  4.4 10.8 %all-to-all-start = ((f32[8,16,128]{2,1,0:T(8,128)}), f32[8,16,128]{2,1,0:T(8,128)S(1)}, u32[]{:S(2)}, u32[]{:S(2)}) async-start(f32[8,16,128]{2,1,0:T(8,128)} %bitcast.14), calls=%async_computation | async-start | bytes 131072 | tf_op jit(solution)/shard_map/all_to_all | solution.py:528
  14.8 9.5 %copy-start.7 = (f32[5,8,256]{2,1,0:T(8,128)S(1)}, f32[5,8,256]{2,1,0:T(8,128)}, u32[]{:S(2)}) copy-start(f32[5,8,256]{2,1,0:T(8,128)} %constant.13.clone.edge_hbm.edge_ref) | copy-start | bytes 122884
  14.8 9.5 %copy-start.9 = (f32[1024]{0:T(1024)S(1)}, f32[1024]{0:T(1024)}, u32[]{:S(2)}) copy-start(f32[1024]{0:T(1024)} %metric_ref.1) | copy-start | bytes 12292
  14.8 9.5 %copy-start.12 = (f32[8]{0:T(128)S(1)}, f32[8]{0:T(128)}, u32[]{:S(2)}) copy-start(f32[8]{0:T(128)} %wave_ref.1) | copy-start | bytes 100
  15.2 16.5 %copy-start.10 = (f32[32,16]{1,0:T(8,128)S(1)}, f32[32,16]{1,0:T(8,128)}, u32[]{:S(2)}) copy-start(f32[32,16]{1,0:T(8,128)} %constant.17.clone.octet_ref) | copy-start | bytes 6148
  16.6 15.1 %all-to-all-start.1 = ((f32[16,2,8,256]{3,2,1,0:T(8,128)}), f32[16,2,8,256]{3,2,1,0:T(8,128)}, u32[]{:S(2)}, u32[]{:S(2)}) async-start(f32[16,2,8,256]{3,2,1,0:T(8,128)} %get-tuple-element.18), calls=%async_computation.1 | async-start | bytes 524288 | tf_op jit(solution)/shard_map/all_to_all | solution.py:543
  25.4 0.8 %copy-start.3 = (f32[64,8,256]{2,1,0:T(8,128)}, f32[64,8,256]{2,1,0:T(8,128)S(1)}, u32[]{:S(2)}) copy-start(f32[64,8,256]{2,1,0:T(8,128)S(1)} %get-tuple-element.23.ratio_ref) | copy-start | bytes 1572868
  26.2 0.8 %copy-start.5 = (f32[64,8,256]{2,1,0:T(8,128)}, f32[64,8,256]{2,1,0:T(8,128)S(1)}, u32[]{:S(2)}) copy-start(f32[64,8,256]{2,1,0:T(8,128)S(1)} %get-tuple-element.24.coupling_ref) | copy-start | bytes 1572868
  27.0 17.4 %copy-start.1 = (f32[64,2,8,256]{3,2,1,0:T(8,128)S(1)}, f32[64,2,8,256]{3,2,1,0:T(8,128)}, u32[]{:S(2)}) copy-start(f32[64,2,8,256]{3,2,1,0:T(8,128)} %get-tuple-element.22.solved_ref) | copy-start | bytes 3145732
  31.7 12.7 %copy-start.2 = (f32[256,256]{1,0:T(8,128)S(1)}, f32[256,256]{1,0:T(8,128)}, u32[]{:S(2)}) copy-start(f32[256,256]{1,0:T(8,128)} %constant.12.clone.sine_hbm.sine_ref) | copy-start | bytes 786436
  31.7 12.7 %copy-start.4 = (f32[64,8,256]{2,1,0:T(8,128)S(1)}, f32[64,8,256]{2,1,0:T(8,128)}, u32[]{:S(2)}) copy-start(f32[64,8,256]{2,1,0:T(8,128)} %copy-done.3) | copy-start | bytes 1572868
  31.7 12.7 %copy-start.6 = (f32[64,8,256]{2,1,0:T(8,128)S(1)}, f32[64,8,256]{2,1,0:T(8,128)}, u32[]{:S(2)}) copy-start(f32[64,8,256]{2,1,0:T(8,128)} %copy-done.5) | copy-start | bytes 1572868

commit v4 on v3

--- a/solution.py
+++ b/solution.py
@@ -204,15 +204,13 @@
 
 
 def factors(ref):
-    sizes = (ROWS, ROWS, ROWS, BANDS, BANDS, 3)
+    sizes = (ROWS, ROWS, BANDS, BANDS, 4)
     starts = np.cumsum((0,) + sizes)
     return [ref.at[pl.ds(int(a), n)] for a, n in zip(starts, sizes)]
 
 
-def factor_kernel(
-    metrics_ref, shift_ref, factor_ref, gamma_ref, base_ref, x_ref
-):
-    alpha_ref, beta_ref, ratio_ref, up_ref, down_ref, final_ref = factors(factor_ref)
+def factor_kernel(metrics_ref, shift_ref, factor_ref, gamma_ref, base_ref, edge_ref, x_ref, above_ref, inverse_ref):
+    over_ref, under_ref, up_ref, down_ref, final_ref = factors(factor_ref)
     mine = lax.axis_index("gy")
     shift = shift_ref[...]
 
@@ -224,8 +222,7 @@
     zero = jnp.zeros((8, COLS), F32)
     together = 4
 
-    def bands(outer, carry):
-        excess_below, flow = carry
+    def bands(outer, _):
         state = [(one, one, zero, zero)] * together
 
         def rows(y, state):
@@ -245,57 +242,55 @@
             height, slope, rest, _ = state[i]
             band = outer * together + i
             gamma = 1.0 / height
-            base = excess(band * ROWS) + rest * gamma + excess_below
-            x = base + flow
+            gamma_ref[band] = gamma
+            base_ref[band] = excess(band * ROWS) + rest * gamma
+            edge_ref[band] = (slope - 1.0) * gamma
+        return 0
+
+    lax.fori_loop(0, BANDS // together, bands, 0)
+
+    flow = one
+    above, down, inverse = one, zero, zero
+    height, slope = one, one
+    rest, rise = one, one
+    for y in range(1, ROWS + 1):
+        if y < ROWS:
+            under_ref[y] = height
+            slope = slope + excess(mine * ROWS + y) * height
+            height = height + slope
+            over_ref[ROWS - y] = rest
+            rise = rise + excess(mine * ROWS + ROWS - y) * rest
+            rest = rest + rise
+        if y % 4 == 0:
+            band = y // 4 - 1
+            x = base_ref[band] + flow
+            if band:
+                x = x + edge_ref[band - 1]
+            x_ref[band] = x
+            gamma = gamma_ref[band]
             up = gamma / (gamma + x)
-            gamma_ref[band] = gamma
-            base_ref[band] = base
-            x_ref[band] = x
             up_ref[band] = up
-            excess_below = (slope - 1.0) * gamma
             flow = up * x
-        return excess_below, flow
-
-    lax.fori_loop(0, BANDS // together, bands, (zero, one))
-
-    above, down, inverse = one, zero, zero
-    for band in range(BANDS - 1, -1, -1):
-        gamma = gamma_ref[band]
-        down_ref[band] = down
-
-        @pl.when(band == mine)
-        def _(above=above, down=down, inverse=inverse, gamma=gamma):
-            final_ref[0] = down
-            final_ref[1] = inverse
-            final_ref[2] = 1.0 / (x_ref[mine] + gamma * above)
-
-        if band:
-            x = base_ref[band] + gamma * above
-            below = gamma_ref[band - 1]
-            inverse = 1.0 / (below + x)
-            down = below * inverse
-            above = x * inverse
-
-    height, slope = one, one
-    for y in range(1, ROWS):
-        beta_ref[y] = height
-        slope = slope + excess(mine * ROWS + y) * height
-        taller = height + slope
-        ratio_ref[y] = height / taller
-        height = taller
-    gamma = 1.0 / height
-    height, slope = one, one
-    for y in range(ROWS - 1, 0, -1):
-        alpha_ref[y] = height * gamma
-        beta_ref[y] = beta_ref[y] * gamma
-        slope = slope + excess(mine * ROWS + y) * height
-        height = height + slope
+            band = BANDS - 1 - band
+            above_ref[band], down_ref[band], inverse_ref[band] = above, down, inverse
+            if band:
+                x = base_ref[band] + edge_ref[band - 1] + gamma_ref[band] * above
+                below = gamma_ref[band - 1]
+                inverse = 1.0 / (below + x)
+                down = below * inverse
+                above = x * inverse
+    gamma = gamma_ref[mine]
+    final_ref[0] = down_ref[mine]
+    final_ref[1] = inverse_ref[mine]
+    final_ref[2] = 1.0 / (x_ref[mine] + gamma * above_ref[mine])
+    final_ref[3] = gamma
+    under_ref[0] = height
 
 
 def spectrum_kernel(
     recv_ref, factor_ref, dft_ref, table_ref, octet_ref, send_ref, own_ref, column_ref
 ):
-    alpha_ref, beta_ref, _, up_ref, down_ref, _ = factors(factor_ref)
+    over_ref, under_ref, up_ref, down_ref, final_ref = factors(factor_ref)
     mine = lax.axis_index("gy")
 
     def take(i):
@@ -323,19 +318,20 @@
     near = [jnp.zeros((8, COLS), F32)] * 2
     far = [jnp.zeros((8, COLS), F32)] * 2
     for y in range(1, ROWS):
-        alpha, beta = alpha_ref[y], beta_ref[y]
+        over, under = over_ref[y], under_ref[y]
         for c in range(2):
             source = wide(columns[c][:, y : y + 1])
             source = jnp.concatenate([source, source], 1)
-            near[c] = near[c] + alpha * source
-            far[c] = far[c] + beta * source
+            near[c] = near[c] + over * source
+            far[c] = far[c] + under * source
+    gamma = final_ref[3]
     sides = []
     for line, extra in enumerate((near, far)):
         re_cos = both[line * 8 : line * 8 + 8, :COLS]
         re_sin = both[line * 8 : line * 8 + 8, COLS:]
         im_cos = both[16 + line * 8 : 24 + line * 8, :COLS]
         im_sin = both[16 + line * 8 : 24 + line * 8, COLS:]
-        sides.append((re_cos + im_sin + extra[0], im_cos - re_sin + extra[1]))
+        sides.append((re_cos + im_sin + extra[0] * gamma, im_cos - re_sin + extra[1] * gamma))
     for c in range(2):
         own_ref[c], own_ref[2 + c] = sides[0][c], sides[1][c]
         column_ref[c] = columns[c]
@@ -359,24 +355,25 @@
     lax.fori_loop(0, mine, below, tuple(sides[0][c] + down * sides[1][c] for c in range(2)))
 
 
-def column_kernel(column_ref, factor_ref, metric_ref, wave_ref, edge_ref, sum_ref, local_ref, coupling_ref, z_ref):
-    ratio_ref = factors(factor_ref)[2]
+def column_kernel(column_ref, factor_ref, metric_ref, wave_ref, edge_ref, out_ref, z_ref, ratio_ref):
+    under_ref = factors(factor_ref)[1]
     first = lax.axis_index("gy") * ROWS
     shift = local_shift(wave_ref, edge_ref)
     height = jnp.ones((8, COLS), F32)
     slope = jnp.ones((8, COLS), F32)
     for y in range(1, ROWS):
         inverse = splat_inverse(metric_ref, first + y)
-        coupling_ref[y] = edge_ref[0] * inverse
+        out_ref[ROWS + y] = edge_ref[0] * inverse
         slope = slope + shift * inverse * height
         taller = height + slope
-        local_ref[y] = height / taller
+        out_ref[y] = height / taller
         height = taller
     lanes = lane_ids()
     columns = [column_ref[c] for c in range(2)]
     state = [jnp.zeros((8, COLS), F32)] * 2
     for y in range(1, ROWS):
-        ratio = ratio_ref[y]
+        ratio = under_ref[y] / under_ref[(y + 1) % ROWS]
+        ratio_ref[y] = ratio
         for c in range(2):
             source = wide(columns[c][:, y : y + 1])
             state[c] = (jnp.concatenate([source, source], 1) + state[c]) * ratio
@@ -388,14 +385,13 @@
         for c in range(2):
             upper[c] = z_ref[y, c] + ratio * upper[c]
             total[c] = jnp.where(lanes == y, row_sum(upper[c]), total[c])
-    for c in range(2):
-        sum_ref[c] = total[c]
+    out_ref[0] = jnp.concatenate(total, 1)
 
 
 def separator_kernel(
-    recv_ref, own_ref, factor_ref, sum_ref, dft_ref, table_ref, octet_ref, send_ref
+    recv_ref, own_ref, factor_ref, local_ref, dft_ref, table_ref, octet_ref, send_ref
 ):
-    alpha_ref, beta_ref, _, _, _, final_ref = factors(factor_ref)
+    over_ref, under_ref, _, _, final_ref = factors(factor_ref)
     mine = lax.axis_index("gy")
     from_below = [own_ref[c] for c in range(2)]
     from_above = [own_ref[2 + c] for c in range(2)]
@@ -409,11 +405,14 @@
     far = [from_above[c] * inverse + down * near[c] for c in range(2)]
     lanes = lane_ids()
     both = dot(jnp.concatenate([near[0], far[0], near[1], far[1]], 0), dft_ref[...])
-    total = [sum_ref[c] for c in range(2)]
+    total = [local_ref[0, :, c * 128 : c * 128 + 128] for c in range(2)]
+    gamma = final_ref[3]
+    near = [value * gamma for value in near]
+    far = [value * gamma for value in far]
     for y in range(1, ROWS):
-        alpha, beta = alpha_ref[y], beta_ref[y]
-        for c in range(2):
-            extra = row_sum(alpha * near[c] + beta * far[c])
+        over, under = over_ref[y], under_ref[y]
+        for c in range(2):
+            extra = row_sum(over * near[c] + under * far[c])
             total[c] = total[c] + jnp.where(lanes == y, extra, 0.0)
     cos, sin = table_ref[0], table_ref[1]
     turned = [[], []]
@@ -439,7 +438,7 @@
             send_ref[pl.ds(10 + c * 3 + pad, 8, stride=16), :] = jnp.zeros((8, 128), F32)
 
 
-def finish_kernel(recv_ref, solved_ref, ratio_ref, coupling_ref, sine_ref, edge_ref, out_hbm, z_ref, o_lo, o_hi, sems):
+def finish_kernel(recv_ref, solved_ref, local_ref, sine_ref, edge_ref, out_hbm, z_ref, o_lo, o_hi, sems):
     def take(i):
         return recv_ref[pl.ds(i, 8, stride=16), :]
 
@@ -452,8 +451,8 @@
     zero_lane = lax.broadcasted_iota(jnp.int32, (8, COLS), 1) == 0
     state = [edges[c * 8 : c * 8 + 8] for c in range(2)]
     for y in range(1, ROWS):
-        ratio = ratio_ref[y]
-        coupling = coupling_ref[y]
+        ratio = local_ref[y]
+        coupling = local_ref[ROWS + y]
         for c in range(2):
             here = wide(columns[c][:, y : y + 1])
             there = wide(columns[c][:, ROWS + y : ROWS + y + 1])
@@ -470,7 +469,7 @@
         for y in range(base + group - 1, base - 1, -1):
             for c in range(2):
                 if y:
-                    upper[c] = z_ref[y, c] + ratio_ref[y] * upper[c]
+                    upper[c] = z_ref[y, c] + local_ref[y] * upper[c]
                     here = wide(columns[c][:, y : y + 1])
                     here = jnp.concatenate([here, here], 1)
                     lines.append(jnp.where(zero_lane, here, upper[c] + solved_ref[y, c]))
@@ -496,14 +495,13 @@
 
 
 def call(kernel, outs, scratch, *operands, scalars=(), far=(), manual=(), space=pltpu.VMEM):
-    smem = pl.BlockSpec(memory_space=pltpu.SMEM)
-    specs = [smem if i in scalars else pl.BlockSpec(memory_space=space) for i in range(len(operands))]
+    places = [pltpu.SMEM if i in scalars else space for i in range(len(operands))]
     if space == pltpu.HBM:
         operands = [pltpu.with_memory_space_constraint(a, space) for a in operands]
     return pl.pallas_call(
         kernel,
         out_shape=[(pltpu.HBM if i in far else pltpu.VMEM)(s, F32) for i, s in enumerate(outs)],
-        in_specs=specs,
+        in_specs=[pl.BlockSpec(memory_space=place) for place in places],
         out_specs=[pl.BlockSpec(memory_space=pltpu.HBM if i in manual else pltpu.VMEM) for i in range(len(outs))],
         scratch_shapes=[pltpu.VMEM(s, F32) if isinstance(s, tuple) else s for s in scratch],
         compiler_params=pltpu.CompilerParams(vmem_limit_bytes=VMEM_LIMIT),
@@ -528,8 +526,8 @@
     recv = lax.all_to_all(send.reshape(8, 16, 128), "gx", 0, 0, tiled=True)
     (factor,) = call(
         factor_kernel,
-        [(3 * ROWS + 2 * BANDS + 3, 8, COLS)],
-        [bands, bands, bands],
+        [(2 * ROWS + 2 * BANDS + 4, 8, COLS)],
+        [bands] * 6,
         metrics.reshape(2048), shift,
         scalars=(0,),
     )
@@ -541,10 +539,10 @@
         far=(0,),
     )
     recv = lax.all_to_all(send, "gy", 0, 0, tiled=True)
-    total, local_ratio, coupling = call(
+    (local,) = call(
         column_kernel,
-        [(2, 8, 128), full, full],
-        [lines],
+        [(2 * ROWS, 8, COLS)],
+        [lines, full],
         column, factor, metric, wavenumber, edge,
         scalars=(2, 3),
     )
@@ -552,14 +550,14 @@
         separator_kernel,
         [(128, 128)],
         [],
-        recv, own, factor, total, dft, table, jnp.asarray(octet_inverse()),
+        recv, own, factor, local, dft, table, jnp.asarray(octet_inverse()),
     )
     recv = lax.all_to_all(send.reshape(8, 16, 128), "gx", 0, 0, tiled=True)
     (out,) = call(
         finish_kernel,
         [(16, ROWS, COLS)],
         [lines, side, side, pltpu.SemaphoreType.DMA((4,))],
-        recv.reshape(128, 128), solved, local_ratio, coupling, sine, edge,
+        recv.reshape(128, 128), solved, local, sine, edge,
         far=(0,), manual=(0,),
     )
     return out.reshape(8, 2, ROWS, COLS)

time: 47.5 us -> 45.9 us (0.966)
  waiting for transfers between devices: 5.03 us -> 6.9 us
  local copies, waits for them, and re-layouts: 1.64 us -> 0.04 us
  Pallas kernels: 15.8 us -> 14.4 us
    unnamed x26 -> x18, local copies, waits for them, and re-layouts: 1.64 us -> 0.04 us
    all_to_all x1, waiting for transfers between devices: 4.66 us -> 6.2 us  [per_device(): recv = lax.all_to_all(send, 'gy', 0, 0, tiled=True)]
    pallas_call x6, Pallas kernels: 15.8 us -> 14.4 us  [call(): pl.pallas_call(kernel, out_shape=[(pltpu.HBM if i in far else pltpu.VMEM)...]
  transfers between devices with their start and end apart: 2 -> 2, of which waited for: 2 -> 2; matrix products, arithmetic and copies ran while one was open for 0% -> 0% of each run, Pallas kernels for 12% -> 11%
where the time goes in v4:
time: 45.9 us; the launch traced here: 45.6 us
  Pallas kernels  14.4 us (31%)
  starting transfers between devices  13.6 us (30%)
  blocking collectives  10.5 us (23%)
  waiting for transfers between devices  6.9 us (15%)
    pallas_call x6, Pallas kernels, call(): pl.pallas_call(kernel, out_shape=[(pltpu.HBM if i in far else pltpu.VMEM)...  14.4 us
    all_to_all x1, blocking collectives, per_device(): recv = lax.all_to_all(send.reshape(8, 16, 128), 'gx', 0, 0, tiled=True)  10.5 us
    all_to_all x1, starting transfers between devices, per_device(): recv = lax.all_to_all(send, 'gy', 0, 0, tiled=True)  7.6 us
    all_to_all x1, waiting for transfers between devices, per_device(): recv = lax.all_to_all(send, 'gy', 0, 0, tiled=True)  6.2 us
    all_to_all x1, starting transfers between devices, per_device(): recv = lax.all_to_all(send.reshape(8, 16, 128), 'gx', 0, 0, tiled=True)  5.98 us
  transfers between devices with their start and end apart: 2, of which 2 were waited for; matrix products, arithmetic and copies ran while one was open for 0% of the time, Pallas kernels for 11%

profile of v4, /device:TPU:1, one launch (start us, length us, event | category | flops | bytes accessed | tf_op | source)
XLA Modules:
  0.0 45.6 jit_solution(304322161066822189)
XLA Ops:
  0.0 0.0 copy-start
  0.0 0.0 copy-start.4
  0.0 0.0 copy-start.7
  0.0 4.3 %shard_map.91 = (f32[64,2,8,256]{3,2,1,0:T(8,128)}, f32[128,128]{1,0:T(8,128)}, f32[16,128]{1,0:T(8,128)S(1)}, f32[8,256]{1,0:T(8,128)S(1)}) custom-call(f32[16,64,256]{2,1,0:T(8,128)} %bitcast.13, f32[1024]{0:T(1024)} %metric_ref.1, f32[8,128]{1,0:T(8,128)} %bitcast.11, f32[8]{0:T(128)} %wave_ref.1, f32[256,256]{1,0:T(8,128)} %constant.12.clone.sine_hbm.sine_ref, ...), custom_call_target="tpu_custom_call" | custom-call | tf_op jit(solution)/shard_map/pallas_call | solution.py:501
  4.4 6.0 %all-to-all-start = ((f32[8,16,128]{2,1,0:T(8,128)}), f32[8,16,128]{2,1,0:T(8,128)S(1)}, u32[]{:S(2)}, u32[]{:S(2)}) async-start(f32[8,16,128]{2,1,0:T(8,128)} %bitcast.14), calls=%async_computation | async-start | bytes 131072 | tf_op jit(solution)/shard_map/all_to_all | solution.py:526
  10.3 4.1 %shard_map.92.factor_ref = f32[164,8,256]{2,1,0:T(8,128)S(1)} custom-call(f32[2048]{0:T(1024)S(1)} %bitcast.12, f32[8,256]{1,0:T(8,128)S(1)} %get-tuple-element.14.shift_ref), custom_call_target="tpu_custom_call" | custom-call | tf_op jit(solution)/shard_map/pallas_call | solution.py:501
  14.4 0.0 copy-start.3
  14.5 0.0 copy-start.5
  14.5 0.0 copy-start.8
  14.5 0.7 %all-to-all-done = f32[8,16,128]{2,1,0:T(8,128)S(1)} async-done(((f32[8,16,128]{2,1,0:T(8,128)}), f32[8,16,128]{2,1,0:T(8,128)S(1)}, u32[]{:S(2)}, u32[]{:S(2)}) %all-to-all-start) | async-done | bytes 65568 | tf_op jit(solution)/shard_map/all_to_all | solution.py:526
  15.2 0.0 copy-done
  15.2 0.0 copy-done.4
  15.2 0.0 copy-done.7
  15.2 1.4 %shard_map.93 = (f32[16,2,8,256]{3,2,1,0:T(8,128)}, f32[4,8,256]{2,1,0:T(8,128)S(1)}, f32[2,8,128]{2,1,0:T(8,128)S(1)}) custom-call(f32[128,128]{1,0:T(8,128)S(1)} %bitcast.8, f32[164,8,256]{2,1,0:T(8,128)S(1)} %shard_map.92.factor_ref, f32[256,512]{1,0:T(8,128)S(1)} %copy-done, f32[2,8,256]{2,1,0:T(8,128)S(1)} %copy-done.4, f32[16,16]{1,0:T(8,128)S(1)} %copy-done.7), custom_call_target="tpu_custom_call" | custom-call | tf_op jit(solution)/shard_map/pallas_call | solution.py:501
  16.6 7.6 %all-to-all-start.1 = ((f32[16,2,8,256]{3,2,1,0:T(8,128)}), f32[16,2,8,256]{3,2,1,0:T(8,128)S(1)}, u32[]{:S(2)}, u32[]{:S(2)}) async-start(f32[16,2,8,256]{3,2,1,0:T(8,128)} %get-tuple-element.15), calls=%async_computation.1 | async-start | bytes 524288 | tf_op jit(solution)/shard_map/all_to_all | solution.py:541
  24.2 0.0 copy-start.6
  24.2 0.0 copy-done.3
  24.2 0.0 copy-done.5
  24.2 0.0 copy-done.8
  24.2 1.1 %shard_map.94.local_ref = f32[128,8,256]{2,1,0:T(8,128)S(1)} custom-call(f32[2,8,128]{2,1,0:T(8,128)S(1)} %get-tuple-element.17.column_ref, f32[164,8,256]{2,1,0:T(8,128)S(1)} %shard_map.92.factor_ref, f32[1024]{0:T(1024)S(1)} %copy-done.5, f32[8]{0:T(128)S(1)} %copy-done.8, f32[5,8,256]{2,1,0:T(8,128)S(1)} %copy-done.3), custom_call_target="tpu_custom_call" | custom-call | tf_op jit(solution)/shard_map/pallas_call | solution.py:501
  25.4 6.2 %all-to-all-done.1.recv_ref = f32[16,2,8,256]{3,2,1,0:T(8,128)S(1)} async-done(((f32[16,2,8,256]{3,2,1,0:T(8,128)}), f32[16,2,8,256]{3,2,1,0:T(8,128)S(1)}, u32[]{:S(2)}, u32[]{:S(2)}) %all-to-all-start.1) | async-done | bytes 262176 | tf_op jit(solution)/shard_map/all_to_all | solution.py:541
  31.6 0.0 copy-done.6
  31.6 0.0 copy-start.1
  31.6 0.0 copy-start.2
  31.6 0.8 %shard_map.95 = f32[128,128]{1,0:T(8,128)S(1)} custom-call(f32[16,2,8,256]{3,2,1,0:T(8,128)S(1)} %all-to-all-done.1.recv_ref, f32[4,8,256]{2,1,0:T(8,128)S(1)} %get-tuple-element.16.own_ref, f32[164,8,256]{2,1,0:T(8,128)S(1)} %shard_map.92.factor_ref, f32[128,8,256]{2,1,0:T(8,128)S(1)} %shard_map.94.local_ref, f32[256,512]{1,0:T(8,128)S(1)} %copy-done, ...), custom_call_target="tpu_custom_call" | custom-call | tf_op jit(solution)/shard_map/pallas_call | solution.py:501
  32.4 10.5 %all_to_all.15 = f32[8,16,128]{2,1,0:T(8,128)S(1)} all-to-all(f32[8,16,128]{2,1,0:T(8,128)S(1)} %bitcast.9), channel_id=1, replica_groups=mesh['gx'=8,'gy'=16] {'gx'}, dimensions={0} | all-to-all | bytes 131072 | tf_op jit(solution)/shard_map/all_to_all | solution.py:555
  42.9 0.0 copy-done.1
  42.9 0.0 copy-done.2
  42.9 2.6 %shard_map.96 = f32[16,64,256]{2,1,0:T(8,128)} custom-call(f32[128,128]{1,0:T(8,128)S(1)} %bitcast.10, f32[64,2,8,256]{3,2,1,0:T(8,128)S(1)} %copy-done.1, f32[128,8,256]{2,1,0:T(8,128)S(1)} %shard_map.94.local_ref, f32[256,256]{1,0:T(8,128)S(1)} %copy-done.2, f32[5,8,256]{2,1,0:T(8,128)S(1)} %copy-done.3), custom_call_target="tpu_custom_call" | custom-call | tf_op jit(solution)/shard_map/pallas_call | solution.py:501
Async XLA Ops:
  0.0 15.2 %copy-start = (f32[256,512]{1,0:T(8,128)S(1)}, f32[256,512]{1,0:T(8,128)}, u32[]{:S(2)}) copy-start(f32[256,512]{1,0:T(8,128)} %constant.14.clone.dft_ref) | copy-start | bytes 1572868
  0.0 15.2 %copy-start.4 = (f32[2,8,256]{2,1,0:T(8,128)S(1)}, f32[2,8,256]{2,1,0:T(8,128)}, u32[]{:S(2)}) copy-start(f32[2,8,256]{2,1,0:T(8,128)} %constant.15.clone.table_ref) | copy-start | bytes 49156
  0.0 15.2 %copy-start.7 = (f32[16,16]{1,0:T(8,128)S(1)}, f32[16,16]{1,0:T(8,128)}, u32[]{:S(2)}) copy-start(f32[16,16]{1,0:T(8,128)} %constant.16.clone.octet_ref) | copy-start | bytes 3076
  4.4 10.8 %all-to-all-start = ((f32[8,16,128]{2,1,0:T(8,128)}), f32[8,16,128]{2,1,0:T(8,128)S(1)}, u32[]{:S(2)}, u32[]{:S(2)}) async-start(f32[8,16,128]{2,1,0:T(8,128)} %bitcast.14), calls=%async_computation | async-start | bytes 131072 | tf_op jit(solution)/shard_map/all_to_all | solution.py:526
  14.4 9.8 %copy-start.3 = (f32[5,8,256]{2,1,0:T(8,128)S(1)}, f32[5,8,256]{2,1,0:T(8,128)}, u32[]{:S(2)}) copy-start(f32[5,8,256]{2,1,0:T(8,128)} %constant.13.clone.edge_hbm.edge_ref) | copy-start | bytes 122884
  14.5 9.8 %copy-start.5 = (f32[1024]{0:T(1024)S(1)}, f32[1024]{0:T(1024)}, u32[]{:S(2)}) copy-start(f32[1024]{0:T(1024)} %metric_ref.1) | copy-start | bytes 12292
  14.5 9.8 %copy-start.8 = (f32[8]{0:T(128)S(1)}, f32[8]{0:T(128)}, u32[]{:S(2)}) copy-start(f32[8]{0:T(128)} %wave_ref.1) | copy-start | bytes 100
  16.6 15.0 %all-to-all-start.1 = ((f32[16,2,8,256]{3,2,1,0:T(8,128)}), f32[16,2,8,256]{3,2,1,0:T(8,128)S(1)}, u32[]{:S(2)}, u32[]{:S(2)}) async-start(f32[16,2,8,256]{3,2,1,0:T(8,128)} %get-tuple-element.15), calls=%async_computation.1 | async-start | bytes 524288 | tf_op jit(solution)/shard_map/all_to_all | solution.py:541
  24.2 7.4 %copy-start.6 = (f32[32,16]{1,0:T(8,128)S(1)}, f32[32,16]{1,0:T(8,128)}, u32[]{:S(2)}) copy-start(f32[32,16]{1,0:T(8,128)} %constant.17.clone.octet_ref) | copy-start | bytes 6148
  31.6 11.3 %copy-start.1 = (f32[64,2,8,256]{3,2,1,0:T(8,128)S(1)}, f32[64,2,8,256]{3,2,1,0:T(8,128)}, u32[]{:S(2)}) copy-start(f32[64,2,8,256]{3,2,1,0:T(8,128)} %get-tuple-element.18.solved_ref) | copy-start | bytes 3145732
  31.6 11.3 %copy-start.2 = (f32[256,256]{1,0:T(8,128)S(1)}, f32[256,256]{1,0:T(8,128)}, u32[]{:S(2)}) copy-start(f32[256,256]{1,0:T(8,128)} %constant.12.clone.sine_hbm.sine_ref) | copy-start | bytes 786436

commit v5 on v4

--- a/solution.py
+++ b/solution.py
@@ -105,8 +105,8 @@
 
 
 def local_kernel(
-    rhs_hbm, metric_hbm, tiled_hbm, wave_hbm, sine_hbm, edge_hbm, solved_hbm, send_ref, metrics_ref, shift_ref,
-    ratio_ref, z_ref, r_lo, r_hi, sine_ref, edge_ref, metric_vec, metric_ref, wave_ref, rhs_sem, sems, out_sem,
+    rhs_hbm, metric_hbm, tiled_hbm, wave_hbm, sine_hbm, edge_hbm, solved_hbm, send_hbm, metrics_hbm, shift_hbm,
+    metrics_ref, shift_ref, send_ref, ratio_ref, z_ref, r_lo, r_hi, sine_ref, edge_ref, metric_vec, metric_ref, wave_ref, rhs_sem, sems, out_sem,
 ):
     first = lax.axis_index("gy") * ROWS
     pairs = (
@@ -129,9 +129,16 @@
         copy.wait()
     metrics_ref[:8, :] = metric_vec[...]
     metrics_ref[8:, :] = 1.0 / metric_vec[...]
-    shift_ref[...] = edge_ref[3] + wave_ref[lax.axis_index("gx")]
+    shift = local_shift(wave_ref, edge_ref)
+    shift_ref[0] = edge_ref[3] + wave_ref[lax.axis_index("gx")]
+    shift_ref[1] = shift
+    shift_ref[2] = edge_ref[0]
+    done = [
+        pltpu.make_async_copy(metrics_ref, metrics_hbm, sems.at[1]), pltpu.make_async_copy(shift_ref, shift_hbm, sems.at[2])
+    ]
+    for copy in done:
+        copy.start()
     lanes = lane_ids()
-    shift = local_shift(wave_ref, edge_ref)
     height = jnp.ones((8, COLS), F32)
     slope = jnp.ones((8, COLS), F32)
     for y in range(1, ROWS):
@@ -165,7 +172,6 @@
     right = edge_ref[1]
     columns = [[jnp.zeros((8, 128), F32)] * 2 for _ in range(2)]
     upper = [jnp.zeros((8, COLS), F32)] * 2
-    done = []
     for y in range(ROWS - 1, 0, -1):
         ratio = ratio_ref[y]
         inverse = splat_inverse(metric_ref, first + y)
@@ -199,20 +205,32 @@
         send_ref[pl.ds(8 + c, 8, stride=16), :] = jnp.where(lanes < ROWS, columns[0][c], columns[1][c])
         for pad in range(3):
             send_ref[pl.ds(10 + c * 3 + pad, 8, stride=16), :] = jnp.zeros((8, 128), F32)
+    done.append(pltpu.make_async_copy(send_ref, send_hbm, sems.at[0]))
+    done[-1].start()
     for copy in done:
         copy.wait()
 
 
 def factors(ref):
-    sizes = (ROWS, ROWS, BANDS, BANDS, 4)
+    sizes = (ROWS, ROWS, ROWS, BANDS, BANDS, 4, ROWS, ROWS)
     starts = np.cumsum((0,) + sizes)
     return [ref.at[pl.ds(int(a), n)] for a, n in zip(starts, sizes)]
 
 
-def factor_kernel(metrics_ref, shift_ref, factor_ref, gamma_ref, base_ref, edge_ref, x_ref, above_ref, inverse_ref):
-    over_ref, under_ref, up_ref, down_ref, final_ref = factors(factor_ref)
+def factor_kernel(
+    metrics_hbm, shift_hbm, factor_ref,
+    gamma_ref, base_ref, edge_ref, x_ref, above_ref, inverse_ref, metrics_ref, shift_ref, sems,
+):
+    copies = [
+        pltpu.make_async_copy(metrics_hbm, metrics_ref, sems.at[0]), pltpu.make_async_copy(shift_hbm, shift_ref, sems.at[1])
+    ]
+    for copy in copies:
+        copy.start()
+    for copy in copies:
+        copy.wait()
+    over_ref, under_ref, ratio_ref, up_ref, down_ref, final_ref, local_ref, coupling_ref = factors(factor_ref)
     mine = lax.axis_index("gy")
-    shift = shift_ref[...]
+    shift = shift_ref[0]
 
     def excess(row):
         double = 2.0 * metrics_ref[row]
@@ -253,11 +271,20 @@
     above, down, inverse = one, zero, zero
     height, slope = one, one
     rest, rise = one, one
+    near, near_slope = one, one
     for y in range(1, ROWS + 1):
         if y < ROWS:
             under_ref[y] = height
             slope = slope + excess(mine * ROWS + y) * height
-            height = height + slope
+            taller = height + slope
+            ratio_ref[y] = height / taller
+            height = taller
+            inverse_metric = metrics_ref[1024 + mine * ROWS + y]
+            coupling_ref[y] = shift_ref[2] * inverse_metric
+            near_slope = near_slope + shift_ref[1] * inverse_metric * near
+            taller = near + near_slope
+            local_ref[y] = near / taller
+            near = taller
             over_ref[ROWS - y] = rest
             rise = rise + excess(mine * ROWS + ROWS - y) * rest
             rest = rest + rise
@@ -284,13 +311,12 @@
     final_ref[1] = inverse_ref[mine]
     final_ref[2] = 1.0 / (x_ref[mine] + gamma * above_ref[mine])
     final_ref[3] = gamma
-    under_ref[0] = height
 
 
 def spectrum_kernel(
-    recv_ref, factor_ref, dft_ref, table_ref, octet_ref, send_ref, own_ref, column_ref
+    recv_ref, factor_ref, dft_ref, table_ref, octet_ref, send_ref, own_ref, z_ref
 ):
-    over_ref, under_ref, up_ref, down_ref, final_ref = factors(factor_ref)
+    _, _, ratio_ref, up_ref, down_ref, _, _, _ = factors(factor_ref)
     mine = lax.axis_index("gy")
 
     def take(i):
@@ -315,65 +341,10 @@
         turned[1].append(im * cos - re * sin)
     both = dot(jnp.concatenate(turned[0] + turned[1], 0), dft_ref[...])
     columns = [mixed[c * 8 : c * 8 + 8, 2 * COLS :] for c in range(2)]
-    near = [jnp.zeros((8, COLS), F32)] * 2
-    far = [jnp.zeros((8, COLS), F32)] * 2
-    for y in range(1, ROWS):
-        over, under = over_ref[y], under_ref[y]
-        for c in range(2):
-            source = wide(columns[c][:, y : y + 1])
-            source = jnp.concatenate([source, source], 1)
-            near[c] = near[c] + over * source
-            far[c] = far[c] + under * source
-    gamma = final_ref[3]
-    sides = []
-    for line, extra in enumerate((near, far)):
-        re_cos = both[line * 8 : line * 8 + 8, :COLS]
-        re_sin = both[line * 8 : line * 8 + 8, COLS:]
-        im_cos = both[16 + line * 8 : 24 + line * 8, :COLS]
-        im_sin = both[16 + line * 8 : 24 + line * 8, COLS:]
-        sides.append((re_cos + im_sin + extra[0] * gamma, im_cos - re_sin + extra[1] * gamma))
-    for c in range(2):
-        own_ref[c], own_ref[2 + c] = sides[0][c], sides[1][c]
-        column_ref[c] = columns[c]
-        send_ref[mine, c] = jnp.zeros((8, COLS), F32)
-    up, down = up_ref[mine], down_ref[mine]
-
-    def above(band, carry):
-        factor = up_ref[band]
-        for c in range(2):
-            send_ref[band, c] = carry[c]
-        return tuple(value * factor for value in carry)
-
-    def below(step, carry):
-        band = mine - 1 - step
-        factor = down_ref[band]
-        for c in range(2):
-            send_ref[band, c] = carry[c]
-        return tuple(value * factor for value in carry)
-
-    lax.fori_loop(mine + 1, BANDS, above, tuple(sides[1][c] + up * sides[0][c] for c in range(2)))
-    lax.fori_loop(0, mine, below, tuple(sides[0][c] + down * sides[1][c] for c in range(2)))
-
-
-def column_kernel(column_ref, factor_ref, metric_ref, wave_ref, edge_ref, out_ref, z_ref, ratio_ref):
-    under_ref = factors(factor_ref)[1]
-    first = lax.axis_index("gy") * ROWS
-    shift = local_shift(wave_ref, edge_ref)
-    height = jnp.ones((8, COLS), F32)
-    slope = jnp.ones((8, COLS), F32)
-    for y in range(1, ROWS):
-        inverse = splat_inverse(metric_ref, first + y)
-        out_ref[ROWS + y] = edge_ref[0] * inverse
-        slope = slope + shift * inverse * height
-        taller = height + slope
-        out_ref[y] = height / taller
-        height = taller
     lanes = lane_ids()
-    columns = [column_ref[c] for c in range(2)]
     state = [jnp.zeros((8, COLS), F32)] * 2
     for y in range(1, ROWS):
-        ratio = under_ref[y] / under_ref[(y + 1) % ROWS]
-        ratio_ref[y] = ratio
+        ratio = ratio_ref[y]
         for c in range(2):
             source = wide(columns[c][:, y : y + 1])
             state[c] = (jnp.concatenate([source, source], 1) + state[c]) * ratio
@@ -385,13 +356,40 @@
         for c in range(2):
             upper[c] = z_ref[y, c] + ratio * upper[c]
             total[c] = jnp.where(lanes == y, row_sum(upper[c]), total[c])
-    out_ref[0] = jnp.concatenate(total, 1)
+    sides = []
+    for line, extra in enumerate((upper, state)):
+        re_cos = both[line * 8 : line * 8 + 8, :COLS]
+        re_sin = both[line * 8 : line * 8 + 8, COLS:]
+        im_cos = both[16 + line * 8 : 24 + line * 8, :COLS]
+        im_sin = both[16 + line * 8 : 24 + line * 8, COLS:]
+        sides.append((re_cos + im_sin + extra[0], im_cos - re_sin + extra[1]))
+    for c in range(2):
+        own_ref[c], own_ref[2 + c] = sides[0][c], sides[1][c]
+        send_ref[mine, c] = jnp.zeros((8, COLS), F32)
+    own_ref[4] = jnp.concatenate(total, 1)
+    up, down = up_ref[mine], down_ref[mine]
+
+    def above(band, carry):
+        factor = up_ref[band]
+        for c in range(2):
+            send_ref[band, c] = carry[c]
+        return tuple(value * factor for value in carry)
+
+    def below(step, carry):
+        band = mine - 1 - step
+        factor = down_ref[band]
+        for c in range(2):
+            send_ref[band, c] = carry[c]
+        return tuple(value * factor for value in carry)
+
+    lax.fori_loop(mine + 1, BANDS, above, tuple(sides[1][c] + up * sides[0][c] for c in range(2)))
+    lax.fori_loop(0, mine, below, tuple(sides[0][c] + down * sides[1][c] for c in range(2)))
 
 
 def separator_kernel(
-    recv_ref, own_ref, factor_ref, local_ref, dft_ref, table_ref, octet_ref, send_ref
+    recv_ref, own_ref, factor_ref, dft_ref, table_ref, octet_ref, send_ref
 ):
-    over_ref, under_ref, _, _, final_ref = factors(factor_ref)
+    over_ref, under_ref, _, _, _, final_ref, _, _ = factors(factor_ref)
     mine = lax.axis_index("gy")
     from_below = [own_ref[c] for c in range(2)]
     from_above = [own_ref[2 + c] for c in range(2)]
@@ -405,7 +403,7 @@
     far = [from_above[c] * inverse + down * near[c] for c in range(2)]
     lanes = lane_ids()
     both = dot(jnp.concatenate([near[0], far[0], near[1], far[1]], 0), dft_ref[...])
-    total = [local_ref[0, :, c * 128 : c * 128 + 128] for c in range(2)]
+    total = [own_ref[4, :, c * 128 : c * 128 + 128] for c in range(2)]
     gamma = final_ref[3]
     near = [value * gamma for value in near]
     far = [value * gamma for value in far]
@@ -438,7 +436,8 @@
             send_ref[pl.ds(10 + c * 3 + pad, 8, stride=16), :] = jnp.zeros((8, 128), F32)
 
 
-def finish_kernel(recv_ref, solved_ref, local_ref, sine_ref, edge_ref, out_hbm, z_ref, o_lo, o_hi, sems):
+def finish_kernel(recv_ref, solved_ref, factor_ref, sine_ref, edge_ref, out_hbm, z_ref, o_lo, o_hi, sems):
+    local_ref, coupling_ref = factors(factor_ref)[6:]
     def take(i):
         return recv_ref[pl.ds(i, 8, stride=16), :]
 
@@ -452,7 +451,7 @@
     state = [edges[c * 8 : c * 8 + 8] for c in range(2)]
     for y in range(1, ROWS):
         ratio = local_ref[y]
-        coupling = local_ref[ROWS + y]
+        coupling = coupling_ref[y]
         for c in range(2):
             here = wide(columns[c][:, y : y + 1])
             there = wide(columns[c][:, ROWS + y : ROWS + y + 1])
@@ -514,50 +513,42 @@
     full, lines, side, bands = (ROWS, 8, COLS), (ROWS, 2, 8, COLS), (16, PITCH, 128), (BANDS, 8, COLS)
     solved, send, metrics, shift = call(
         local_kernel,
-        [lines, (128, 128), (16, 128), (8, COLS)],
+        [lines, (128, 128), (16, 128), (3, 8, COLS)],
         [
-            full, lines, side, side, (COLS, COLS), (5, 8, COLS), (8, 128),
+            (16, 128), (3, 8, COLS), (128, 128), full, lines, side, side, (COLS, COLS), (5, 8, COLS), (8, 128),
             pltpu.SMEM((1024,), F32), pltpu.SMEM((8,), F32),
             pltpu.SemaphoreType.DMA((4,)), pltpu.SemaphoreType.DMA((5,)), pltpu.SemaphoreType.DMA((4,)),
         ],
         rhs.reshape(16, ROWS, COLS), metric, metric.reshape(8, 128), wavenumber, sine, edge,
-        space=pltpu.HBM, far=(0, 1), manual=(0,),
+        space=pltpu.HBM, far=(0, 1, 2, 3), manual=(0, 1, 2, 3),
     )
     recv = lax.all_to_all(send.reshape(8, 16, 128), "gx", 0, 0, tiled=True)
     (factor,) = call(
         factor_kernel,
-        [(2 * ROWS + 2 * BANDS + 4, 8, COLS)],
-        [bands] * 6,
+        [(5 * ROWS + 2 * BANDS + 4, 8, COLS)],
+        [bands] * 6 + [pltpu.SMEM((2048,), F32), (3, 8, COLS), pltpu.SemaphoreType.DMA((2,))],
         metrics.reshape(2048), shift,
-        scalars=(0,),
-    )
-    send, own, column = call(
+        space=pltpu.HBM,
+    )
+    send, own = call(
         spectrum_kernel,
-        [(BANDS, 2, 8, COLS), (4, 8, COLS), (2, 8, 128)],
-        [],
+        [(BANDS, 2, 8, COLS), (5, 8, COLS)],
+        [lines],
         recv.reshape(128, 128), factor, dft, table, jnp.asarray(octet_forward()),
-        far=(0,),
     )
     recv = lax.all_to_all(send, "gy", 0, 0, tiled=True)
-    (local,) = call(
-        column_kernel,
-        [(2 * ROWS, 8, COLS)],
-        [lines, full],
-        column, factor, metric, wavenumber, edge,
-        scalars=(2, 3),
-    )
     (send,) = call(
         separator_kernel,
         [(128, 128)],
         [],
-        recv, own, factor, local, dft, table, jnp.asarray(octet_inverse()),
+        recv, own, factor, dft, table, jnp.asarray(octet_inverse()),
     )
     recv = lax.all_to_all(send.reshape(8, 16, 128), "gx", 0, 0, tiled=True)
     (out,) = call(
         finish_kernel,
         [(16, ROWS, COLS)],
         [lines, side, side, pltpu.SemaphoreType.DMA((4,))],
-        recv.reshape(128, 128), solved, local, sine, edge,
+        recv.reshape(128, 128), solved, factor, sine, edge,
         far=(0,), manual=(0,),
     )
     return out.reshape(8, 2, ROWS, COLS)

time: 45.9 us -> 45.3 us (0.987)
  blocking collectives: 10.5 us -> 25.8 us
  starting transfers between devices: 13.6 us -> 5.98 us
  waiting for transfers between devices: 6.9 us -> 0.29 us
  Pallas kernels: 14.4 us -> 12.7 us
    all_to_all x0 -> x1, blocking collectives: none -> 14.9 us  [per_device(): recv = lax.all_to_all(send, 'gy', 0, 0, tiled=True)]
    all_to_all x1 -> x0, starting transfers between devices: 7.6 us -> none  [per_device(): recv = lax.all_to_all(send, 'gy', 0, 0, tiled=True)]
    all_to_all x1 -> x0, waiting for transfers between devices: 6.2 us -> none  [per_device(): recv = lax.all_to_all(send, 'gy', 0, 0, tiled=True)]
    pallas_call x6 -> x5, Pallas kernels: 14.4 us -> 12.7 us  [call(): pl.pallas_call(kernel, out_shape=[(pltpu.HBM if i in far else pltpu.VMEM)...]
  transfers between devices with their start and end apart: 2 -> 1, of which waited for: 2 -> 1; matrix products, arithmetic and copies ran while one was open for 0% -> 0% of each run, Pallas kernels for 11% -> 10%
where the time goes in v5:
time: 45.3 us; the launch traced here: 44.9 us
  blocking collectives  25.8 us (57%)
  Pallas kernels  12.7 us (28%)
  starting transfers between devices  5.98 us (13%)
    all_to_all x1, blocking collectives, per_device(): recv = lax.all_to_all(send, 'gy', 0, 0, tiled=True)  14.9 us
    pallas_call x5, Pallas kernels, call(): pl.pallas_call(kernel, out_shape=[(pltpu.HBM if i in far else pltpu.VMEM)...  12.7 us
    all_to_all x1, blocking collectives, per_device(): recv = lax.all_to_all(send.reshape(8, 16, 128), 'gx', 0, 0, tiled=True)  11 us
    all_to_all x1, starting transfers between devices, per_device(): recv = lax.all_to_all(send.reshape(8, 16, 128), 'gx', 0, 0, tiled=True)  5.98 us
  transfers between devices with their start and end apart: 1, of which 1 were waited for; matrix products, arithmetic and copies ran while one was open for 0% of the time, Pallas kernels for 10%

profile of v5, /device:TPU:1, one launch (start us, length us, event | category | flops | bytes accessed | tf_op | source)
XLA Modules:
  0.0 44.9 jit_solution(17625483843481337926)
XLA Ops:
  0.0 0.0 copy-start.4
  0.0 0.0 copy-start
  0.0 0.0 copy-start.6
  0.0 3.8 %shard_map.91 = (f32[64,2,8,256]{3,2,1,0:T(8,128)}, f32[128,128]{1,0:T(8,128)}, f32[16,128]{1,0:T(8,128)}, f32[3,8,256]{2,1,0:T(8,128)}) custom-call(f32[16,64,256]{2,1,0:T(8,128)} %bitcast.11, f32[1024]{0:T(1024)} %metric_hbm.1, f32[8,128]{1,0:T(8,128)} %bitcast.13, f32[8]{0:T(128)} %wave_hbm.1, f32[256,256]{1,0:T(8,128)} %constant.12.clone.sine_hbm.sine_ref, ...), custom_call_target="tpu_custom_call" | custom-call | tf_op jit(solution)/shard_map/pallas_call | solution.py:500
  3.8 6.0 %all-to-all-start = ((f32[8,16,128]{2,1,0:T(8,128)}), f32[8,16,128]{2,1,0:T(8,128)S(1)}, u32[]{:S(2)}, u32[]{:S(2)}) async-start(f32[8,16,128]{2,1,0:T(8,128)} %bitcast.12), calls=%async_computation | async-start | bytes 131072 | tf_op jit(solution)/shard_map/all_to_all | solution.py:525
  9.8 0.0 copy-start.5
  9.8 4.5 %shard_map.92.factor_ref = f32[356,8,256]{2,1,0:T(8,128)S(1)} custom-call(f32[2048]{0:T(1024)} %bitcast.14, f32[3,8,256]{2,1,0:T(8,128)} %get-tuple-element.13.shift_hbm), custom_call_target="tpu_custom_call" | custom-call | tf_op jit(solution)/shard_map/pallas_call | solution.py:500
  14.4 0.3 all-to-all-done
  14.7 0.0 copy-done.4
  14.7 0.0 copy-done
  14.7 0.0 copy-done.6
  14.7 0.9 %shard_map.93 = (f32[16,2,8,256]{3,2,1,0:T(8,128)S(1)}, f32[5,8,256]{2,1,0:T(8,128)S(1)}) custom-call(f32[128,128]{1,0:T(8,128)S(1)} %bitcast.8, f32[356,8,256]{2,1,0:T(8,128)S(1)} %shard_map.92.factor_ref, f32[256,512]{1,0:T(8,128)S(1)} %copy-done, f32[2,8,256]{2,1,0:T(8,128)S(1)} %copy-done.4, f32[16,16]{1,0:T(8,128)S(1)} %copy-done.6), custom_call_target="tpu_custom_call" | custom-call | tf_op jit(solution)/shard_map/pallas_call | solution.py:500
  15.6 0.0 copy-start.1
  15.6 0.0 copy-start.2
  15.6 0.0 copy-start.3
  15.6 14.9 %all_to_all.15.recv_ref = f32[16,2,8,256]{3,2,1,0:T(8,128)S(1)} all-to-all(f32[16,2,8,256]{3,2,1,0:T(8,128)S(1)} %get-tuple-element.14), channel_id=1, replica_groups=mesh['gx'=8,'gy'=16] {'gy'}, dimensions={0} | all-to-all | bytes 524288 | tf_op jit(solution)/shard_map/all_to_all | solution.py:539
  30.5 0.0 copy-done.5
  30.5 0.8 %shard_map.94 = f32[128,128]{1,0:T(8,128)S(1)} custom-call(f32[16,2,8,256]{3,2,1,0:T(8,128)S(1)} %all_to_all.15.recv_ref, f32[5,8,256]{2,1,0:T(8,128)S(1)} %get-tuple-element.15.own_ref, f32[356,8,256]{2,1,0:T(8,128)S(1)} %shard_map.92.factor_ref, f32[256,512]{1,0:T(8,128)S(1)} %copy-done, f32[2,8,256]{2,1,0:T(8,128)S(1)} %copy-done.4, f32[32,16]{1,0:T(8,128)S(1)} %copy-done.5), custom_call_target="tpu_custom_call" | custom-call | tf_op jit(solution)/shard_map/pallas_call | solution.py:500
  31.3 11.0 %all_to_all.16 = f32[8,16,128]{2,1,0:T(8,128)S(1)} all-to-all(f32[8,16,128]{2,1,0:T(8,128)S(1)} %bitcast.10), channel_id=1, replica_groups=mesh['gx'=8,'gy'=16] {'gx'}, dimensions={0} | all-to-all | bytes 131072 | tf_op jit(solution)/shard_map/all_to_all | solution.py:546
  42.3 0.0 copy-done.1
  42.3 0.0 copy-done.2
  42.3 0.0 copy-done.3
  42.3 2.7 %shard_map.95 = f32[16,64,256]{2,1,0:T(8,128)} custom-call(f32[128,128]{1,0:T(8,128)S(1)} %bitcast.9, f32[64,2,8,256]{3,2,1,0:T(8,128)S(1)} %copy-done.1, f32[356,8,256]{2,1,0:T(8,128)S(1)} %shard_map.92.factor_ref, f32[256,256]{1,0:T(8,128)S(1)} %copy-done.2, f32[5,8,256]{2,1,0:T(8,128)S(1)} %copy-done.3), custom_call_target="tpu_custom_call" | custom-call | tf_op jit(solution)/shard_map/pallas_call | solution.py:500
Async XLA Ops:
  0.0 14.7 %copy-start.4 = (f32[2,8,256]{2,1,0:T(8,128)S(1)}, f32[2,8,256]{2,1,0:T(8,128)}, u32[]{:S(2)}) copy-start(f32[2,8,256]{2,1,0:T(8,128)} %constant.15.clone.table_ref) | copy-start | bytes 49156
  0.0 14.7 %copy-start = (f32[256,512]{1,0:T(8,128)S(1)}, f32[256,512]{1,0:T(8,128)}, u32[]{:S(2)}) copy-start(f32[256,512]{1,0:T(8,128)} %constant.14.clone.dft_ref) | copy-start | bytes 1572868
  0.0 14.7 %copy-start.6 = (f32[16,16]{1,0:T(8,128)S(1)}, f32[16,16]{1,0:T(8,128)}, u32[]{:S(2)}) copy-start(f32[16,16]{1,0:T(8,128)} %constant.16.clone.octet_ref) | copy-start | bytes 3076
  3.8 10.8 %all-to-all-start = ((f32[8,16,128]{2,1,0:T(8,128)}), f32[8,16,128]{2,1,0:T(8,128)S(1)}, u32[]{:S(2)}, u32[]{:S(2)}) async-start(f32[8,16,128]{2,1,0:T(8,128)} %bitcast.12), calls=%async_computation | async-start | bytes 131072 | tf_op jit(solution)/shard_map/all_to_all | solution.py:525
  9.8 20.7 %copy-start.5 = (f32[32,16]{1,0:T(8,128)S(1)}, f32[32,16]{1,0:T(8,128)}, u32[]{:S(2)}) copy-start(f32[32,16]{1,0:T(8,128)} %constant.17.clone.octet_ref) | copy-start | bytes 6148
  15.6 26.7 %copy-start.1 = (f32[64,2,8,256]{3,2,1,0:T(8,128)S(1)}, f32[64,2,8,256]{3,2,1,0:T(8,128)}, u32[]{:S(2)}) copy-start(f32[64,2,8,256]{3,2,1,0:T(8,128)} %get-tuple-element.16.solved_ref) | copy-start | bytes 3145732
  15.6 26.7 %copy-start.2 = (f32[256,256]{1,0:T(8,128)S(1)}, f32[256,256]{1,0:T(8,128)}, u32[]{:S(2)}) copy-start(f32[256,256]{1,0:T(8,128)} %constant.12.clone.sine_hbm.sine_ref) | copy-start | bytes 786436
  15.6 26.7 %copy-start.3 = (f32[5,8,256]{2,1,0:T(8,128)S(1)}, f32[5,8,256]{2,1,0:T(8,128)}, u32[]{:S(2)}) copy-start(f32[5,8,256]{2,1,0:T(8,128)} %constant.13.clone.edge_hbm.edge_ref) | copy-start | bytes 122884

commit v6 on v5

--- a/solution.py
+++ b/solution.py
@@ -105,7 +105,7 @@
 
 
 def local_kernel(
-    rhs_hbm, metric_hbm, tiled_hbm, wave_hbm, sine_hbm, edge_hbm, solved_hbm, send_hbm, metrics_hbm, shift_hbm,
+    rhs_hbm, metric_hbm, tiled_hbm, wave_hbm, sine_hbm, edge_hbm, solved_hbm, send_hbm, metrics_hbm, shift_hbm, ratio_hbm,
     metrics_ref, shift_ref, send_ref, ratio_ref, z_ref, r_lo, r_hi, sine_ref, edge_ref, metric_vec, metric_ref, wave_ref, rhs_sem, sems, out_sem,
 ):
     first = lax.axis_index("gy") * ROWS
@@ -130,9 +130,7 @@
     metrics_ref[:8, :] = metric_vec[...]
     metrics_ref[8:, :] = 1.0 / metric_vec[...]
     shift = local_shift(wave_ref, edge_ref)
-    shift_ref[0] = edge_ref[3] + wave_ref[lax.axis_index("gx")]
-    shift_ref[1] = shift
-    shift_ref[2] = edge_ref[0]
+    shift_ref[...] = edge_ref[3] + wave_ref[lax.axis_index("gx")]
     done = [
         pltpu.make_async_copy(metrics_ref, metrics_hbm, sems.at[1]), pltpu.make_async_copy(shift_ref, shift_hbm, sems.at[2])
     ]
@@ -146,6 +144,9 @@
         taller = height + slope
         ratio_ref[y] = height / taller
         height = taller
+    ratio_ref[0] = jnp.ones((8, COLS), F32)
+    done.append(pltpu.make_async_copy(ratio_ref, ratio_hbm, sems.at[3]))
+    done[-1].start()
     small[4].wait()
     sine = sine_ref[...]
     flat = [ref.reshape(16 * PITCH, 128) for ref in (r_lo, r_hi)]
@@ -212,7 +213,7 @@
 
 
 def factors(ref):
-    sizes = (ROWS, ROWS, ROWS, BANDS, BANDS, 4, ROWS, ROWS)
+    sizes = (ROWS, ROWS, ROWS, BANDS, BANDS, 4)
     starts = np.cumsum((0,) + sizes)
     return [ref.at[pl.ds(int(a), n)] for a, n in zip(starts, sizes)]
 
@@ -228,9 +229,9 @@
         copy.start()
     for copy in copies:
         copy.wait()
-    over_ref, under_ref, ratio_ref, up_ref, down_ref, final_ref, local_ref, coupling_ref = factors(factor_ref)
+    over_ref, under_ref, ratio_ref, up_ref, down_ref, final_ref = factors(factor_ref)
     mine = lax.axis_index("gy")
-    shift = shift_ref[0]
+    shift = shift_ref[...]
 
     def excess(row):
         double = 2.0 * metrics_ref[row]
@@ -271,7 +272,6 @@
     above, down, inverse = one, zero, zero
     height, slope = one, one
     rest, rise = one, one
-    near, near_slope = one, one
     for y in range(1, ROWS + 1):
         if y < ROWS:
             under_ref[y] = height
@@ -279,12 +279,6 @@
             taller = height + slope
             ratio_ref[y] = height / taller
             height = taller
-            inverse_metric = metrics_ref[1024 + mine * ROWS + y]
-            coupling_ref[y] = shift_ref[2] * inverse_metric
-            near_slope = near_slope + shift_ref[1] * inverse_metric * near
-            taller = near + near_slope
-            local_ref[y] = near / taller
-            near = taller
             over_ref[ROWS - y] = rest
             rise = rise + excess(mine * ROWS + ROWS - y) * rest
             rest = rest + rise
@@ -316,7 +310,7 @@
 def spectrum_kernel(
     recv_ref, factor_ref, dft_ref, table_ref, octet_ref, send_ref, own_ref, z_ref
 ):
-    _, _, ratio_ref, up_ref, down_ref, _, _, _ = factors(factor_ref)
+    _, _, ratio_ref, up_ref, down_ref, _ = factors(factor_ref)
     mine = lax.axis_index("gy")
 
     def take(i):
@@ -389,7 +383,7 @@
 def separator_kernel(
     recv_ref, own_ref, factor_ref, dft_ref, table_ref, octet_ref, send_ref
 ):
-    over_ref, under_ref, _, _, _, final_ref, _, _ = factors(factor_ref)
+    over_ref, under_ref, _, _, _, final_ref = factors(factor_ref)
     mine = lax.axis_index("gy")
     from_below = [own_ref[c] for c in range(2)]
     from_above = [own_ref[2 + c] for c in range(2)]
@@ -436,8 +430,12 @@
             send_ref[pl.ds(10 + c * 3 + pad, 8, stride=16), :] = jnp.zeros((8, 128), F32)
 
 
-def finish_kernel(recv_ref, solved_ref, factor_ref, sine_ref, edge_ref, out_hbm, z_ref, o_lo, o_hi, sems):
-    local_ref, coupling_ref = factors(factor_ref)[6:]
+def finish_kernel(recv_ref, solved_ref, local_ref, metric_ref, sine_ref, edge_ref, out_hbm, z_ref, o_lo, o_hi, sems):
+    band = lax.axis_index("gy")
+    lanes = lane_ids()
+    metric = jnp.broadcast_to(metric_ref[pl.ds(band // 2, 1), :], (8, 128))
+    swapped = pltpu.roll(metric, ROWS, 1)
+    metric = jnp.where((lanes < ROWS) == (band % 2 == 0), metric, swapped)
     def take(i):
         return recv_ref[pl.ds(i, 8, stride=16), :]
 
@@ -446,18 +444,18 @@
     far = [jnp.concatenate([take(4 + c * 2), take(5 + c * 2)], 1) for c in range(2)]
     columns = [take(8 + c) for c in range(2)]
     edges = dot(jnp.concatenate(near + far, 0), sine)
-    flip = edge_ref[4]
+    scaled = [value / metric for value in columns]
+    left, flip = edge_ref[0], edge_ref[4]
     zero_lane = lax.broadcasted_iota(jnp.int32, (8, COLS), 1) == 0
     state = [edges[c * 8 : c * 8 + 8] for c in range(2)]
     for y in range(1, ROWS):
         ratio = local_ref[y]
-        coupling = coupling_ref[y]
-        for c in range(2):
-            here = wide(columns[c][:, y : y + 1])
-            there = wide(columns[c][:, ROWS + y : ROWS + y + 1])
+        for c in range(2):
+            here = wide(scaled[c][:, y : y + 1])
+            there = wide(scaled[c][:, ROWS + y : ROWS + y + 1])
             here = jnp.concatenate([here, here], 1)
             there = jnp.concatenate([there, there], 1)
-            state[c] = (state[c] + coupling * (here + flip * there)) * ratio
+            state[c] = (state[c] + left * (here + flip * there)) * ratio
             z_ref[y, c] = state[c]
     upper = [edges[16 + c * 8 : 24 + c * 8] for c in range(2)]
     flat = [ref.reshape(16 * PITCH, 128) for ref in (o_lo, o_hi)]
@@ -511,22 +509,22 @@
     sine, edge = jnp.asarray(sine_table()), jnp.asarray(edge_table())
     dft, table = jnp.asarray(dft_table()), jnp.asarray(wave_table())
     full, lines, side, bands = (ROWS, 8, COLS), (ROWS, 2, 8, COLS), (16, PITCH, 128), (BANDS, 8, COLS)
-    solved, send, metrics, shift = call(
+    solved, send, metrics, shift, ratio = call(
         local_kernel,
-        [lines, (128, 128), (16, 128), (3, 8, COLS)],
+        [lines, (128, 128), (16, 128), (8, COLS), full],
         [
-            (16, 128), (3, 8, COLS), (128, 128), full, lines, side, side, (COLS, COLS), (5, 8, COLS), (8, 128),
+            (16, 128), (8, COLS), (128, 128), full, lines, side, side, (COLS, COLS), (5, 8, COLS), (8, 128),
             pltpu.SMEM((1024,), F32), pltpu.SMEM((8,), F32),
             pltpu.SemaphoreType.DMA((4,)), pltpu.SemaphoreType.DMA((5,)), pltpu.SemaphoreType.DMA((4,)),
         ],
         rhs.reshape(16, ROWS, COLS), metric, metric.reshape(8, 128), wavenumber, sine, edge,
-        space=pltpu.HBM, far=(0, 1, 2, 3), manual=(0, 1, 2, 3),
+        space=pltpu.HBM, far=range(5), manual=range(5),
     )
     recv = lax.all_to_all(send.reshape(8, 16, 128), "gx", 0, 0, tiled=True)
     (factor,) = call(
         factor_kernel,
-        [(5 * ROWS + 2 * BANDS + 4, 8, COLS)],
-        [bands] * 6 + [pltpu.SMEM((2048,), F32), (3, 8, COLS), pltpu.SemaphoreType.DMA((2,))],
+        [(3 * ROWS + 2 * BANDS + 4, 8, COLS)],
+        [bands] * 6 + [pltpu.SMEM((2048,), F32), (8, COLS), pltpu.SemaphoreType.DMA((2,))],
         metrics.reshape(2048), shift,
         space=pltpu.HBM,
     )
@@ -548,7 +546,7 @@
         finish_kernel,
         [(16, ROWS, COLS)],
         [lines, side, side, pltpu.SemaphoreType.DMA((4,))],
-        recv.reshape(128, 128), solved, factor, sine, edge,
+        recv.reshape(128, 128), solved, ratio, metric.reshape(8, 128), sine, edge,
         far=(0,), manual=(0,),
     )
     return out.reshape(8, 2, ROWS, COLS)

time: 45.3 us -> 45.2 us (level)
  no operation moved by 1% of the time
where the time goes in v6:
time: 45.2 us; the launch traced here: 44.9 us
  blocking collectives  25.6 us (57%)
  Pallas kernels  12.6 us (28%)
  starting transfers between devices  5.98 us (13%)
  waiting for transfers between devices  0.54 us (1%)
    all_to_all x1, blocking collectives, per_device(): recv = lax.all_to_all(send, 'gy', 0, 0, tiled=True)  14.9 us
    pallas_call x5, Pallas kernels, call(): pl.pallas_call(kernel, out_shape=[(pltpu.HBM if i in far else pltpu.VMEM)...  12.6 us
    all_to_all x1, blocking collectives, per_device(): recv = lax.all_to_all(send.reshape(8, 16, 128), 'gx', 0, 0, tiled=True)  10.7 us
    all_to_all x1, starting transfers between devices, per_device(): recv = lax.all_to_all(send.reshape(8, 16, 128), 'gx', 0, 0, tiled=True)  5.98 us
  transfers between devices with their start and end apart: 1, of which 1 were waited for; matrix products, arithmetic and copies ran while one was open for 0% of the time, Pallas kernels for 10%

profile of v6, /device:TPU:1, one launch (start us, length us, event | category | flops | bytes accessed | tf_op | source)
XLA Modules:
  0.0 44.9 jit_solution(747174043578321771)
XLA Ops:
  0.0 0.0 copy-start.5
  0.0 0.0 copy-start
  0.0 0.0 copy-start.8
  0.0 3.8 %shard_map.91 = (f32[64,2,8,256]{3,2,1,0:T(8,128)}, f32[128,128]{1,0:T(8,128)}, f32[16,128]{1,0:T(8,128)}, f32[8,256]{1,0:T(8,128)}, f32[64,8,256]{2,1,0:T(8,128)}) custom-call(f32[16,64,256]{2,1,0:T(8,128)} %bitcast.13, f32[1024]{0:T(1024)} %metric_hbm.1, f32[8,128]{1,0:T(8,128)} %bitcast.11, f32[8]{0:T(128)} %wave_hbm.1, ...), custom_call_target="tpu_custom_call" | custom-call | tf_op jit(solution)/shard_map/pallas_call | solution.py:498
  3.8 6.0 %all-to-all-start = ((f32[8,16,128]{2,1,0:T(8,128)}), f32[8,16,128]{2,1,0:T(8,128)S(1)}, u32[]{:S(2)}, u32[]{:S(2)}) async-start(f32[8,16,128]{2,1,0:T(8,128)} %bitcast.14), calls=%async_computation | async-start | bytes 131072 | tf_op jit(solution)/shard_map/all_to_all | solution.py:523
  9.8 4.3 %shard_map.92.factor_ref = f32[228,8,256]{2,1,0:T(8,128)S(1)} custom-call(f32[2048]{0:T(1024)} %bitcast.15, f32[8,256]{1,0:T(8,128)} %get-tuple-element.14.shift_hbm), custom_call_target="tpu_custom_call" | custom-call | tf_op jit(solution)/shard_map/pallas_call | solution.py:498
  14.1 0.0 copy-start.7
  14.1 0.5 %all-to-all-done = f32[8,16,128]{2,1,0:T(8,128)S(1)} async-done(((f32[8,16,128]{2,1,0:T(8,128)}), f32[8,16,128]{2,1,0:T(8,128)S(1)}, u32[]{:S(2)}, u32[]{:S(2)}) %all-to-all-start) | async-done | bytes 65568 | tf_op jit(solution)/shard_map/all_to_all | solution.py:523
  14.7 0.0 copy-done.5
  14.7 0.0 copy-done
  14.7 0.0 copy-done.8
  14.7 0.9 %shard_map.93 = (f32[16,2,8,256]{3,2,1,0:T(8,128)S(1)}, f32[5,8,256]{2,1,0:T(8,128)S(1)}) custom-call(f32[128,128]{1,0:T(8,128)S(1)} %bitcast.8, f32[228,8,256]{2,1,0:T(8,128)S(1)} %shard_map.92.factor_ref, f32[256,512]{1,0:T(8,128)S(1)} %copy-done, f32[2,8,256]{2,1,0:T(8,128)S(1)} %copy-done.5, f32[16,16]{1,0:T(8,128)S(1)} %copy-done.8), custom_call_target="tpu_custom_call" | custom-call | tf_op jit(solution)/shard_map/pallas_call | solution.py:498
  15.6 0.0 copy-start.1
  15.6 0.0 copy-start.2
  15.6 0.0 copy-start.3
  15.6 0.0 copy-start.4
  15.6 0.0 copy-start.6
  15.7 14.9 %all_to_all.15.recv_ref = f32[16,2,8,256]{3,2,1,0:T(8,128)S(1)} all-to-all(f32[16,2,8,256]{3,2,1,0:T(8,128)S(1)} %get-tuple-element.15), channel_id=1, replica_groups=mesh['gx'=8,'gy'=16] {'gy'}, dimensions={0} | all-to-all | bytes 524288 | tf_op jit(solution)/shard_map/all_to_all | solution.py:537
  30.6 0.0 copy-done.7
  30.6 0.8 %shard_map.94 = f32[128,128]{1,0:T(8,128)S(1)} custom-call(f32[16,2,8,256]{3,2,1,0:T(8,128)S(1)} %all_to_all.15.recv_ref, f32[5,8,256]{2,1,0:T(8,128)S(1)} %get-tuple-element.16.own_ref, f32[228,8,256]{2,1,0:T(8,128)S(1)} %shard_map.92.factor_ref, f32[256,512]{1,0:T(8,128)S(1)} %copy-done, f32[2,8,256]{2,1,0:T(8,128)S(1)} %copy-done.5, f32[32,16]{1,0:T(8,128)S(1)} %copy-done.7), custom_call_target="tpu_custom_call" | custom-call | tf_op jit(solution)/shard_map/pallas_call | solution.py:498
  31.4 10.7 %all_to_all.16 = f32[8,16,128]{2,1,0:T(8,128)S(1)} all-to-all(f32[8,16,128]{2,1,0:T(8,128)S(1)} %bitcast.9), channel_id=1, replica_groups=mesh['gx'=8,'gy'=16] {'gx'}, dimensions={0} | all-to-all | bytes 131072 | tf_op jit(solution)/shard_map/all_to_all | solution.py:544
  42.1 0.0 copy-done.1
  42.1 0.0 copy-done.2
  42.1 0.0 copy-done.3
  42.1 0.0 copy-done.4
  42.1 0.0 copy-done.6
  42.1 2.8 %shard_map.95 = f32[16,64,256]{2,1,0:T(8,128)} custom-call(f32[128,128]{1,0:T(8,128)S(1)} %bitcast.10, f32[64,2,8,256]{3,2,1,0:T(8,128)S(1)} %copy-done.2, f32[64,8,256]{2,1,0:T(8,128)S(1)} %copy-done.3, f32[8,128]{1,0:T(8,128)S(1)} %bitcast.12, f32[256,256]{1,0:T(8,128)S(1)} %copy-done.1, f32[5,8,256]{2,1,0:T(8,128)S(1)} %copy-done.4), custom_call_target="tpu_custom_call" | custom-call | tf_op jit(solution)/shard_map/pallas_call | solution.py:498
Async XLA Ops:
  0.0 14.7 %copy-start.5 = (f32[2,8,256]{2,1,0:T(8,128)S(1)}, f32[2,8,256]{2,1,0:T(8,128)}, u32[]{:S(2)}) copy-start(f32[2,8,256]{2,1,0:T(8,128)} %constant.15.clone.table_ref) | copy-start | bytes 49156
  0.0 14.7 %copy-start = (f32[256,512]{1,0:T(8,128)S(1)}, f32[256,512]{1,0:T(8,128)}, u32[]{:S(2)}) copy-start(f32[256,512]{1,0:T(8,128)} %constant.14.clone.dft_ref) | copy-start | bytes 1572868
  0.0 14.7 %copy-start.8 = (f32[16,16]{1,0:T(8,128)S(1)}, f32[16,16]{1,0:T(8,128)}, u32[]{:S(2)}) copy-start(f32[16,16]{1,0:T(8,128)} %constant.16.clone.octet_ref) | copy-start | bytes 3076
  3.8 10.8 %all-to-all-start = ((f32[8,16,128]{2,1,0:T(8,128)}), f32[8,16,128]{2,1,0:T(8,128)S(1)}, u32[]{:S(2)}, u32[]{:S(2)}) async-start(f32[8,16,128]{2,1,0:T(8,128)} %bitcast.14), calls=%async_computation | async-start | bytes 131072 | tf_op jit(solution)/shard_map/all_to_all | solution.py:523
  14.1 16.4 %copy-start.7 = (f32[32,16]{1,0:T(8,128)S(1)}, f32[32,16]{1,0:T(8,128)}, u32[]{:S(2)}) copy-start(f32[32,16]{1,0:T(8,128)} %constant.17.clone.octet_ref) | copy-start | bytes 6148
  15.6 26.5 %copy-start.1 = (f32[256,256]{1,0:T(8,128)S(1)}, f32[256,256]{1,0:T(8,128)}, u32[]{:S(2)}) copy-start(f32[256,256]{1,0:T(8,128)} %constant.12.clone.sine_hbm.sine_ref) | copy-start | bytes 786436
  15.6 26.5 %copy-start.2 = (f32[64,2,8,256]{3,2,1,0:T(8,128)S(1)}, f32[64,2,8,256]{3,2,1,0:T(8,128)}, u32[]{:S(2)}) copy-start(f32[64,2,8,256]{3,2,1,0:T(8,128)} %get-tuple-element.17.solved_ref) | copy-start | bytes 3145732
  15.6 26.4 %copy-start.3 = (f32[64,8,256]{2,1,0:T(8,128)S(1)}, f32[64,8,256]{2,1,0:T(8,128)}, u32[]{:S(2)}) copy-start(f32[64,8,256]{2,1,0:T(8,128)} %get-tuple-element.18.local_ref) | copy-start | bytes 1572868
  15.6 26.4 %copy-start.4 = (f32[5,8,256]{2,1,0:T(8,128)S(1)}, f32[5,8,256]{2,1,0:T(8,128)}, u32[]{:S(2)}) copy-start(f32[5,8,256]{2,1,0:T(8,128)} %constant.13.clone.edge_hbm.edge_ref) | copy-start | bytes 122884
  15.6 26.4 %copy-start.6 = (f32[1024]{0:T(1024)S(1)}, f32[1024]{0:T(1024)}, u32[]{:S(2)}) copy-start(f32[1024]{0:T(1024)} %metric_hbm.1) | copy-start | bytes 12292

commit v7 on v6

--- a/solution.py
+++ b/solution.py
@@ -76,8 +76,12 @@
     return f32(np.concatenate(parts, 0) / NX)
 
 
-def dot(a, b):
-    return jnp.dot(a, b, precision=lax.Precision.HIGHEST, preferred_element_type=F32)
+def dot(a, b, precision=lax.Precision.HIGHEST):
+    return jnp.dot(a, b, precision=precision, preferred_element_type=F32)
+
+
+def short_dot(a, b):
+    return dot(a, b, lax.Precision.HIGH)
 
 
 def lane_ids():
@@ -396,7 +400,7 @@
     near = [(from_below[c] + down * from_above[c]) * pivot for c in range(2)]
     far = [from_above[c] * inverse + down * near[c] for c in range(2)]
     lanes = lane_ids()
-    both = dot(jnp.concatenate([near[0], far[0], near[1], far[1]], 0), dft_ref[...])
+    both = short_dot(jnp.concatenate([near[0], far[0], near[1], far[1]], 0), dft_ref[...])
     total = [own_ref[4, :, c * 128 : c * 128 + 128] for c in range(2)]
     gamma = final_ref[3]
     near = [value * gamma for value in near]
@@ -418,7 +422,7 @@
         turned[0].append(re * cos - im * sin)
         turned[1].append(re * sin + im * cos)
     stacked = [jnp.concatenate(turned[c] + [total[c]], 1) for c in range(2)]
-    out = dot(octet_ref[...], jnp.concatenate(stacked, 0))
+    out = short_dot(octet_ref[...], jnp.concatenate(stacked, 0))
     for c in range(2):
         for i in range(4):
             row = (i // 2) * 4 + c * 2 + i % 2
@@ -443,7 +447,7 @@
     near = [jnp.concatenate([take(c * 2), take(c * 2 + 1)], 1) for c in range(2)]
     far = [jnp.concatenate([take(4 + c * 2), take(5 + c * 2)], 1) for c in range(2)]
     columns = [take(8 + c) for c in range(2)]
-    edges = dot(jnp.concatenate(near + far, 0), sine)
+    edges = short_dot(jnp.concatenate(near + far, 0), sine)
     scaled = [value / metric for value in columns]
     left, flip = edge_ref[0], edge_ref[4]
     zero_lane = lax.broadcasted_iota(jnp.int32, (8, COLS), 1) == 0
@@ -461,18 +465,8 @@
     flat = [ref.reshape(16 * PITCH, 128) for ref in (o_lo, o_hi)]
     group, half = 8, ROWS // 2
     copies = []
-    for base in range(ROWS - group, -1, -group):
-        lines = []
-        for y in range(base + group - 1, base - 1, -1):
-            for c in range(2):
-                if y:
-                    upper[c] = z_ref[y, c] + local_ref[y] * upper[c]
-                    here = wide(columns[c][:, y : y + 1])
-                    here = jnp.concatenate([here, here], 1)
-                    lines.append(jnp.where(zero_lane, here, upper[c] + solved_ref[y, c]))
-                else:
-                    lines.append(edges[c * 8 : c * 8 + 8])
-        product = dot(jnp.concatenate(lines, 0), sine)
+
+    def store(base, product):
         for i in range(2 * group):
             rows = pl.ds(i % 2 * PITCH + base + group - 1 - i // 2, 8, stride=2 * PITCH)
             flat[0][rows, :] = product[i * 8 : i * 8 + 8, :128]
@@ -487,6 +481,24 @@
                     )
                 )
                 copies[-1].start()
+
+    behind = None
+    for base in range(ROWS - group, -1, -group):
+        lines = []
+        for y in range(base + group - 1, base - 1, -1):
+            for c in range(2):
+                if y:
+                    upper[c] = z_ref[y, c] + local_ref[y] * upper[c]
+                    here = wide(columns[c][:, y : y + 1])
+                    here = jnp.concatenate([here, here], 1)
+                    lines.append(jnp.where(zero_lane, here, upper[c] + solved_ref[y, c]))
+                else:
+                    lines.append(edges[c * 8 : c * 8 + 8])
+        product = short_dot(jnp.concatenate(lines, 0), sine)
+        if behind:
+            store(*behind)
+        behind = (base, product)
+    store(*behind)
     for copy in copies:
         copy.wait()
 

time: 45.2 us -> 44.4 us (0.982)
  Pallas kernels: 12.6 us -> 11.8 us
    pallas_call x5, Pallas kernels: 12.6 us -> 11.8 us  [call(): pl.pallas_call(kernel, out_shape=[(pltpu.HBM if i in far else pltpu.VMEM)...]
where the time goes in v7:
time: 44.4 us; the launch traced here: 44.1 us
  blocking collectives  25.6 us (58%)
  Pallas kernels  11.8 us (27%)
  starting transfers between devices  5.98 us (13%)
  waiting for transfers between devices  0.54 us (1%)
    all_to_all x1, blocking collectives, per_device(): recv = lax.all_to_all(send, 'gy', 0, 0, tiled=True)  14.9 us
    pallas_call x5, Pallas kernels, call(): pl.pallas_call(kernel, out_shape=[(pltpu.HBM if i in far else pltpu.VMEM)...  11.8 us
    all_to_all x1, blocking collectives, per_device(): recv = lax.all_to_all(send.reshape(8, 16, 128), 'gx', 0, 0, tiled=True)  10.7 us
    all_to_all x1, starting transfers between devices, per_device(): recv = lax.all_to_all(send.reshape(8, 16, 128), 'gx', 0, 0, tiled=True)  5.98 us
  transfers between devices with their start and end apart: 1, of which 1 were waited for; matrix products, arithmetic and copies ran while one was open for 0% of the time, Pallas kernels for 10%

profile of v7, /device:TPU:1, one launch (start us, length us, event | category | flops | bytes accessed | tf_op | source)
XLA Modules:
  0.0 44.1 jit_solution(12455464235589965274)
XLA Ops:
  0.0 0.0 copy-start.5
  0.0 0.0 copy-start
  0.0 0.0 copy-start.8
  0.0 3.8 %shard_map.91 = (f32[64,2,8,256]{3,2,1,0:T(8,128)}, f32[128,128]{1,0:T(8,128)}, f32[16,128]{1,0:T(8,128)}, f32[8,256]{1,0:T(8,128)}, f32[64,8,256]{2,1,0:T(8,128)}) custom-call(f32[16,64,256]{2,1,0:T(8,128)} %bitcast.13, f32[1024]{0:T(1024)} %metric_hbm.1, f32[8,128]{1,0:T(8,128)} %bitcast.11, f32[8]{0:T(128)} %wave_hbm.1, ...), custom_call_target="tpu_custom_call" | custom-call | tf_op jit(solution)/shard_map/pallas_call | solution.py:510
  3.8 6.0 %all-to-all-start = ((f32[8,16,128]{2,1,0:T(8,128)}), f32[8,16,128]{2,1,0:T(8,128)S(1)}, u32[]{:S(2)}, u32[]{:S(2)}) async-start(f32[8,16,128]{2,1,0:T(8,128)} %bitcast.14), calls=%async_computation | async-start | bytes 131072 | tf_op jit(solution)/shard_map/all_to_all | solution.py:535
  9.8 4.3 %shard_map.92.factor_ref = f32[228,8,256]{2,1,0:T(8,128)S(1)} custom-call(f32[2048]{0:T(1024)} %bitcast.15, f32[8,256]{1,0:T(8,128)} %get-tuple-element.14.shift_hbm), custom_call_target="tpu_custom_call" | custom-call | tf_op jit(solution)/shard_map/pallas_call | solution.py:510
  14.1 0.0 copy-start.7
  14.1 0.5 %all-to-all-done = f32[8,16,128]{2,1,0:T(8,128)S(1)} async-done(((f32[8,16,128]{2,1,0:T(8,128)}), f32[8,16,128]{2,1,0:T(8,128)S(1)}, u32[]{:S(2)}, u32[]{:S(2)}) %all-to-all-start) | async-done | bytes 65568 | tf_op jit(solution)/shard_map/all_to_all | solution.py:535
  14.7 0.0 copy-done.5
  14.7 0.0 copy-done
  14.7 0.0 copy-done.8
  14.7 0.9 %shard_map.93 = (f32[16,2,8,256]{3,2,1,0:T(8,128)S(1)}, f32[5,8,256]{2,1,0:T(8,128)S(1)}) custom-call(f32[128,128]{1,0:T(8,128)S(1)} %bitcast.8, f32[228,8,256]{2,1,0:T(8,128)S(1)} %shard_map.92.factor_ref, f32[256,512]{1,0:T(8,128)S(1)} %copy-done, f32[2,8,256]{2,1,0:T(8,128)S(1)} %copy-done.5, f32[16,16]{1,0:T(8,128)S(1)} %copy-done.8), custom_call_target="tpu_custom_call" | custom-call | tf_op jit(solution)/shard_map/pallas_call | solution.py:510
  15.6 0.0 copy-start.1
  15.6 0.0 copy-start.2
  15.6 0.0 copy-start.3
  15.6 0.0 copy-start.4
  15.6 0.0 copy-start.6
  15.7 14.9 %all_to_all.15.recv_ref = f32[16,2,8,256]{3,2,1,0:T(8,128)S(1)} all-to-all(f32[16,2,8,256]{3,2,1,0:T(8,128)S(1)} %get-tuple-element.15), channel_id=1, replica_groups=mesh['gx'=8,'gy'=16] {'gy'}, dimensions={0} | all-to-all | bytes 524288 | tf_op jit(solution)/shard_map/all_to_all | solution.py:549
  30.6 0.0 copy-done.7
  30.6 0.6 %shard_map.94 = f32[128,128]{1,0:T(8,128)S(1)} custom-call(f32[16,2,8,256]{3,2,1,0:T(8,128)S(1)} %all_to_all.15.recv_ref, f32[5,8,256]{2,1,0:T(8,128)S(1)} %get-tuple-element.16.own_ref, f32[228,8,256]{2,1,0:T(8,128)S(1)} %shard_map.92.factor_ref, f32[256,512]{1,0:T(8,128)S(1)} %copy-done, f32[2,8,256]{2,1,0:T(8,128)S(1)} %copy-done.5, f32[32,16]{1,0:T(8,128)S(1)} %copy-done.7), custom_call_target="tpu_custom_call" | custom-call | tf_op jit(solution)/shard_map/pallas_call | solution.py:510
  31.2 10.7 %all_to_all.16 = f32[8,16,128]{2,1,0:T(8,128)S(1)} all-to-all(f32[8,16,128]{2,1,0:T(8,128)S(1)} %bitcast.9), channel_id=1, replica_groups=mesh['gx'=8,'gy'=16] {'gx'}, dimensions={0} | all-to-all | bytes 131072 | tf_op jit(solution)/shard_map/all_to_all | solution.py:556
  41.8 0.0 copy-done.1
  41.8 0.0 copy-done.2
  41.8 0.0 copy-done.3
  41.9 0.0 copy-done.4
  41.9 0.0 copy-done.6
  41.9 2.2 %shard_map.95 = f32[16,64,256]{2,1,0:T(8,128)} custom-call(f32[128,128]{1,0:T(8,128)S(1)} %bitcast.10, f32[64,2,8,256]{3,2,1,0:T(8,128)S(1)} %copy-done.2, f32[64,8,256]{2,1,0:T(8,128)S(1)} %copy-done.3, f32[8,128]{1,0:T(8,128)S(1)} %bitcast.12, f32[256,256]{1,0:T(8,128)S(1)} %copy-done.1, f32[5,8,256]{2,1,0:T(8,128)S(1)} %copy-done.4), custom_call_target="tpu_custom_call" | custom-call | tf_op jit(solution)/shard_map/pallas_call | solution.py:510
Async XLA Ops:
  0.0 14.7 %copy-start.5 = (f32[2,8,256]{2,1,0:T(8,128)S(1)}, f32[2,8,256]{2,1,0:T(8,128)}, u32[]{:S(2)}) copy-start(f32[2,8,256]{2,1,0:T(8,128)} %constant.15.clone.table_ref) | copy-start | bytes 49156
  0.0 14.7 %copy-start = (f32[256,512]{1,0:T(8,128)S(1)}, f32[256,512]{1,0:T(8,128)}, u32[]{:S(2)}) copy-start(f32[256,512]{1,0:T(8,128)} %constant.14.clone.dft_ref) | copy-start | bytes 1572868
  0.0 14.7 %copy-start.8 = (f32[16,16]{1,0:T(8,128)S(1)}, f32[16,16]{1,0:T(8,128)}, u32[]{:S(2)}) copy-start(f32[16,16]{1,0:T(8,128)} %constant.16.clone.octet_ref) | copy-start | bytes 3076
  3.8 10.8 %all-to-all-start = ((f32[8,16,128]{2,1,0:T(8,128)}), f32[8,16,128]{2,1,0:T(8,128)S(1)}, u32[]{:S(2)}, u32[]{:S(2)}) async-start(f32[8,16,128]{2,1,0:T(8,128)} %bitcast.14), calls=%async_computation | async-start | bytes 131072 | tf_op jit(solution)/shard_map/all_to_all | solution.py:535
  14.1 16.4 %copy-start.7 = (f32[32,16]{1,0:T(8,128)S(1)}, f32[32,16]{1,0:T(8,128)}, u32[]{:S(2)}) copy-start(f32[32,16]{1,0:T(8,128)} %constant.17.clone.octet_ref) | copy-start | bytes 6148
  15.6 26.2 %copy-start.1 = (f32[256,256]{1,0:T(8,128)S(1)}, f32[256,256]{1,0:T(8,128)}, u32[]{:S(2)}) copy-start(f32[256,256]{1,0:T(8,128)} %constant.12.clone.sine_hbm.sine_ref) | copy-start | bytes 786436
  15.6 26.2 %copy-start.2 = (f32[64,2,8,256]{3,2,1,0:T(8,128)S(1)}, f32[64,2,8,256]{3,2,1,0:T(8,128)}, u32[]{:S(2)}) copy-start(f32[64,2,8,256]{3,2,1,0:T(8,128)} %get-tuple-element.17.solved_ref) | copy-start | bytes 3145732
  15.6 26.2 %copy-start.3 = (f32[64,8,256]{2,1,0:T(8,128)S(1)}, f32[64,8,256]{2,1,0:T(8,128)}, u32[]{:S(2)}) copy-start(f32[64,8,256]{2,1,0:T(8,128)} %get-tuple-element.18.local_ref) | copy-start | bytes 1572868
  15.6 26.2 %copy-start.4 = (f32[5,8,256]{2,1,0:T(8,128)S(1)}, f32[5,8,256]{2,1,0:T(8,128)}, u32[]{:S(2)}) copy-start(f32[5,8,256]{2,1,0:T(8,128)} %constant.13.clone.edge_hbm.edge_ref) | copy-start | bytes 122884
  15.6 26.2 %copy-start.6 = (f32[1024]{0:T(1024)S(1)}, f32[1024]{0:T(1024)}, u32[]{:S(2)}) copy-start(f32[1024]{0:T(1024)} %metric_hbm.1) | copy-start | bytes 12292

commit v8 on v7

--- a/solution.py
+++ b/solution.py
@@ -97,7 +97,11 @@
 
 
 def splat_inverse(metric_ref, row):
-    return 1.0 / jnp.full((8, COLS), metric_ref[row], F32)
+    return 1.0 / jnp.full((8, 128), metric_ref[row], F32)
+
+
+def twice(values):
+    return jnp.concatenate([values, values], 1)
 
 
 def local_shift(wave_ref, edge_ref):
@@ -110,7 +114,7 @@
 
 def local_kernel(
     rhs_hbm, metric_hbm, tiled_hbm, wave_hbm, sine_hbm, edge_hbm, solved_hbm, send_hbm, metrics_hbm, shift_hbm, ratio_hbm,
-    metrics_ref, shift_ref, send_ref, ratio_ref, z_ref, r_lo, r_hi, sine_ref, edge_ref, metric_vec, metric_ref, wave_ref, rhs_sem, sems, out_sem,
+    metrics_ref, shift_ref, send_ref, inverse_ref, ratio_ref, z_ref, r_lo, r_hi, sine_ref, edge_ref, metric_vec, metric_ref, wave_ref, rhs_sem, sems, out_sem,
 ):
     first = lax.axis_index("gy") * ROWS
     pairs = (
@@ -144,7 +148,9 @@
     height = jnp.ones((8, COLS), F32)
     slope = jnp.ones((8, COLS), F32)
     for y in range(1, ROWS):
-        slope = slope + shift * splat_inverse(metric_ref, first + y) * height
+        inverse = splat_inverse(metric_ref, first + y)
+        inverse_ref[y] = inverse
+        slope = slope + shift * twice(inverse) * height
         taller = height + slope
         ratio_ref[y] = height / taller
         height = taller
@@ -168,7 +174,7 @@
         lines = dot(jnp.concatenate([line(y, c) for y in range(base, base + group) for c in range(2)], 0), sine)
         for y in range(max(base, 1), base + group):
             ratio = ratio_ref[y]
-            inverse = splat_inverse(metric_ref, first + y)
+            inverse = twice(inverse_ref[y])
             for c in range(2):
                 at = ((y - base) * 2 + c) * 8
                 state[c] = (lines[at : at + 8] * inverse + state[c]) * ratio
@@ -179,15 +185,15 @@
     upper = [jnp.zeros((8, COLS), F32)] * 2
     for y in range(ROWS - 1, 0, -1):
         ratio = ratio_ref[y]
-        inverse = splat_inverse(metric_ref, first + y)
+        inverse = inverse_ref[y]
         for c in range(2):
             upper[c] = z_ref[y, c] + ratio * upper[c]
             z_ref[y, c] = upper[c]
             a = upper[c] * left
             source = flat[0][pl.ds(c * PITCH + y, 8, stride=2 * PITCH), :]
-            a = (a[:, :128] + a[:, 128:] + jnp.where(lanes == 0, source, 0.0)) * inverse[:, :128]
+            a = (a[:, :128] + a[:, 128:] + jnp.where(lanes == 0, source, 0.0)) * inverse
             b = upper[c] * right
-            b = (b[:, :128] + b[:, 128:]) * inverse[:, :128]
+            b = (b[:, :128] + b[:, 128:]) * inverse
             columns[0][c] = jnp.where(lanes == y, wide(jnp.sum(a, axis=1, keepdims=True)), columns[0][c])
             columns[1][c] = jnp.where(lanes == y + ROWS, wide(jnp.sum(b, axis=1, keepdims=True)), columns[1][c])
         if y % 16 == 0:
@@ -199,7 +205,7 @@
     edges = jnp.concatenate([z_ref[y, c] for y in (1, ROWS - 1) for c in range(2)], 0)
     edges = dot(edges, sine)
     zero_lane = lax.broadcasted_iota(jnp.int32, (8, COLS), 1) == 0
-    inverse = splat_inverse(metric_ref, first)
+    inverse = twice(splat_inverse(metric_ref, first))
     for c in range(2):
         near = jnp.where(zero_lane, 0.0, edges[c * 8 : c * 8 + 8]) + line(0, c) * inverse
         far = jnp.where(zero_lane, 0.0, edges[16 + c * 8 : 24 + c * 8])
@@ -246,7 +252,7 @@
     together = 4
 
     def bands(outer, _):
-        state = [(one, one, zero, zero)] * together
+        state = [(one, one, one, zero)] * together
 
         def rows(y, state):
             out = []
@@ -255,7 +261,7 @@
                 t = excess((outer * together + i) * ROWS + y)
                 slope = slope + t * height
                 height = height + slope
-                rise = rise + t * (rest + 1.0)
+                rise = rise + t * rest
                 rest = rest + rise
                 out.append((height, slope, rest, rise))
             return tuple(out)
@@ -266,7 +272,7 @@
             band = outer * together + i
             gamma = 1.0 / height
             gamma_ref[band] = gamma
-            base_ref[band] = excess(band * ROWS) + rest * gamma
+            base_ref[band] = excess(band * ROWS) + (rest - 1.0) * gamma
             edge_ref[band] = (slope - 1.0) * gamma
         return 0
 
@@ -525,7 +531,7 @@
         local_kernel,
         [lines, (128, 128), (16, 128), (8, COLS), full],
         [
-            (16, 128), (8, COLS), (128, 128), full, lines, side, side, (COLS, COLS), (5, 8, COLS), (8, 128),
+            (16, 128), (8, COLS), (128, 128), (ROWS, 8, 128), full, lines, side, side, (COLS, COLS), (5, 8, COLS), (8, 128),
             pltpu.SMEM((1024,), F32), pltpu.SMEM((8,), F32),
             pltpu.SemaphoreType.DMA((4,)), pltpu.SemaphoreType.DMA((5,)), pltpu.SemaphoreType.DMA((4,)),
         ],

time: 44.4 us -> 44.2 us (level)
  transfers between devices with their start and end apart: 1 -> 1, of which waited for: 1 -> 1; matrix products, arithmetic and copies ran while one was open for 0% -> 0% of each run, Pallas kernels for 10% -> 9%
where the time goes in v8:
time: 44.2 us; the launch traced here: 43.8 us
  blocking collectives  25.3 us (57%)
  Pallas kernels  11.6 us (26%)
  starting transfers between devices  5.98 us (14%)
  waiting for transfers between devices  0.8 us (2%)
    all_to_all x1, blocking collectives, per_device(): recv = lax.all_to_all(send, 'gy', 0, 0, tiled=True)  14.9 us
    pallas_call x5, Pallas kernels, call(): pl.pallas_call(kernel, out_shape=[(pltpu.HBM if i in far else pltpu.VMEM)...  11.6 us
    all_to_all x1, blocking collectives, per_device(): recv = lax.all_to_all(send.reshape(8, 16, 128), 'gx', 0, 0, tiled=True)  10.4 us
    all_to_all x1, starting transfers between devices, per_device(): recv = lax.all_to_all(send.reshape(8, 16, 128), 'gx', 0, 0, tiled=True)  5.98 us
  transfers between devices with their start and end apart: 1, of which 1 were waited for; matrix products, arithmetic and copies ran while one was open for 0% of the time, Pallas kernels for 9%

profile of v8, /device:TPU:1, one launch (start us, length us, event | category | flops | bytes accessed | tf_op | source)
XLA Modules:
  0.0 43.8 jit_solution(6992462482300435758)
XLA Ops:
  0.0 0.0 copy-start.5
  0.0 0.0 copy-start
  0.0 0.0 copy-start.8
  0.0 3.8 %shard_map.91 = (f32[64,2,8,256]{3,2,1,0:T(8,128)}, f32[128,128]{1,0:T(8,128)}, f32[16,128]{1,0:T(8,128)}, f32[8,256]{1,0:T(8,128)}, f32[64,8,256]{2,1,0:T(8,128)}) custom-call(f32[16,64,256]{2,1,0:T(8,128)} %bitcast.13, f32[1024]{0:T(1024)} %metric_hbm.1, f32[8,128]{1,0:T(8,128)} %bitcast.11, f32[8]{0:T(128)} %wave_hbm.1, ...), custom_call_target="tpu_custom_call" | custom-call | tf_op jit(solution)/shard_map/pallas_call | solution.py:516
  3.8 6.0 %all-to-all-start = ((f32[8,16,128]{2,1,0:T(8,128)}), f32[8,16,128]{2,1,0:T(8,128)S(1)}, u32[]{:S(2)}, u32[]{:S(2)}) async-start(f32[8,16,128]{2,1,0:T(8,128)} %bitcast.14), calls=%async_computation | async-start | bytes 131072 | tf_op jit(solution)/shard_map/all_to_all | solution.py:541
  9.8 4.0 %shard_map.92.factor_ref = f32[228,8,256]{2,1,0:T(8,128)S(1)} custom-call(f32[2048]{0:T(1024)} %bitcast.15, f32[8,256]{1,0:T(8,128)} %get-tuple-element.14.shift_hbm), custom_call_target="tpu_custom_call" | custom-call | tf_op jit(solution)/shard_map/pallas_call | solution.py:516
  13.9 0.0 copy-start.7
  13.9 0.8 %all-to-all-done = f32[8,16,128]{2,1,0:T(8,128)S(1)} async-done(((f32[8,16,128]{2,1,0:T(8,128)}), f32[8,16,128]{2,1,0:T(8,128)S(1)}, u32[]{:S(2)}, u32[]{:S(2)}) %all-to-all-start) | async-done | bytes 65568 | tf_op jit(solution)/shard_map/all_to_all | solution.py:541
  14.7 0.0 copy-done.5
  14.7 0.0 copy-done
  14.7 0.0 copy-done.8
  14.7 0.9 %shard_map.93 = (f32[16,2,8,256]{3,2,1,0:T(8,128)S(1)}, f32[5,8,256]{2,1,0:T(8,128)S(1)}) custom-call(f32[128,128]{1,0:T(8,128)S(1)} %bitcast.8, f32[228,8,256]{2,1,0:T(8,128)S(1)} %shard_map.92.factor_ref, f32[256,512]{1,0:T(8,128)S(1)} %copy-done, f32[2,8,256]{2,1,0:T(8,128)S(1)} %copy-done.5, f32[16,16]{1,0:T(8,128)S(1)} %copy-done.8), custom_call_target="tpu_custom_call" | custom-call | tf_op jit(solution)/shard_map/pallas_call | solution.py:516
  15.6 0.0 copy-start.1
  15.6 0.0 copy-start.2
  15.6 0.0 copy-start.3
  15.6 0.0 copy-start.4
  15.7 0.0 copy-start.6
  15.7 14.9 %all_to_all.15.recv_ref = f32[16,2,8,256]{3,2,1,0:T(8,128)S(1)} all-to-all(f32[16,2,8,256]{3,2,1,0:T(8,128)S(1)} %get-tuple-element.15), channel_id=1, replica_groups=mesh['gx'=8,'gy'=16] {'gy'}, dimensions={0} | all-to-all | bytes 524288 | tf_op jit(solution)/shard_map/all_to_all | solution.py:555
  30.6 0.0 copy-done.7
  30.6 0.6 %shard_map.94 = f32[128,128]{1,0:T(8,128)S(1)} custom-call(f32[16,2,8,256]{3,2,1,0:T(8,128)S(1)} %all_to_all.15.recv_ref, f32[5,8,256]{2,1,0:T(8,128)S(1)} %get-tuple-element.16.own_ref, f32[228,8,256]{2,1,0:T(8,128)S(1)} %shard_map.92.factor_ref, f32[256,512]{1,0:T(8,128)S(1)} %copy-done, f32[2,8,256]{2,1,0:T(8,128)S(1)} %copy-done.5, f32[32,16]{1,0:T(8,128)S(1)} %copy-done.7), custom_call_target="tpu_custom_call" | custom-call | tf_op jit(solution)/shard_map/pallas_call | solution.py:516
  31.2 10.4 %all_to_all.16 = f32[8,16,128]{2,1,0:T(8,128)S(1)} all-to-all(f32[8,16,128]{2,1,0:T(8,128)S(1)} %bitcast.9), channel_id=1, replica_groups=mesh['gx'=8,'gy'=16] {'gx'}, dimensions={0} | all-to-all | bytes 131072 | tf_op jit(solution)/shard_map/all_to_all | solution.py:562
  41.6 0.0 copy-done.1
  41.6 0.0 copy-done.2
  41.6 0.0 copy-done.3
  41.6 0.0 copy-done.4
  41.6 0.0 copy-done.6
  41.6 2.2 %shard_map.95 = f32[16,64,256]{2,1,0:T(8,128)} custom-call(f32[128,128]{1,0:T(8,128)S(1)} %bitcast.10, f32[64,2,8,256]{3,2,1,0:T(8,128)S(1)} %copy-done.2, f32[64,8,256]{2,1,0:T(8,128)S(1)} %copy-done.3, f32[8,128]{1,0:T(8,128)S(1)} %bitcast.12, f32[256,256]{1,0:T(8,128)S(1)} %copy-done.1, f32[5,8,256]{2,1,0:T(8,128)S(1)} %copy-done.4), custom_call_target="tpu_custom_call" | custom-call | tf_op jit(solution)/shard_map/pallas_call | solution.py:516
Async XLA Ops:
  0.0 14.7 %copy-start.5 = (f32[2,8,256]{2,1,0:T(8,128)S(1)}, f32[2,8,256]{2,1,0:T(8,128)}, u32[]{:S(2)}) copy-start(f32[2,8,256]{2,1,0:T(8,128)} %constant.15.clone.table_ref) | copy-start | bytes 49156
  0.0 14.7 %copy-start = (f32[256,512]{1,0:T(8,128)S(1)}, f32[256,512]{1,0:T(8,128)}, u32[]{:S(2)}) copy-start(f32[256,512]{1,0:T(8,128)} %constant.14.clone.dft_ref) | copy-start | bytes 1572868
  0.0 14.7 %copy-start.8 = (f32[16,16]{1,0:T(8,128)S(1)}, f32[16,16]{1,0:T(8,128)}, u32[]{:S(2)}) copy-start(f32[16,16]{1,0:T(8,128)} %constant.16.clone.octet_ref) | copy-start | bytes 3076
  3.8 10.8 %all-to-all-start = ((f32[8,16,128]{2,1,0:T(8,128)}), f32[8,16,128]{2,1,0:T(8,128)S(1)}, u32[]{:S(2)}, u32[]{:S(2)}) async-start(f32[8,16,128]{2,1,0:T(8,128)} %bitcast.14), calls=%async_computation | async-start | bytes 131072 | tf_op jit(solution)/shard_map/all_to_all | solution.py:541
  13.9 16.7 %copy-start.7 = (f32[32,16]{1,0:T(8,128)S(1)}, f32[32,16]{1,0:T(8,128)}, u32[]{:S(2)}) copy-start(f32[32,16]{1,0:T(8,128)} %constant.17.clone.octet_ref) | copy-start | bytes 6148
  15.6 26.0 %copy-start.1 = (f32[256,256]{1,0:T(8,128)S(1)}, f32[256,256]{1,0:T(8,128)}, u32[]{:S(2)}) copy-start(f32[256,256]{1,0:T(8,128)} %constant.12.clone.sine_hbm.sine_ref) | copy-start | bytes 786436
  15.6 26.0 %copy-start.2 = (f32[64,2,8,256]{3,2,1,0:T(8,128)S(1)}, f32[64,2,8,256]{3,2,1,0:T(8,128)}, u32[]{:S(2)}) copy-start(f32[64,2,8,256]{3,2,1,0:T(8,128)} %get-tuple-element.17.solved_ref) | copy-start | bytes 3145732
  15.6 26.0 %copy-start.3 = (f32[64,8,256]{2,1,0:T(8,128)S(1)}, f32[64,8,256]{2,1,0:T(8,128)}, u32[]{:S(2)}) copy-start(f32[64,8,256]{2,1,0:T(8,128)} %get-tuple-element.18.local_ref) | copy-start | bytes 1572868
  15.6 26.0 %copy-start.4 = (f32[5,8,256]{2,1,0:T(8,128)S(1)}, f32[5,8,256]{2,1,0:T(8,128)}, u32[]{:S(2)}) copy-start(f32[5,8,256]{2,1,0:T(8,128)} %constant.13.clone.edge_hbm.edge_ref) | copy-start | bytes 122884
  15.7 26.0 %copy-start.6 = (f32[1024]{0:T(1024)S(1)}, f32[1024]{0:T(1024)}, u32[]{:S(2)}) copy-start(f32[1024]{0:T(1024)} %metric_hbm.1) | copy-start | bytes 12292

commit v9 on v8

--- a/solution.py
+++ b/solution.py
@@ -369,25 +369,23 @@
         sides.append((re_cos + im_sin + extra[0], im_cos - re_sin + extra[1]))
     for c in range(2):
         own_ref[c], own_ref[2 + c] = sides[0][c], sides[1][c]
-        send_ref[mine, c] = jnp.zeros((8, COLS), F32)
     own_ref[4] = jnp.concatenate(total, 1)
     up, down = up_ref[mine], down_ref[mine]
-
-    def above(band, carry):
+    zero = jnp.zeros((8, COLS), F32)
+    first = [sides[1][c] + up * sides[0][c] for c in range(2)]
+    last = [sides[0][c] + down * sides[1][c] for c in range(2)]
+    above = [zero] * 2
+    rows = []
+    for band in range(BANDS):
+        rows.append(above)
         factor = up_ref[band]
-        for c in range(2):
-            send_ref[band, c] = carry[c]
-        return tuple(value * factor for value in carry)
-
-    def below(step, carry):
-        band = mine - 1 - step
+        above = [jnp.where(band == mine, first[c], above[c] * factor) for c in range(2)]
+    below = [zero] * 2
+    for band in range(BANDS - 1, -1, -1):
         factor = down_ref[band]
         for c in range(2):
-            send_ref[band, c] = carry[c]
-        return tuple(value * factor for value in carry)
-
-    lax.fori_loop(mine + 1, BANDS, above, tuple(sides[1][c] + up * sides[0][c] for c in range(2)))
-    lax.fori_loop(0, mine, below, tuple(sides[0][c] + down * sides[1][c] for c in range(2)))
+            send_ref[band, c] = rows[band][c] + below[c]
+        below = [jnp.where(band == mine, last[c], below[c] * factor) for c in range(2)]
 
 
 def separator_kernel(

time: 44.2 us -> 44.1 us (level)
  no operation moved by 1% of the time
where the time goes in v9:
time: 44.1 us; the launch traced here: 43.7 us
  blocking collectives  25.3 us (57%)
  Pallas kernels  11.5 us (26%)
  starting transfers between devices  5.98 us (14%)
  waiting for transfers between devices  0.8 us (2%)
    all_to_all x1, blocking collectives, per_device(): recv = lax.all_to_all(send, 'gy', 0, 0, tiled=True)  14.9 us
    pallas_call x5, Pallas kernels, call(): pl.pallas_call(kernel, out_shape=[(pltpu.HBM if i in far else pltpu.VMEM)...  11.5 us
    all_to_all x1, blocking collectives, per_device(): recv = lax.all_to_all(send.reshape(8, 16, 128), 'gx', 0, 0, tiled=True)  10.4 us
    all_to_all x1, starting transfers between devices, per_device(): recv = lax.all_to_all(send.reshape(8, 16, 128), 'gx', 0, 0, tiled=True)  5.98 us
  transfers between devices with their start and end apart: 1, of which 1 were waited for; matrix products, arithmetic and copies ran while one was open for 0% of the time, Pallas kernels for 9%

profile of v9, /device:TPU:1, one launch (start us, length us, event | category | flops | bytes accessed | tf_op | source)
XLA Modules:
  0.0 43.7 jit_solution(4106543012932345330)
XLA Ops:
  0.0 0.0 copy-start.5
  0.0 0.0 copy-start
  0.0 0.0 copy-start.8
  0.0 3.8 %shard_map.91 = (f32[64,2,8,256]{3,2,1,0:T(8,128)}, f32[128,128]{1,0:T(8,128)}, f32[16,128]{1,0:T(8,128)}, f32[8,256]{1,0:T(8,128)}, f32[64,8,256]{2,1,0:T(8,128)}) custom-call(f32[16,64,256]{2,1,0:T(8,128)} %bitcast.13, f32[1024]{0:T(1024)} %metric_hbm.1, f32[8,128]{1,0:T(8,128)} %bitcast.11, f32[8]{0:T(128)} %wave_hbm.1, ...), custom_call_target="tpu_custom_call" | custom-call | tf_op jit(solution)/shard_map/pallas_call | solution.py:514
  3.8 6.0 %all-to-all-start = ((f32[8,16,128]{2,1,0:T(8,128)}), f32[8,16,128]{2,1,0:T(8,128)S(1)}, u32[]{:S(2)}, u32[]{:S(2)}) async-start(f32[8,16,128]{2,1,0:T(8,128)} %bitcast.14), calls=%async_computation | async-start | bytes 131072 | tf_op jit(solution)/shard_map/all_to_all | solution.py:539
  9.8 4.0 %shard_map.92.factor_ref = f32[228,8,256]{2,1,0:T(8,128)S(1)} custom-call(f32[2048]{0:T(1024)} %bitcast.15, f32[8,256]{1,0:T(8,128)} %get-tuple-element.14.shift_hbm), custom_call_target="tpu_custom_call" | custom-call | tf_op jit(solution)/shard_map/pallas_call | solution.py:514
  13.9 0.0 copy-start.7
  13.9 0.8 %all-to-all-done = f32[8,16,128]{2,1,0:T(8,128)S(1)} async-done(((f32[8,16,128]{2,1,0:T(8,128)}), f32[8,16,128]{2,1,0:T(8,128)S(1)}, u32[]{:S(2)}, u32[]{:S(2)}) %all-to-all-start) | async-done | bytes 65568 | tf_op jit(solution)/shard_map/all_to_all | solution.py:539
  14.7 0.0 copy-done.5
  14.7 0.0 copy-done
  14.7 0.0 copy-done.8
  14.7 0.8 %shard_map.93 = (f32[16,2,8,256]{3,2,1,0:T(8,128)S(1)}, f32[5,8,256]{2,1,0:T(8,128)S(1)}) custom-call(f32[128,128]{1,0:T(8,128)S(1)} %bitcast.8, f32[228,8,256]{2,1,0:T(8,128)S(1)} %shard_map.92.factor_ref, f32[256,512]{1,0:T(8,128)S(1)} %copy-done, f32[2,8,256]{2,1,0:T(8,128)S(1)} %copy-done.5, f32[16,16]{1,0:T(8,128)S(1)} %copy-done.8), custom_call_target="tpu_custom_call" | custom-call | tf_op jit(solution)/shard_map/pallas_call | solution.py:514
  15.5 0.0 copy-start.1
  15.5 0.0 copy-start.2
  15.5 0.0 copy-start.3
  15.6 0.0 copy-start.4
  15.6 0.0 copy-start.6
  15.6 14.9 %all_to_all.15.recv_ref = f32[16,2,8,256]{3,2,1,0:T(8,128)S(1)} all-to-all(f32[16,2,8,256]{3,2,1,0:T(8,128)S(1)} %get-tuple-element.15), channel_id=1, replica_groups=mesh['gx'=8,'gy'=16] {'gy'}, dimensions={0} | all-to-all | bytes 524288 | tf_op jit(solution)/shard_map/all_to_all | solution.py:553
  30.5 0.0 copy-done.7
  30.5 0.6 %shard_map.94 = f32[128,128]{1,0:T(8,128)S(1)} custom-call(f32[16,2,8,256]{3,2,1,0:T(8,128)S(1)} %all_to_all.15.recv_ref, f32[5,8,256]{2,1,0:T(8,128)S(1)} %get-tuple-element.16.own_ref, f32[228,8,256]{2,1,0:T(8,128)S(1)} %shard_map.92.factor_ref, f32[256,512]{1,0:T(8,128)S(1)} %copy-done, f32[2,8,256]{2,1,0:T(8,128)S(1)} %copy-done.5, f32[32,16]{1,0:T(8,128)S(1)} %copy-done.7), custom_call_target="tpu_custom_call" | custom-call | tf_op jit(solution)/shard_map/pallas_call | solution.py:514
  31.1 10.4 %all_to_all.16 = f32[8,16,128]{2,1,0:T(8,128)S(1)} all-to-all(f32[8,16,128]{2,1,0:T(8,128)S(1)} %bitcast.9), channel_id=1, replica_groups=mesh['gx'=8,'gy'=16] {'gx'}, dimensions={0} | all-to-all | bytes 131072 | tf_op jit(solution)/shard_map/all_to_all | solution.py:560
  41.5 0.0 copy-done.1
  41.5 0.0 copy-done.2
  41.5 0.0 copy-done.3
  41.5 0.0 copy-done.4
  41.5 0.0 copy-done.6
  41.5 2.2 %shard_map.95 = f32[16,64,256]{2,1,0:T(8,128)} custom-call(f32[128,128]{1,0:T(8,128)S(1)} %bitcast.10, f32[64,2,8,256]{3,2,1,0:T(8,128)S(1)} %copy-done.2, f32[64,8,256]{2,1,0:T(8,128)S(1)} %copy-done.3, f32[8,128]{1,0:T(8,128)S(1)} %bitcast.12, f32[256,256]{1,0:T(8,128)S(1)} %copy-done.1, f32[5,8,256]{2,1,0:T(8,128)S(1)} %copy-done.4), custom_call_target="tpu_custom_call" | custom-call | tf_op jit(solution)/shard_map/pallas_call | solution.py:514
Async XLA Ops:
  0.0 14.7 %copy-start.5 = (f32[2,8,256]{2,1,0:T(8,128)S(1)}, f32[2,8,256]{2,1,0:T(8,128)}, u32[]{:S(2)}) copy-start(f32[2,8,256]{2,1,0:T(8,128)} %constant.15.clone.table_ref) | copy-start | bytes 49156
  0.0 14.7 %copy-start = (f32[256,512]{1,0:T(8,128)S(1)}, f32[256,512]{1,0:T(8,128)}, u32[]{:S(2)}) copy-start(f32[256,512]{1,0:T(8,128)} %constant.14.clone.dft_ref) | copy-start | bytes 1572868
  0.0 14.7 %copy-start.8 = (f32[16,16]{1,0:T(8,128)S(1)}, f32[16,16]{1,0:T(8,128)}, u32[]{:S(2)}) copy-start(f32[16,16]{1,0:T(8,128)} %constant.16.clone.octet_ref) | copy-start | bytes 3076
  3.8 10.8 %all-to-all-start = ((f32[8,16,128]{2,1,0:T(8,128)}), f32[8,16,128]{2,1,0:T(8,128)S(1)}, u32[]{:S(2)}, u32[]{:S(2)}) async-start(f32[8,16,128]{2,1,0:T(8,128)} %bitcast.14), calls=%async_computation | async-start | bytes 131072 | tf_op jit(solution)/shard_map/all_to_all | solution.py:539
  13.9 16.6 %copy-start.7 = (f32[32,16]{1,0:T(8,128)S(1)}, f32[32,16]{1,0:T(8,128)}, u32[]{:S(2)}) copy-start(f32[32,16]{1,0:T(8,128)} %constant.17.clone.octet_ref) | copy-start | bytes 6148
  15.5 26.0 %copy-start.1 = (f32[256,256]{1,0:T(8,128)S(1)}, f32[256,256]{1,0:T(8,128)}, u32[]{:S(2)}) copy-start(f32[256,256]{1,0:T(8,128)} %constant.12.clone.sine_hbm.sine_ref) | copy-start | bytes 786436
  15.5 26.0 %copy-start.2 = (f32[64,2,8,256]{3,2,1,0:T(8,128)S(1)}, f32[64,2,8,256]{3,2,1,0:T(8,128)}, u32[]{:S(2)}) copy-start(f32[64,2,8,256]{3,2,1,0:T(8,128)} %get-tuple-element.17.solved_ref) | copy-start | bytes 3145732
  15.5 26.0 %copy-start.3 = (f32[64,8,256]{2,1,0:T(8,128)S(1)}, f32[64,8,256]{2,1,0:T(8,128)}, u32[]{:S(2)}) copy-start(f32[64,8,256]{2,1,0:T(8,128)} %get-tuple-element.18.local_ref) | copy-start | bytes 1572868
  15.6 25.9 %copy-start.4 = (f32[5,8,256]{2,1,0:T(8,128)S(1)}, f32[5,8,256]{2,1,0:T(8,128)}, u32[]{:S(2)}) copy-start(f32[5,8,256]{2,1,0:T(8,128)} %constant.13.clone.edge_hbm.edge_ref) | copy-start | bytes 122884
  15.6 25.9 %copy-start.6 = (f32[1024]{0:T(1024)S(1)}, f32[1024]{0:T(1024)}, u32[]{:S(2)}) copy-start(f32[1024]{0:T(1024)} %metric_hbm.1) | copy-start | bytes 12292

commit v10 on v9

--- a/solution.py
+++ b/solution.py
@@ -467,7 +467,7 @@
             z_ref[y, c] = state[c]
     upper = [edges[16 + c * 8 : 24 + c * 8] for c in range(2)]
     flat = [ref.reshape(16 * PITCH, 128) for ref in (o_lo, o_hi)]
-    group, half = 8, ROWS // 2
+    group, half = 16, ROWS // 2
     copies = []
 
     def store(base, product):

time: 44.1 us -> 44.1 us (level)
  no operation moved by 1% of the time
where the time goes in v10:
time: 44.1 us; the launch traced here: 43.7 us
  blocking collectives  25.3 us (57%)
  Pallas kernels  11.5 us (26%)
  starting transfers between devices  5.98 us (14%)
  waiting for transfers between devices  0.8 us (2%)
    all_to_all x1, blocking collectives, per_device(): recv = lax.all_to_all(send, 'gy', 0, 0, tiled=True)  14.9 us
    pallas_call x5, Pallas kernels, call(): pl.pallas_call(kernel, out_shape=[(pltpu.HBM if i in far else pltpu.VMEM)...  11.5 us
    all_to_all x1, blocking collectives, per_device(): recv = lax.all_to_all(send.reshape(8, 16, 128), 'gx', 0, 0, tiled=True)  10.4 us
    all_to_all x1, starting transfers between devices, per_device(): recv = lax.all_to_all(send.reshape(8, 16, 128), 'gx', 0, 0, tiled=True)  5.98 us
  transfers between devices with their start and end apart: 1, of which 1 were waited for; matrix products, arithmetic and copies ran while one was open for 0% of the time, Pallas kernels for 9%

profile of v10, /device:TPU:1, one launch (start us, length us, event | category | flops | bytes accessed | tf_op | source)
XLA Modules:
  0.0 43.7 jit_solution(8507127320475440112)
XLA Ops:
  0.0 0.0 copy-start.5
  0.0 0.0 copy-start
  0.0 0.0 copy-start.8
  0.0 3.8 %shard_map.91 = (f32[64,2,8,256]{3,2,1,0:T(8,128)}, f32[128,128]{1,0:T(8,128)}, f32[16,128]{1,0:T(8,128)}, f32[8,256]{1,0:T(8,128)}, f32[64,8,256]{2,1,0:T(8,128)}) custom-call(f32[16,64,256]{2,1,0:T(8,128)} %bitcast.13, f32[1024]{0:T(1024)} %metric_hbm.1, f32[8,128]{1,0:T(8,128)} %bitcast.11, f32[8]{0:T(128)} %wave_hbm.1, ...), custom_call_target="tpu_custom_call" | custom-call | tf_op jit(solution)/shard_map/pallas_call | solution.py:514
  3.8 6.0 %all-to-all-start = ((f32[8,16,128]{2,1,0:T(8,128)}), f32[8,16,128]{2,1,0:T(8,128)S(1)}, u32[]{:S(2)}, u32[]{:S(2)}) async-start(f32[8,16,128]{2,1,0:T(8,128)} %bitcast.14), calls=%async_computation | async-start | bytes 131072 | tf_op jit(solution)/shard_map/all_to_all | solution.py:539
  9.8 4.0 %shard_map.92.factor_ref = f32[228,8,256]{2,1,0:T(8,128)S(1)} custom-call(f32[2048]{0:T(1024)} %bitcast.15, f32[8,256]{1,0:T(8,128)} %get-tuple-element.14.shift_hbm), custom_call_target="tpu_custom_call" | custom-call | tf_op jit(solution)/shard_map/pallas_call | solution.py:514
  13.9 0.0 copy-start.7
  13.9 0.8 %all-to-all-done = f32[8,16,128]{2,1,0:T(8,128)S(1)} async-done(((f32[8,16,128]{2,1,0:T(8,128)}), f32[8,16,128]{2,1,0:T(8,128)S(1)}, u32[]{:S(2)}, u32[]{:S(2)}) %all-to-all-start) | async-done | bytes 65568 | tf_op jit(solution)/shard_map/all_to_all | solution.py:539
  14.7 0.0 copy-done.5
  14.7 0.0 copy-done
  14.7 0.0 copy-done.8
  14.7 0.8 %shard_map.93 = (f32[16,2,8,256]{3,2,1,0:T(8,128)S(1)}, f32[5,8,256]{2,1,0:T(8,128)S(1)}) custom-call(f32[128,128]{1,0:T(8,128)S(1)} %bitcast.8, f32[228,8,256]{2,1,0:T(8,128)S(1)} %shard_map.92.factor_ref, f32[256,512]{1,0:T(8,128)S(1)} %copy-done, f32[2,8,256]{2,1,0:T(8,128)S(1)} %copy-done.5, f32[16,16]{1,0:T(8,128)S(1)} %copy-done.8), custom_call_target="tpu_custom_call" | custom-call | tf_op jit(solution)/shard_map/pallas_call | solution.py:514
  15.5 0.0 copy-start.1
  15.5 0.0 copy-start.2
  15.5 0.0 copy-start.3
  15.6 0.0 copy-start.4
  15.6 0.0 copy-start.6
  15.6 14.9 %all_to_all.15.recv_ref = f32[16,2,8,256]{3,2,1,0:T(8,128)S(1)} all-to-all(f32[16,2,8,256]{3,2,1,0:T(8,128)S(1)} %get-tuple-element.15), channel_id=1, replica_groups=mesh['gx'=8,'gy'=16] {'gy'}, dimensions={0} | all-to-all | bytes 524288 | tf_op jit(solution)/shard_map/all_to_all | solution.py:553
  30.5 0.0 copy-done.7
  30.5 0.6 %shard_map.94 = f32[128,128]{1,0:T(8,128)S(1)} custom-call(f32[16,2,8,256]{3,2,1,0:T(8,128)S(1)} %all_to_all.15.recv_ref, f32[5,8,256]{2,1,0:T(8,128)S(1)} %get-tuple-element.16.own_ref, f32[228,8,256]{2,1,0:T(8,128)S(1)} %shard_map.92.factor_ref, f32[256,512]{1,0:T(8,128)S(1)} %copy-done, f32[2,8,256]{2,1,0:T(8,128)S(1)} %copy-done.5, f32[32,16]{1,0:T(8,128)S(1)} %copy-done.7), custom_call_target="tpu_custom_call" | custom-call | tf_op jit(solution)/shard_map/pallas_call | solution.py:514
  31.1 10.4 %all_to_all.16 = f32[8,16,128]{2,1,0:T(8,128)S(1)} all-to-all(f32[8,16,128]{2,1,0:T(8,128)S(1)} %bitcast.9), channel_id=1, replica_groups=mesh['gx'=8,'gy'=16] {'gx'}, dimensions={0} | all-to-all | bytes 131072 | tf_op jit(solution)/shard_map/all_to_all | solution.py:560
  41.5 0.0 copy-done.1
  41.5 0.0 copy-done.2
  41.5 0.0 copy-done.3
  41.5 0.0 copy-done.4
  41.5 0.0 copy-done.6
  41.5 2.2 %shard_map.95 = f32[16,64,256]{2,1,0:T(8,128)} custom-call(f32[128,128]{1,0:T(8,128)S(1)} %bitcast.10, f32[64,2,8,256]{3,2,1,0:T(8,128)S(1)} %copy-done.2, f32[64,8,256]{2,1,0:T(8,128)S(1)} %copy-done.3, f32[8,128]{1,0:T(8,128)S(1)} %bitcast.12, f32[256,256]{1,0:T(8,128)S(1)} %copy-done.1, f32[5,8,256]{2,1,0:T(8,128)S(1)} %copy-done.4), custom_call_target="tpu_custom_call" | custom-call | tf_op jit(solution)/shard_map/pallas_call | solution.py:514
Async XLA Ops:
  0.0 14.7 %copy-start.5 = (f32[2,8,256]{2,1,0:T(8,128)S(1)}, f32[2,8,256]{2,1,0:T(8,128)}, u32[]{:S(2)}) copy-start(f32[2,8,256]{2,1,0:T(8,128)} %constant.15.clone.table_ref) | copy-start | bytes 49156
  0.0 14.7 %copy-start = (f32[256,512]{1,0:T(8,128)S(1)}, f32[256,512]{1,0:T(8,128)}, u32[]{:S(2)}) copy-start(f32[256,512]{1,0:T(8,128)} %constant.14.clone.dft_ref) | copy-start | bytes 1572868
  0.0 14.7 %copy-start.8 = (f32[16,16]{1,0:T(8,128)S(1)}, f32[16,16]{1,0:T(8,128)}, u32[]{:S(2)}) copy-start(f32[16,16]{1,0:T(8,128)} %constant.16.clone.octet_ref) | copy-start | bytes 3076
  3.8 10.8 %all-to-all-start = ((f32[8,16,128]{2,1,0:T(8,128)}), f32[8,16,128]{2,1,0:T(8,128)S(1)}, u32[]{:S(2)}, u32[]{:S(2)}) async-start(f32[8,16,128]{2,1,0:T(8,128)} %bitcast.14), calls=%async_computation | async-start | bytes 131072 | tf_op jit(solution)/shard_map/all_to_all | solution.py:539
  13.9 16.6 %copy-start.7 = (f32[32,16]{1,0:T(8,128)S(1)}, f32[32,16]{1,0:T(8,128)}, u32[]{:S(2)}) copy-start(f32[32,16]{1,0:T(8,128)} %constant.17.clone.octet_ref) | copy-start | bytes 6148
  15.5 26.0 %copy-start.1 = (f32[256,256]{1,0:T(8,128)S(1)}, f32[256,256]{1,0:T(8,128)}, u32[]{:S(2)}) copy-start(f32[256,256]{1,0:T(8,128)} %constant.12.clone.sine_hbm.sine_ref) | copy-start | bytes 786436
  15.5 26.0 %copy-start.2 = (f32[64,2,8,256]{3,2,1,0:T(8,128)S(1)}, f32[64,2,8,256]{3,2,1,0:T(8,128)}, u32[]{:S(2)}) copy-start(f32[64,2,8,256]{3,2,1,0:T(8,128)} %get-tuple-element.17.solved_ref) | copy-start | bytes 3145732
  15.5 26.0 %copy-start.3 = (f32[64,8,256]{2,1,0:T(8,128)S(1)}, f32[64,8,256]{2,1,0:T(8,128)}, u32[]{:S(2)}) copy-start(f32[64,8,256]{2,1,0:T(8,128)} %get-tuple-element.18.local_ref) | copy-start | bytes 1572868
  15.6 25.9 %copy-start.4 = (f32[5,8,256]{2,1,0:T(8,128)S(1)}, f32[5,8,256]{2,1,0:T(8,128)}, u32[]{:S(2)}) copy-start(f32[5,8,256]{2,1,0:T(8,128)} %constant.13.clone.edge_hbm.edge_ref) | copy-start | bytes 122884
  15.6 25.9 %copy-start.6 = (f32[1024]{0:T(1024)S(1)}, f32[1024]{0:T(1024)}, u32[]{:S(2)}) copy-start(f32[1024]{0:T(1024)} %metric_hbm.1) | copy-start | bytes 12292
